TPU v7x, 32 devices: a whole 2x2x4 slice. The times are simulated.
32 devices in a mesh: section: 4 (over y, x), dp: 8 (over z, core).
Axes of the slice: x: 2, y: 2, z: 4, core: 2. Of those that a mesh axis runs over, the one named last changes fastest.
Arguments:
- token_ids: int32 [64, 256], P('dp'), may hold values from 0 to 26
- timesteps: int32 [64], P('dp'), may hold values from 0 to 999
- token_table: bfloat16 [27, 768], replicated, may hold values from -6 to 6
- time_table: bfloat16 [1000, 768], replicated, may hold values from -3 to 3
- attn_gain: bfloat16 [4, 384], P('section'), may hold values from 0.5 to 1.5
- attn_shift: bfloat16 [4, 384], P('section'), may hold values from -1 to 1
- qkv_weight: bfloat16 [4, 384, 2304], P('section'), may hold values from -0.21875 to 0.21875
- query_bias: bfloat16 [4, 384], P('section'), may hold values from -2.5 to 2.5
- value_bias: bfloat16 [4, 384], P('section'), may hold values from -1.5 to 1.5
- proj_weight: bfloat16 [4, 384, 768], P('section'), may hold values from -1.75 to 1.75
- proj_bias: bfloat16 [4, 384], P('section'), may hold values from -1 to 1
- mlp_gain: bfloat16 [4, 384], P('section'), may hold values from 0.5 to 1.5
- mlp_shift: bfloat16 [4, 384], P('section'), may hold values from -1 to 1
- up_weight: bfloat16 [4, 384, 3072], P('section'), may hold values from -0.21875 to 0.21875
- up_bias: bfloat16 [4, 1536], P('section'), may hold values from -2.5 to 2.5
- down_weight: bfloat16 [4, 1536, 768], P('section'), may hold values from -0.109375 to 0.109375
- down_bias: bfloat16 [4, 384], P('section'), may hold values from -1 to 1
- cotangent: bfloat16 [64, 256, 768], P('dp'), may hold values from -6 to 6
Outputs:
- activations: float32 [64, 256, 768], P('dp', None, 'section')
- token_table_grad: float32 [27, 768], P(None, 'section')
- time_table_grad: float32 [1000, 768], P(None, 'section')
- attn_gain_grad: float32 [4, 384], P('section', 'dp')
- attn_shift_grad: float32 [4, 384], P('section', 'dp')
- qkv_weight_grad: float32 [4, 384, 2304], P('section', 'dp')
- query_bias_grad: float32 [4, 384], P('section', 'dp')
- value_bias_grad: float32 [4, 384], P('section', 'dp')
- proj_weight_grad: float32 [4, 384, 768], P('section', 'dp')
- proj_bias_grad: float32 [4, 384], P('section', 'dp')
- mlp_gain_grad: float32 [4, 384], P('section', 'dp')
- mlp_shift_grad: float32 [4, 384], P('section', 'dp')
- up_weight_grad: float32 [4, 384, 3072], P('section', 'dp')
- up_bias_grad: float32 [4, 1536], P('section', 'dp')
- down_weight_grad: float32 [4, 1536, 768], P('section', 'dp')
- down_bias_grad: float32 [4, 384], P('section', 'dp')
Inputs may be any that keep to these rules, and one draw needn't show every extreme that they name: `timesteps`: a row of time_table for each sequence.
All inputs are finite; a program needn't handle non-finite values.
Results may differ from a plain program's by a relative error of at most 0.014.
Values may be sent and summed in bfloat16 or wider, within the bound.
A program may use at most 192 MiB of HBM per device.

v0:
```python
import math

import jax
import jax.numpy as jnp
from jax import lax
from jax.sharding import PartitionSpec as P

HEADS = 12
MB_ROWS = 2


EPS = 1e-05
HIGHEST = lax.Precision.HIGHEST


def swapped(value, axis, bit):
    mask = 2**bit
    pairs = [(source, source ^ mask) for source in range(lax.axis_size(axis))]
    return lax.ppermute(value, axis, pairs)


def passed_along(block, axis, distance):
    devices = range(lax.axis_size(axis))
    route = [(i - distance, i) for i in devices if i - distance in devices]
    return lax.ppermute(block, axis, route)


def layer_norm(inputs, gain, shift):
    mean = jnp.mean(inputs, axis=-1, keepdims=True)
    centered = inputs - mean
    spread = jnp.mean(centered * centered, axis=-1, keepdims=True)
    return centered * lax.rsqrt(spread + EPS) * gain + shift


def norm_back(inputs, gain, shift, grad):
    _, pull = jax.vjp(layer_norm, inputs, gain, shift)
    return pull(grad)


def gelu_tanh(values):
    return jax.nn.gelu(values, approximate=True)


def attend_front(inputs, attn):
    gain, shift, w_joint, b_query, b_value = attn[:5]
    batch, length, width = inputs.shape
    size = width // HEADS
    scale = 1.0 / math.sqrt(size)
    normal = layer_norm(inputs, gain.astype(jnp.float32), shift.astype(jnp.float32))
    normal = normal.astype(jnp.bfloat16).reshape(batch * length, width)
    joint = jnp.dot(normal, w_joint, preferred_element_type=jnp.float32)
    query = (
        (joint[:, :width] + b_query.astype(jnp.float32))
        .astype(jnp.bfloat16)
        .reshape(batch, length, HEADS, size)
    )
    keys = joint[:, width : 2 * width].astype(jnp.bfloat16).reshape(batch, length, HEADS, size)
    values = (
        (joint[:, 2 * width :] + b_value.astype(jnp.float32))
        .astype(jnp.bfloat16)
        .reshape(batch, length, HEADS, size)
    )
    scores = jnp.einsum("bqhd,bkhd->bhqk", query, keys, preferred_element_type=jnp.float32) * scale
    largest = jnp.max(scores, axis=-1, keepdims=True)
    expo = jnp.exp(scores - largest)
    probs = expo / jnp.sum(expo, axis=-1, keepdims=True)
    probs_low = probs.astype(jnp.bfloat16)
    mixed = jnp.einsum("bhqk,bkhd->bqhd", probs_low, values, preferred_element_type=jnp.float32)
    mixed = mixed.astype(jnp.bfloat16).reshape(batch * length, width)
    return (normal, query, keys, values, probs, probs_low, mixed, scale)


def attend_forward(inputs, attn):
    mixed = attend_front(inputs, attn)[6]
    branch = jnp.dot(mixed, attn[5], preferred_element_type=jnp.float32) + attn[6].astype(
        jnp.float32
    )
    return inputs + branch.reshape(inputs.shape)


def attend_back(inputs, attn, grad):
    gain, shift, w_joint, b_query, b_value, w_proj, b_proj = attn
    batch, length, width = inputs.shape
    normal, query, keys, values, probs, probs_low, mixed, scale = attend_front(inputs, attn)
    d_branch = grad.reshape(batch * length, width).astype(jnp.bfloat16)
    g_proj_bias = jnp.sum(d_branch.astype(jnp.float32), axis=0)
    g_proj = jnp.einsum("td,te->de", mixed, d_branch, preferred_element_type=jnp.float32)
    d_mixed = jnp.einsum("te,de->td", d_branch, w_proj, preferred_element_type=jnp.float32)
    d_mixed = d_mixed.astype(jnp.bfloat16).reshape(query.shape)
    d_values = jnp.einsum(
        "bhqk,bqhd->bkhd", probs_low, d_mixed, preferred_element_type=jnp.float32
    ).astype(jnp.bfloat16)
    d_probs = jnp.einsum("bqhd,bkhd->bhqk", d_mixed, values, preferred_element_type=jnp.float32)
    d_scores = (probs * (d_probs - jnp.sum(probs * d_probs, axis=-1, keepdims=True))).astype(
        jnp.bfloat16
    )
    d_query = (
        jnp.einsum("bhqk,bkhd->bqhd", d_scores, keys, preferred_element_type=jnp.float32) * scale
    ).astype(jnp.bfloat16)
    d_keys = (
        jnp.einsum("bhqk,bqhd->bkhd", d_scores, query, preferred_element_type=jnp.float32) * scale
    ).astype(jnp.bfloat16)
    flat_query = d_query.reshape(batch * length, width)
    flat_values = d_values.reshape(batch * length, width)
    d_joint = jnp.concatenate(
        [flat_query, d_keys.reshape(batch * length, width), flat_values], axis=1
    )
    g_query_bias = jnp.sum(flat_query.astype(jnp.float32), axis=0)
    g_value_bias = jnp.sum(flat_values.astype(jnp.float32), axis=0)
    g_joint = jnp.einsum("td,te->de", normal, d_joint, preferred_element_type=jnp.float32)
    d_normal = jnp.einsum(
        "te,de->td", d_joint, w_joint, preferred_element_type=jnp.float32
    ).reshape(inputs.shape)
    d_inputs, g_gain, g_shift = norm_back(
        inputs, gain.astype(jnp.float32), shift.astype(jnp.float32), d_normal
    )
    return (
        grad + d_inputs,
        (g_gain, g_shift, g_joint, g_query_bias, g_value_bias, g_proj, g_proj_bias),
    )


def feed_front(inputs, mlp):
    gain, shift, w_up, b_up = mlp[:4]
    batch, length, width = inputs.shape
    normal = layer_norm(inputs, gain.astype(jnp.float32), shift.astype(jnp.float32))
    normal = normal.astype(jnp.bfloat16).reshape(batch * length, width)
    before = jnp.dot(normal, w_up, preferred_element_type=jnp.float32) + b_up.astype(jnp.float32)
    after = gelu_tanh(before).astype(jnp.bfloat16)
    return (normal, before, after)


def feed_forward(inputs, mlp):
    after = feed_front(inputs, mlp)[2]
    branch = jnp.dot(after, mlp[4], preferred_element_type=jnp.float32) + mlp[5].astype(jnp.float32)
    return inputs + branch.reshape(inputs.shape)


def feed_back(inputs, mlp, grad):
    gain, shift, w_up, b_up, w_down, b_down = mlp
    width = inputs.shape[2]
    normal, before, after = feed_front(inputs, mlp)
    d_branch = grad.reshape(-1, width).astype(jnp.bfloat16)
    g_down_bias = jnp.sum(d_branch.astype(jnp.float32), axis=0)
    g_down = jnp.einsum("tf,td->fd", after, d_branch, preferred_element_type=jnp.float32)
    d_after = jnp.einsum("td,fd->tf", d_branch, w_down, preferred_element_type=jnp.float32)
    _, pull = jax.vjp(gelu_tanh, before)
    d_before = pull(d_after)[0].astype(jnp.bfloat16)
    g_up_bias = jnp.sum(d_before.astype(jnp.float32), axis=0)
    g_up = jnp.einsum("td,tf->df", normal, d_before, preferred_element_type=jnp.float32)
    d_normal = jnp.einsum("tf,df->td", d_before, w_up, preferred_element_type=jnp.float32).reshape(
        inputs.shape
    )
    d_inputs, g_gain, g_shift = norm_back(
        inputs, gain.astype(jnp.float32), shift.astype(jnp.float32), d_normal
    )
    return (grad + d_inputs, (g_gain, g_shift, g_up, g_up_bias, g_down, g_down_bias))


def embed(token_rows, time_rows, token_table, time_table):
    letters = jnp.arange(token_table.shape[0], dtype=jnp.int32)
    onehot = (token_rows[..., None] == letters).astype(jnp.bfloat16)
    tokens = jnp.einsum("blv,vd->bld", onehot, token_table, preferred_element_type=jnp.float32)
    return tokens + jnp.take(time_table, time_rows, axis=0).astype(jnp.float32)[:, None, :]


def table_grads(token_rows, time_rows, grad, letters_count, times_count):
    letters = jnp.arange(letters_count, dtype=jnp.int32)
    onehot = (token_rows[..., None] == letters).astype(jnp.float32)
    token_part = jnp.einsum("blv,bld->vd", onehot, grad, precision=HIGHEST)
    moments = jnp.arange(times_count, dtype=jnp.int32)
    time_onehot = (time_rows[:, None] == moments).astype(jnp.float32)
    time_part = jnp.einsum("bt,bd->td", time_onehot, jnp.sum(grad, axis=1), precision=HIGHEST)
    return (token_part, time_part)


def per_device(
    token_ids,
    timesteps,
    token_table,
    time_table,
    attn_gain,
    attn_shift,
    qkv_weight,
    query_bias,
    value_bias,
    proj_weight,
    proj_bias,
    mlp_gain,
    mlp_shift,
    up_weight,
    up_bias,
    down_weight,
    down_bias,
    cotangent,
):
    sections = lax.axis_size("section")
    section = lax.axis_index("section")
    lower = section % 2 == 0
    mine = (
        attn_gain[0],
        attn_shift[0],
        qkv_weight[0],
        query_bias[0],
        value_bias[0],
        proj_weight[0],
        proj_bias[0],
        mlp_gain[0],
        mlp_shift[0],
        up_weight[0],
        up_bias[0],
        down_weight[0],
        down_bias[0],
    )
    partner = swapped(
        (
            attn_gain[0],
            attn_shift[0],
            qkv_weight[0],
            query_bias[0],
            value_bias[0],
            proj_weight[0],
            proj_bias[0],
            mlp_gain[0],
            mlp_shift[0],
            up_weight[0],
            up_bias[0],
            down_weight[0],
            down_bias[0],
        ),
        "section",
        0,
    )
    whole = tuple(
        (
            jnp.concatenate(
                [jnp.where(lower, ours, theirs), jnp.where(lower, theirs, ours)], axis=0
            )
            for ours, theirs in zip(mine, partner)
        )
    )
    attn = whole[:7]
    mlp = whole[7:]
    rows_dev, length = token_ids.shape
    width = cotangent.shape[2]
    micro = rows_dev // MB_ROWS
    turns = micro + sections - 1
    letters_count = token_table.shape[0]
    times_count = time_table.shape[0]

    def attend_run(inputs):
        return attend_forward(inputs, attn)

    def feed_run(inputs):
        return feed_forward(inputs, mlp)

    def spare_run(inputs):
        return jnp.zeros_like(inputs)

    def forward_step(count, carry):
        received, kept, finals = carry
        index = count - section
        valid = (index >= 0) & (index < micro)
        slot = jnp.clip(index, 0, micro - 1)
        start = slot * MB_ROWS
        token_rows = lax.dynamic_slice_in_dim(token_ids, start, MB_ROWS, 0)
        time_rows = lax.dynamic_slice_in_dim(timesteps, start, MB_ROWS, 0)
        first = embed(token_rows, time_rows, token_table, time_table)
        inputs = jnp.where(section == 0, first, received.astype(jnp.float32))
        which = jnp.where(valid, section % 2, 2)
        outputs = lax.switch(which, [attend_run, feed_run, spare_run], inputs)
        previous = lax.dynamic_index_in_dim(kept, slot, 0, keepdims=False)
        kept = lax.dynamic_update_index_in_dim(kept, jnp.where(valid, inputs, previous), slot, 0)
        landed = lax.dynamic_index_in_dim(finals, slot, 0, keepdims=False)
        closing = valid & (section == sections - 1)
        finals = lax.dynamic_update_index_in_dim(
            finals, jnp.where(closing, outputs, landed), slot, 0
        )
        sent = passed_along(outputs.astype(jnp.bfloat16), "section", 1)
        return (sent, kept, finals)

    start_carry = (
        jnp.zeros((MB_ROWS, length, width), jnp.bfloat16),
        jnp.zeros((micro, MB_ROWS, length, width), jnp.float32),
        jnp.zeros((micro, MB_ROWS, length, width), jnp.float32),
    )
    _, kept, finals = lax.fori_loop(0, turns, forward_step, start_carry)

    def attend_grad(inputs, grad, attn_total, mlp_total):
        d_inputs, grads = attend_back(inputs, attn, grad)
        return (
            d_inputs,
            tuple((total + part for total, part in zip(attn_total, grads))),
            mlp_total,
        )

    def feed_grad(inputs, grad, attn_total, mlp_total):
        d_inputs, grads = feed_back(inputs, mlp, grad)
        return (
            d_inputs,
            attn_total,
            tuple((total + part for total, part in zip(mlp_total, grads))),
        )

    def spare_grad(inputs, grad, attn_total, mlp_total):
        return (jnp.zeros_like(inputs), attn_total, mlp_total)

    def backward_step(count, carry):
        received, attn_total, mlp_total, table_total = carry
        index = count - (sections - 1 - section)
        valid = (index >= 0) & (index < micro)
        slot = jnp.clip(index, 0, micro - 1)
        start = slot * MB_ROWS
        seed = lax.dynamic_slice_in_dim(cotangent, start, MB_ROWS, 0).astype(jnp.float32)
        grad = jnp.where(section == sections - 1, seed, received.astype(jnp.float32))
        inputs = lax.dynamic_index_in_dim(kept, slot, 0, keepdims=False)
        which = jnp.where(valid, section % 2, 2)
        d_inputs, attn_total, mlp_total = lax.switch(
            which, [attend_grad, feed_grad, spare_grad], inputs, grad, attn_total, mlp_total
        )
        token_rows = lax.dynamic_slice_in_dim(token_ids, start, MB_ROWS, 0)
        time_rows = lax.dynamic_slice_in_dim(timesteps, start, MB_ROWS, 0)

        def add_tables(totals):
            token_part, time_part = table_grads(
                token_rows, time_rows, d_inputs, letters_count, times_count
            )
            return (totals[0] + token_part, totals[1] + time_part)

        def keep_tables(totals):
            return totals

        table_total = lax.cond(valid & (section == 0), add_tables, keep_tables, table_total)
        sent = passed_along(d_inputs.astype(jnp.bfloat16), "section", -1)
        return (sent, attn_total, mlp_total, table_total)

    attn_zero = tuple((jnp.zeros(weight.shape, jnp.float32) for weight in attn))
    mlp_zero = tuple((jnp.zeros(weight.shape, jnp.float32) for weight in mlp))
    table_zero = (
        jnp.zeros((letters_count, width), jnp.float32),
        jnp.zeros((times_count, width), jnp.float32),
    )
    back_start = (
        jnp.zeros((MB_ROWS, length, width), jnp.bfloat16),
        attn_zero,
        mlp_zero,
        table_zero,
    )
    _, attn_total, mlp_total, table_total = lax.fori_loop(0, turns, backward_step, back_start)
    activations = lax.psum_scatter(
        finals.reshape(rows_dev, length, width).astype(jnp.bfloat16),
        "section",
        scatter_dimension=2,
        tiled=True,
    ).astype(jnp.float32)
    token_quarter, time_quarter = (
        lax.psum_scatter(
            table_total[0].astype(jnp.bfloat16), "section", scatter_dimension=1, tiled=True
        ).astype(jnp.float32),
        lax.psum_scatter(
            table_total[1].astype(jnp.bfloat16), "section", scatter_dimension=1, tiled=True
        ).astype(jnp.float32),
    )
    token_grad, time_grad = lax.psum((token_quarter, time_quarter), "dp")
    totals = attn_total + mlp_total
    halves = tuple((grad.reshape((2, grad.shape[0] // 2) + grad.shape[1:]) for grad in totals))
    summed = (
        lax.psum_scatter(halves[0], "dp", scatter_dimension=1, tiled=True),
        lax.psum_scatter(halves[1], "dp", scatter_dimension=1, tiled=True),
        lax.psum_scatter(halves[2], "dp", scatter_dimension=1, tiled=True),
        lax.psum_scatter(halves[3], "dp", scatter_dimension=1, tiled=True),
        lax.psum_scatter(halves[4], "dp", scatter_dimension=1, tiled=True),
        lax.psum_scatter(halves[5], "dp", scatter_dimension=1, tiled=True),
        lax.psum_scatter(halves[6], "dp", scatter_dimension=1, tiled=True),
        lax.psum_scatter(halves[7], "dp", scatter_dimension=1, tiled=True),
        lax.psum_scatter(halves[8], "dp", scatter_dimension=1, tiled=True),
        lax.psum_scatter(halves[9], "dp", scatter_dimension=1, tiled=True),
        lax.psum_scatter(halves[10], "dp", scatter_dimension=1, tiled=True),
        lax.psum_scatter(halves[11], "dp", scatter_dimension=1, tiled=True),
        lax.psum_scatter(halves[12], "dp", scatter_dimension=1, tiled=True),
    )
    kept_half = tuple((jnp.where(lower, pair[0], pair[1]) for pair in summed))
    given = tuple((jnp.where(lower, pair[1], pair[0]) for pair in summed))
    arrived = (
        swapped(given[0].astype(jnp.bfloat16), "section", 0).astype(jnp.float32),
        swapped(given[1].astype(jnp.bfloat16), "section", 0).astype(jnp.float32),
        swapped(given[2].astype(jnp.bfloat16), "section", 0).astype(jnp.float32),
        swapped(given[3].astype(jnp.bfloat16), "section", 0).astype(jnp.float32),
        swapped(given[4].astype(jnp.bfloat16), "section", 0).astype(jnp.float32),
        swapped(given[5].astype(jnp.bfloat16), "section", 0).astype(jnp.float32),
        swapped(given[6].astype(jnp.bfloat16), "section", 0).astype(jnp.float32),
        swapped(given[7].astype(jnp.bfloat16), "section", 0).astype(jnp.float32),
        swapped(given[8].astype(jnp.bfloat16), "section", 0).astype(jnp.float32),
        swapped(given[9].astype(jnp.bfloat16), "section", 0).astype(jnp.float32),
        swapped(given[10].astype(jnp.bfloat16), "section", 0).astype(jnp.float32),
        swapped(given[11].astype(jnp.bfloat16), "section", 0).astype(jnp.float32),
        swapped(given[12].astype(jnp.bfloat16), "section", 0).astype(jnp.float32),
    )
    result = tuple(((ours + theirs)[None] for ours, theirs in zip(kept_half, arrived)))
    return (
        activations,
        token_grad,
        time_grad,
        result[0],
        result[1],
        result[2],
        result[3],
        result[4],
        result[5],
        result[6],
        result[7],
        result[8],
        result[9],
        result[10],
        result[11],
        result[12],
    )


def solution(mesh):
    return jax.shard_map(
        per_device,
        mesh=mesh,
        in_specs=(
            P("dp", None),
            P("dp"),
            P(),
            P(),
            P("section", None),
            P("section", None),
            P("section", None, None),
            P("section", None),
            P("section", None),
            P("section", None, None),
            P("section", None),
            P("section", None),
            P("section", None),
            P("section", None, None),
            P("section", None),
            P("section", None, None),
            P("section", None),
            P("dp", None, None),
        ),
        out_specs=(
            P("dp", None, "section"),
            P(None, "section"),
            P(None, "section"),
            P("section", "dp"),
            P("section", "dp"),
            P("section", "dp", None),
            P("section", "dp"),
            P("section", "dp"),
            P("section", "dp", None),
            P("section", "dp"),
            P("section", "dp"),
            P("section", "dp"),
            P("section", "dp", None),
            P("section", "dp"),
            P("section", "dp", None),
            P("section", "dp"),
        ),
        check_vma=False,
    )
```

profile of v0, /device:TPU:0, one launch (start us, length us, event | category | flops | bytes accessed | tf_op | source)
XLA Modules:
  0.0 1941.8 jit_solution(7969792027314247134)
XLA Ops:
  28.4 50.0 %collective-permute-done.7 = bf16[384,768]{1,0:T(8,128)(2,1)S(1)} collective-permute-done((bf16[384,768]{1,0:T(8,128)(2,1)S(1)}, bf16[384,768]{1,0:T(8,128)(2,1)S(1)}, u32[]{:S(2)}, u32[]{:S(2)}) %collective-permute-start.7) | collective-permute-done | bytes 589856 | tf_op jit(solution)/shard_map/ppermute | solution.py:19
  81.8 47.2 %collective-permute-done.13 = bf16[1536,768]{1,0:T(8,128)(2,1)S(1)} collective-permute-done((bf16[1536,768]{1,0:T(8,128)(2,1)S(1)}, bf16[1536,768]{1,0:T(8,128)(2,1)S(1)}, u32[]{:S(2)}, u32[]{:S(2)}) %collective-permute-start.13) | collective-permute-done | bytes 2359328 | tf_op jit(solution)/shard_map/ppermute | solution.py:19
  131.8 44.0 %collective-permute-done.11 = bf16[384,3072]{1,0:T(8,128)(2,1)S(1)} collective-permute-done((bf16[384,3072]{1,0:T(8,128)(2,1)}, bf16[384,3072]{1,0:T(8,128)(2,1)S(1)}, u32[]{:S(2)}, u32[]{:S(2)}) %collective-permute-start.11) | collective-permute-done | bytes 2359328 | tf_op jit(solution)/shard_map/ppermute | solution.py:19
  182.8 301.7 %while.64 = (s32[]{:T(128)}, bf16[2,256,768]{2,1,0:T(8,128)(2,1)}, f32[4,2,256,768]{3,2,1,0:T(8,128)}, bf16[4,2,256,768]{3,2,1,0:T(8,128)(2,1)}, s32[]{:T(128)},...) while((s32[]{:T(128)}, bf16[2,256,768]{2,1,0:T(8,128)(2,1)}, ...), condition=%wide.region_10.11_spmd, body=%wide.region_0.10_spmd.sunk | while | flops 4875116032 | bytes 110280952 | solution.py:287
  202.2 22.3 %conditional.6 = (bf16[2,256,768]{2,1,0:T(8,128)(2,1)S(1)}) conditional(s32[]{:T(128)} %clamp.24, (f32[2,256,768]{2,1,0:T(8,128)S(1)}, bf16[768]{0:T(1024)(128)(2,1)S(1)}, bf16[768]{0:T(1024)(128)(2,1)S(1)}, bf16[768,2304]{1,0:T(8,128)(2,1)}, bf16[768]{0:T(1024)(128)(2,1)S(1)}, /*index=5*/bf16[768]{0:T(1024)(128)(2,1)S(1)}, ...), branch_computations={%region_1.5_spmd, %region_6.8_spmd, %region_9.9_spmd} | conditional | flops 4851898368 | bytes 91332192 | solution.py:271
  228.2 11.3 collective-permute-done
  247.7 22.3 %conditional.6 = (bf16[2,256,768]{2,1,0:T(8,128)(2,1)S(1)}) conditional(s32[]{:T(128)} %clamp.24, (f32[2,256,768]{2,1,0:T(8,128)S(1)}, bf16[768]{0:T(1024)(128)(2,1)S(1)}, bf16[768]{0:T(1024)(128)(2,1)S(1)}, bf16[768,2304]{1,0:T(8,128)(2,1)}, bf16[768]{0:T(1024)(128)(2,1)S(1)}, /*index=5*/bf16[768]{0:T(1024)(128)(2,1)S(1)}, ...), branch_computations={%region_1.5_spmd, %region_6.8_spmd, %region_9.9_spmd} | conditional | flops 4851898368 | bytes 91332192 | solution.py:271
  273.6 10.7 collective-permute-done
  292.5 22.3 %conditional.6 = (bf16[2,256,768]{2,1,0:T(8,128)(2,1)S(1)}) conditional(s32[]{:T(128)} %clamp.24, (f32[2,256,768]{2,1,0:T(8,128)S(1)}, bf16[768]{0:T(1024)(128)(2,1)S(1)}, bf16[768]{0:T(1024)(128)(2,1)S(1)}, bf16[768,2304]{1,0:T(8,128)(2,1)}, bf16[768]{0:T(1024)(128)(2,1)S(1)}, /*index=5*/bf16[768]{0:T(1024)(128)(2,1)S(1)}, ...), branch_computations={%region_1.5_spmd, %region_6.8_spmd, %region_9.9_spmd} | conditional | flops 4851898368 | bytes 91332192 | solution.py:271
  318.5 10.0 collective-permute-done
  336.7 22.3 %conditional.6 = (bf16[2,256,768]{2,1,0:T(8,128)(2,1)S(1)}) conditional(s32[]{:T(128)} %clamp.24, (f32[2,256,768]{2,1,0:T(8,128)S(1)}, bf16[768]{0:T(1024)(128)(2,1)S(1)}, bf16[768]{0:T(1024)(128)(2,1)S(1)}, bf16[768,2304]{1,0:T(8,128)(2,1)}, bf16[768]{0:T(1024)(128)(2,1)S(1)}, /*index=5*/bf16[768]{0:T(1024)(128)(2,1)S(1)}, ...), branch_computations={%region_1.5_spmd, %region_6.8_spmd, %region_9.9_spmd} | conditional | flops 4851898368 | bytes 91332192 | solution.py:271
  362.6 9.4 collective-permute-done
  380.2 17.1 collective-permute-start
  399.7 8.5 collective-permute-done
  416.4 12.6 collective-permute-start
  431.2 7.2 collective-permute-done
  446.6 27.6 %collective-permute-start = (bf16[2,256,768]{2,1,0:T(8,128)(2,1)S(1)}, bf16[2,256,768]{2,1,0:T(8,128)(2,1)S(1)}, u32[]{:S(2)}, u32[]{:S(2)}) collective-permute-start(bf16[2,256,768]{2,1,0:T(8,128)(2,1)S(1)} %get-tuple-element.2554), channel_id=1, source_target_pairs={{0,8},{8,16},{16,24},{1,9},{9,17},{17,25},{2,10},{10,18},{18,26},{... | collective-permute-start | bytes 2359304 | tf_op jit(solution)/shard_map/while/body/eval_jaxpr/ppermute | solution.py:25
  476.5 7.2 collective-permute-done
  502.1 719.1 %while.65 = (s32[]{:T(128)}, bf16[2,256,768]{2,1,0:T(8,128)(2,1)}, f32[768]{0:T(1024)S(1)}, f32[768]{0:T(1024)S(1)}, f32[768,2304]{1,0:T(8,128)}, /*index=5*/f32...) while((s32[]{:T(128)}, bf16[2,256,768]{2,1,0:T(8,128)(2,1)}, ...), condition=%wide.region_39.40_spmd, body=%wide.region_12.39_spmd.sunk | while | flops 12298592256 | bytes 354661120 | solution.py:349
  505.5 19.2 conditional.7
  527.7 14.1 collective-permute-done.1
  545.9 19.2 conditional.7
  568.1 22.3 %collective-permute-done.1 = bf16[2,256,768]{2,1,0:T(8,128)(2,1)S(1)} collective-permute-done((bf16[2,256,768]{2,1,0:T(8,128)(2,1)S(1)}, bf16[2,256,768]{2,1,0:T(8,128)(2,1)S(1)}, u32[]{:S(2)}, u32[]{:S(2)}) %collective-permute-start.1) | collective-permute-done | bytes 786464 | tf_op jit(solution)/shard_map/while/body/eval_jaxpr/ppermute | solution.py:25
  594.6 11.9 conditional.7
  609.4 149.2 %collective-permute-done.1 = bf16[2,256,768]{2,1,0:T(8,128)(2,1)S(1)} collective-permute-done((bf16[2,256,768]{2,1,0:T(8,128)(2,1)S(1)}, bf16[2,256,768]{2,1,0:T(8,128)(2,1)S(1)}, u32[]{:S(2)}, u32[]{:S(2)}) %collective-permute-start.1) | collective-permute-done | bytes 786464 | tf_op jit(solution)/shard_map/while/body/eval_jaxpr/ppermute | solution.py:25
  763.2 94.2 %conditional.7 = (f32[2,256,768]{2,1,0:T(8,128)}, f32[768]{0:T(1024)S(1)}, f32[768]{0:T(1024)S(1)}, f32[768,2304]{1,0:T(8,128)}, f32[768]{0:T(1024)S(1)}, /*inde...) conditional(s32[]{:T(128)} %clamp.25, ...), branch_computations={%region_13.25_spmd, %region_26.34_spmd, %region_35.35_spmd} | conditional | flops 12149989376 | bytes 323952320 | solution.py:318
  877.0 94.2 %conditional.7 = (f32[2,256,768]{2,1,0:T(8,128)}, f32[768]{0:T(1024)S(1)}, f32[768]{0:T(1024)S(1)}, f32[768,2304]{1,0:T(8,128)}, f32[768]{0:T(1024)S(1)}, /*inde...) conditional(s32[]{:T(128)} %clamp.25, ...), branch_computations={%region_13.25_spmd, %region_26.34_spmd, %region_35.35_spmd} | conditional | flops 12149989376 | bytes 323952320 | solution.py:318
  928.0 6.8 multiply_reduce_fusion.3
  991.5 94.2 %conditional.7 = (f32[2,256,768]{2,1,0:T(8,128)}, f32[768]{0:T(1024)S(1)}, f32[768]{0:T(1024)S(1)}, f32[768,2304]{1,0:T(8,128)}, f32[768]{0:T(1024)S(1)}, /*inde...) conditional(s32[]{:T(128)} %clamp.25, ...), branch_computations={%region_13.25_spmd, %region_26.34_spmd, %region_35.35_spmd} | conditional | flops 12149989376 | bytes 323952320 | solution.py:318
  1042.7 6.8 multiply_reduce_fusion.3
  1105.7 94.2 %conditional.7 = (f32[2,256,768]{2,1,0:T(8,128)}, f32[768]{0:T(1024)S(1)}, f32[768]{0:T(1024)S(1)}, f32[768,2304]{1,0:T(8,128)}, f32[768]{0:T(1024)S(1)}, /*inde...) conditional(s32[]{:T(128)} %clamp.25, ...), branch_computations={%region_13.25_spmd, %region_26.34_spmd, %region_35.35_spmd} | conditional | flops 12149989376 | bytes 323952320 | solution.py:318
  1156.6 6.8 multiply_reduce_fusion.3
  1239.9 11.8 reduce-scatter.69.cloned.1.call-done
  1254.2 28.3 %reduce-scatter.65.cloned.1.call-done = f32[48,2]{1,0:T(8,128)} async-done(((f32[384,2]{1,0:T(8,128)}), f32[48,2]{1,0:T(8,128)}) %reduce-scatter.65.cloned.1.call-update) | async-done | bytes 400
  1284.9 28.2 %reduce-scatter.63.cloned.1.call-done = f32[48,2]{1,0:T(8,128)} async-done(((f32[384,2]{1,0:T(8,128)}), f32[48,2]{1,0:T(8,128)}) %reduce-scatter.63.cloned.1.call-update) | async-done | bytes 400
  1315.6 28.1 %reduce-scatter.61.cloned.1.call-done = f32[48,2]{1,0:T(8,128)} async-done(((f32[384,2]{1,0:T(8,128)}), f32[48,2]{1,0:T(8,128)}) %reduce-scatter.61.cloned.1.call-update) | async-done | bytes 400
  1346.2 28.0 %reduce-scatter.59.cloned.1.call-done = f32[48,2]{1,0:T(8,128)} async-done(((f32[384,2]{1,0:T(8,128)}), f32[48,2]{1,0:T(8,128)}) %reduce-scatter.59.cloned.1.call-update) | async-done | bytes 400
  1376.7 28.2 %reduce-scatter.57.cloned.1.call-done = f32[48,2]{1,0:T(8,128)} async-done(((f32[384,2]{1,0:T(8,128)}), f32[48,2]{1,0:T(8,128)}) %reduce-scatter.57.cloned.1.call-update) | async-done | bytes 400
  1405.9 30.2 %reduce-scatter.55.cloned.1.call-done = f32[48,2]{1,0:T(8,128)} async-done(((f32[384,2]{1,0:T(8,128)}), f32[48,2]{1,0:T(8,128)}) %reduce-scatter.55.cloned.1.call-update) | async-done | bytes 400
  1437.2 30.3 %reduce-scatter.53.cloned.1.call-done = f32[48,2]{1,0:T(8,128)} async-done(((f32[384,2]{1,0:T(8,128)}), f32[48,2]{1,0:T(8,128)}) %reduce-scatter.53.cloned.1.call-update) | async-done | bytes 400
  1476.2 23.7 %reduce-scatter.67.cloned.1.call-done = f32[192,2]{1,0:T(8,128)} async-done(((f32[1536,2]{1,0:T(8,128)}), f32[192,2]{1,0:T(8,128)}) %reduce-scatter.67.cloned.1.call-update) | async-done | bytes 1552
  1502.8 33.9 %reduce-scatter.43.cloned.1.call-done = f32[2,48,768]{2,1,0:T(8,128)} async-done(((f32[2,384,768]{2,1,0:T(8,128)}), f32[2,48,768]{2,1,0:T(8,128)}) %reduce-scatter.43.cloned.1.call-update) | async-done | bytes 294928 | tf_op jit(solution)/shard_map/reduce_scatter | solution.py:373
  1539.9 23.6 %reduce-scatter.49.cloned.1.call-done = bf16[192,27]{1,0:T(8,128)(2,1)} async-done(((bf16[768,27]{1,0:T(8,128)(2,1)}), bf16[192,27]{1,0:T(8,128)(2,1)}) %reduce-scatter.49.cloned.1.call-update) | async-done | bytes 10384
  1564.3 33.8 %reduce-scatter.51.cloned.1.call-done = bf16[192,1000]{1,0:T(8,128)(2,1)} async-done(((bf16[768,1000]{1,0:T(8,128)(2,1)}), bf16[192,1000]{1,0:T(8,128)(2,1)}) %reduce-scatter.51.cloned.1.call-update) | async-done | bytes 384016
  1599.3 60.2 %all-reduce.2 = (f32[27,192]{1,0:T(8,128)}, f32[1000,192]{1,0:T(8,128)S(1)}) all-reduce(bf16[27,192]{1,0:T(8,128)(2,1)S(1)} %copy.178, bf16[1000,192]{1,0:T(8,128)(2,1)S(1)} %copy.180), channel_id=1, replica_groups=mesh['section'=4,'dp'=8] {'dp'}, use_global_device_ids=true, to_apply=%region_41.42 | all-reduce | flops 197184 | bytes 1183104 | tf_op jit(solution)/shard_map/psum | solution.py:364
  1663.9 61.9 %reduce-scatter.41.cloned.1.call-done = f32[2,48,2304]{2,1,0:T(8,128)} async-done(((f32[2,384,2304]{2,1,0:T(8,128)}), f32[2,48,2304]{2,1,0:T(8,128)}) %reduce-scatter.41.cloned.1.call-update) | async-done | bytes 884752 | tf_op jit(solution)/shard_map/reduce_scatter | solution.py:370
  1728.5 97.3 %reduce-scatter.45.cloned.1.call-done = f32[2,48,3072]{2,1,0:T(8,128)} async-done(((f32[2,384,3072]{2,1,0:T(8,128)}), f32[2,48,3072]{2,1,0:T(8,128)}) %reduce-scatter.45.cloned.1.call-update) | async-done | bytes 1179664 | tf_op jit(solution)/shard_map/reduce_scatter | solution.py:377
  1830.7 95.2 %reduce-scatter.47.cloned.1.call-done = f32[2,192,768]{2,1,0:T(8,128)} async-done(((f32[2,1536,768]{2,1,0:T(8,128)}), f32[2,192,768]{2,1,0:T(8,128)}) %reduce-scatter.47.cloned.1.call-update) | async-done | bytes 1179664 | tf_op jit(solution)/shard_map/reduce_scatter | solution.py:379
  (941 shorter events, 732.9 us)
Async XLA Ops:
  7.3 1244.4 %reduce-scatter.69.cloned.1.call-start = ((), (), s32[]{:S(2)}) async-start(), calls=%async_computation.31 | async-start | bytes 221184
  8.2 11.4 collective-permute-start.14
  11.8 7.8 collective-permute-start.10
  12.6 9.1 collective-permute-start.9
  21.9 6.5 collective-permute-start.12
  24.0 55.7 %collective-permute-start.4 = (bf16[384,2304]{1,0:T(8,128)(2,1)}, bf16[384,2304]{1,0:T(8,128)(2,1)S(1)}, u32[]{:S(2)}, u32[]{:S(2)}) collective-permute-start(bf16[384,2304]{1,0:T(8,128)(2,1)} %bitcast.323), channel_id=1, source_target_pairs={{0,8},{8,0},{16,24},{24,16},{1,9},{9,1},{17,25},{25,17},{2,10},{10... | collective-permute-start | bytes 5308424 | tf_op jit(solution)/shard_map/ppermute | solution.py:19
  24.1 54.3 %collective-permute-start.7 = (bf16[384,768]{1,0:T(8,128)(2,1)S(1)}, bf16[384,768]{1,0:T(8,128)(2,1)S(1)}, u32[]{:S(2)}, u32[]{:S(2)}) collective-permute-start(bf16[384,768]{1,0:T(8,128)(2,1)S(1)} %bitcast.333), channel_id=1, source_target_pairs={{0,8},{8,0},{16,24},{24,16},{1,9},{9,1},{17,25},{25,17},{2,10},{10... | collective-permute-start | bytes 1769480 | tf_op jit(solution)/shard_map/ppermute | solution.py:19
  26.2 102.8 %collective-permute-start.13 = (bf16[1536,768]{1,0:T(8,128)(2,1)S(1)}, bf16[1536,768]{1,0:T(8,128)(2,1)S(1)}, u32[]{:S(2)}, u32[]{:S(2)}) collective-permute-start(bf16[1536,768]{1,0:T(8,128)(2,1)S(1)} %bitcast.321), channel_id=1, source_target_pairs={{0,8},{8,0},{16,24},{24,16},{1,9},{9,1},{17,25},{25,17},{2,10},{10... | collective-permute-start | bytes 7077896 | tf_op jit(solution)/shard_map/ppermute | solution.py:19
  26.3 149.5 %collective-permute-start.11 = (bf16[384,3072]{1,0:T(8,128)(2,1)}, bf16[384,3072]{1,0:T(8,128)(2,1)S(1)}, u32[]{:S(2)}, u32[]{:S(2)}) collective-permute-start(bf16[384,3072]{1,0:T(8,128)(2,1)} %bitcast.322), channel_id=1, source_target_pairs={{0,8},{8,0},{16,24},{24,16},{1,9},{9,1},{17,25},{25,17},{2,10},{10... | collective-permute-start | bytes 7077896 | tf_op jit(solution)/shard_map/ppermute | solution.py:19
  224.5 15.0 collective-permute-start
  270.0 14.3 collective-permute-start
  314.9 13.7 collective-permute-start
  359.0 13.0 collective-permute-start
  380.2 27.9 %collective-permute-start = (bf16[2,256,768]{2,1,0:T(8,128)(2,1)S(1)}, bf16[2,256,768]{2,1,0:T(8,128)(2,1)S(1)}, u32[]{:S(2)}, u32[]{:S(2)}) collective-permute-start(bf16[2,256,768]{2,1,0:T(8,128)(2,1)S(1)} %get-tuple-element.2554), channel_id=1, source_target_pairs={{0,8},{8,16},{16,24},{1,9},{9,17},{17,25},{2,10},{10,18},{18,26},{... | collective-permute-start | bytes 2359304 | tf_op jit(solution)/shard_map/while/body/eval_jaxpr/ppermute | solution.py:25
  416.4 22.0 %collective-permute-start = (bf16[2,256,768]{2,1,0:T(8,128)(2,1)S(1)}, bf16[2,256,768]{2,1,0:T(8,128)(2,1)S(1)}, u32[]{:S(2)}, u32[]{:S(2)}) collective-permute-start(bf16[2,256,768]{2,1,0:T(8,128)(2,1)S(1)} %get-tuple-element.2554), channel_id=1, source_target_pairs={{0,8},{8,16},{16,24},{1,9},{9,17},{17,25},{2,10},{10,18},{18,26},{... | collective-permute-start | bytes 2359304 | tf_op jit(solution)/shard_map/while/body/eval_jaxpr/ppermute | solution.py:25
  446.6 37.1 %collective-permute-start = (bf16[2,256,768]{2,1,0:T(8,128)(2,1)S(1)}, bf16[2,256,768]{2,1,0:T(8,128)(2,1)S(1)}, u32[]{:S(2)}, u32[]{:S(2)}) collective-permute-start(bf16[2,256,768]{2,1,0:T(8,128)(2,1)S(1)} %get-tuple-element.2554), channel_id=1, source_target_pairs={{0,8},{8,16},{16,24},{1,9},{9,17},{17,25},{2,10},{10,18},{18,26},{... | collective-permute-start | bytes 2359304 | tf_op jit(solution)/shard_map/while/body/eval_jaxpr/ppermute | solution.py:25
  526.3 15.4 collective-permute-start.1
  566.8 23.6 %collective-permute-start.1 = (bf16[2,256,768]{2,1,0:T(8,128)(2,1)S(1)}, bf16[2,256,768]{2,1,0:T(8,128)(2,1)S(1)}, u32[]{:S(2)}, u32[]{:S(2)}) collective-permute-start(bf16[2,256,768]{2,1,0:T(8,128)(2,1)S(1)} %convert_element_type.540), channel_id=1, source_target_pairs={{8,0},{16,8},{24,16},{9,1},{17,9},{25,17},{10,2},{18,10},{26,18},{... | collective-permute-start | bytes 2359304 | tf_op jit(solution)/shard_map/while/body/eval_jaxpr/ppermute | solution.py:25
  608.1 150.6 %collective-permute-start.1 = (bf16[2,256,768]{2,1,0:T(8,128)(2,1)S(1)}, bf16[2,256,768]{2,1,0:T(8,128)(2,1)S(1)}, u32[]{:S(2)}, u32[]{:S(2)}) collective-permute-start(bf16[2,256,768]{2,1,0:T(8,128)(2,1)S(1)} %convert_element_type.540), channel_id=1, source_target_pairs={{8,0},{16,8},{24,16},{9,1},{17,9},{25,17},{10,2},{18,10},{26,18},{... | collective-permute-start | bytes 2359304 | tf_op jit(solution)/shard_map/while/body/eval_jaxpr/ppermute | solution.py:25
  859.0 13.9 collective-permute-start.1
  972.9 14.4 collective-permute-start.1
  1087.3 13.9 collective-permute-start.1
  1201.6 13.9 collective-permute-start.1
  1222.0 60.4 %reduce-scatter.65.cloned.1.call-start = ((), (), s32[]{:S(2)}) async-start(), calls=%async_computation.29 | async-start | bytes 221184
  1222.9 90.2 %reduce-scatter.63.cloned.1.call-start = ((), (), s32[]{:S(2)}) async-start(), calls=%async_computation.28 | async-start | bytes 221184
  1223.8 119.9 %reduce-scatter.61.cloned.1.call-start = ((), (), s32[]{:S(2)}) async-start(), calls=%async_computation.27 | async-start | bytes 221184
  1224.7 149.5 %reduce-scatter.59.cloned.1.call-start = ((), (), s32[]{:S(2)}) async-start(), calls=%async_computation.26 | async-start | bytes 221184
  1225.6 179.3 %reduce-scatter.57.cloned.1.call-start = ((), (), s32[]{:S(2)}) async-start(), calls=%async_computation.25 | async-start | bytes 221184
  1226.5 209.6 %reduce-scatter.55.cloned.1.call-start = ((), (), s32[]{:S(2)}) async-start(), calls=%async_computation.24 | async-start | bytes 221184
  1227.5 240.0 %reduce-scatter.53.cloned.1.call-start = ((), (), s32[]{:S(2)}) async-start(), calls=%async_computation.23 | async-start | bytes 221184
  1228.4 271.6 %reduce-scatter.67.cloned.1.call-start = ((), (), s32[]{:S(2)}) async-start(), calls=%async_computation.30 | async-start | bytes 884736
  1229.6 307.0 %reduce-scatter.43.cloned.1.call-start = ((), (), s32[]{:S(2)}) async-start(), calls=%async_computation.18 | async-start | bytes 2654208 | tf_op jit(solution)/shard_map/reduce_scatter | solution.py:373
  1230.2 333.2 %reduce-scatter.49.cloned.1.call-start = ((), (), s32[]{:S(2)}) async-start(), calls=%async_computation.21 | async-start | bytes 245760
  1231.2 367.0 %reduce-scatter.51.cloned.1.call-start = ((), (), s32[]{:S(2)}) async-start(), calls=%async_computation.22 | async-start | bytes 1966080
  1235.3 426.2 %reduce-scatter.39.cloned.1.call-start = ((), (), s32[]{:S(2)}) async-start(), calls=%async_computation.16 | async-start | bytes 3932160 | tf_op jit(solution)/shard_map/reduce_scatter | solution.py:350
  1238.1 487.6 %reduce-scatter.41.cloned.1.call-start = ((), (), s32[]{:S(2)}) async-start(), calls=%async_computation.17 | async-start | bytes 7962624 | tf_op jit(solution)/shard_map/reduce_scatter | solution.py:370
  1238.7 587.1 %reduce-scatter.45.cloned.1.call-start = ((), (), s32[]{:S(2)}) async-start(), calls=%async_computation.19 | async-start | bytes 10616832 | tf_op jit(solution)/shard_map/reduce_scatter | solution.py:377
  1239.3 686.7 %reduce-scatter.47.cloned.1.call-start = ((), (), s32[]{:S(2)}) async-start(), calls=%async_computation.20 | async-start | bytes 10616832 | tf_op jit(solution)/shard_map/reduce_scatter | solution.py:379
  1252.7 215.9 %collective-permute-start.27 = (bf16[48]{0:T(256)(128)(2,1)S(1)}, bf16[48]{0:T(256)(128)(2,1)S(1)}, u32[]{:S(2)}, u32[]{:S(2)}) collective-permute-start(bf16[48]{0:T(256)(128)(2,1)S(1)} %fusion.140), channel_id=1, source_target_pairs={{0,8},{8,0},{16,24},{24,16},{1,9},{9,1},{17,25},{25,17},{2,10},{10... | collective-permute-start | bytes 296 | tf_op jit(solution)/shard_map/ppermute | solution.py:19
  1283.5 187.1 %collective-permute-start.23 = (bf16[48]{0:T(256)(128)(2,1)S(1)}, bf16[48]{0:T(256)(128)(2,1)S(1)}, u32[]{:S(2)}, u32[]{:S(2)}) collective-permute-start(bf16[48]{0:T(256)(128)(2,1)S(1)} %fusion.135), channel_id=1, source_target_pairs={{0,8},{8,0},{16,24},{24,16},{1,9},{9,1},{17,25},{25,17},{2,10},{10... | collective-permute-start | bytes 296 | tf_op jit(solution)/shard_map/ppermute | solution.py:19
  1314.2 157.5 %collective-permute-start.22 = (bf16[48]{0:T(256)(128)(2,1)S(1)}, bf16[48]{0:T(256)(128)(2,1)S(1)}, u32[]{:S(2)}, u32[]{:S(2)}) collective-permute-start(bf16[48]{0:T(256)(128)(2,1)S(1)} %fusion.130), channel_id=1, source_target_pairs={{0,8},{8,0},{16,24},{24,16},{1,9},{9,1},{17,25},{25,17},{2,10},{10... | collective-permute-start | bytes 296 | tf_op jit(solution)/shard_map/ppermute | solution.py:19
  1344.8 128.8 %collective-permute-start.21 = (bf16[48]{0:T(256)(128)(2,1)S(1)}, bf16[48]{0:T(256)(128)(2,1)S(1)}, u32[]{:S(2)}, u32[]{:S(2)}) collective-permute-start(bf16[48]{0:T(256)(128)(2,1)S(1)} %fusion.125), channel_id=1, source_target_pairs={{0,8},{8,0},{16,24},{24,16},{1,9},{9,1},{17,25},{25,17},{2,10},{10... | collective-permute-start | bytes 296 | tf_op jit(solution)/shard_map/ppermute | solution.py:19
  1375.3 98.8 %collective-permute-start.19 = (bf16[48]{0:T(256)(128)(2,1)S(1)}, bf16[48]{0:T(256)(128)(2,1)S(1)}, u32[]{:S(2)}, u32[]{:S(2)}) collective-permute-start(bf16[48]{0:T(256)(128)(2,1)S(1)} %fusion.120), channel_id=1, source_target_pairs={{0,8},{8,0},{16,24},{24,16},{1,9},{9,1},{17,25},{25,17},{2,10},{10... | collective-permute-start | bytes 296 | tf_op jit(solution)/shard_map/ppermute | solution.py:19
  1501.2 38.1 %collective-permute-start.25 = (bf16[192]{0:T(256)(128)(2,1)S(1)}, bf16[192]{0:T(256)(128)(2,1)S(1)}, u32[]{:S(2)}, u32[]{:S(2)}) collective-permute-start(bf16[192]{0:T(256)(128)(2,1)S(1)} %fusion.100), channel_id=1, source_target_pairs={{0,8},{8,0},{16,24},{24,16},{1,9},{9,1},{17,25},{25,17},{2,10},{10... | collective-permute-start | bytes 1160 | tf_op jit(solution)/shard_map/ppermute | solution.py:19
  1537.7 123.0 %collective-permute-start.20 = (bf16[48,768]{1,0:T(8,128)(2,1)S(1)}, bf16[48,768]{1,0:T(8,128)(2,1)S(1)}, u32[]{:S(2)}, u32[]{:S(2)}) collective-permute-start(bf16[48,768]{1,0:T(8,128)(2,1)S(1)} %fusion.98), channel_id=1, source_target_pairs={{0,8},{8,0},{16,24},{24,16},{1,9},{9,1},{17,25},{25,17},{2,10},{10... | collective-permute-start | bytes 221192 | tf_op jit(solution)/shard_map/ppermute | solution.py:19
  1727.0 101.8 %collective-permute-start.17 = (bf16[48,2304]{1,0:T(8,128)(2,1)S(1)}, bf16[48,2304]{1,0:T(8,128)(2,1)S(1)}, u32[]{:S(2)}, u32[]{:S(2)}) collective-permute-start(bf16[48,2304]{1,0:T(8,128)(2,1)S(1)} %fusion.96), channel_id=1, source_target_pairs={{0,8},{8,0},{16,24},{24,16},{1,9},{9,1},{17,25},{25,17},{2,10},{10... | collective-permute-start | bytes 663560 | tf_op jit(solution)/shard_map/ppermute | solution.py:19
  1827.2 101.7 %collective-permute-start.24 = (bf16[48,3072]{1,0:T(8,128)(2,1)S(1)}, bf16[48,3072]{1,0:T(8,128)(2,1)S(1)}, u32[]{:S(2)}, u32[]{:S(2)}) collective-permute-start(bf16[48,3072]{1,0:T(8,128)(2,1)S(1)} %fusion.94), channel_id=1, source_target_pairs={{0,8},{8,0},{16,24},{24,16},{1,9},{9,1},{17,25},{25,17},{2,10},{10... | collective-permute-start | bytes 884744 | tf_op jit(solution)/shard_map/ppermute | solution.py:19
  1927.4 6.8 collective-permute-start.26
  (140 other events, 816.6 us)
Sparse Core Ops, SparseCore 0:
  1222.1 29.4 reduce-scatter.68
  1254.0 28.3 reduce-scatter.64
  1284.7 28.3 reduce-scatter.62
  1315.3 28.3 reduce-scatter.60
  1345.8 28.3 reduce-scatter.58
  1376.4 28.4 reduce-scatter.56
  1407.7 28.3 reduce-scatter.54
  1439.0 28.4 reduce-scatter.52
  1470.4 29.5 reduce-scatter.66
  1502.2 34.4 reduce-scatter.42
  1540.2 23.1 reduce-scatter.48
  1567.2 30.9 reduce-scatter.50
  1601.4 43.9 reduce-scatter.38
  1647.6 78.0 reduce-scatter.40
  1728.0 97.7 reduce-scatter.44
  1828.1 97.8 reduce-scatter.46
where the time goes:
time: 1950 us; the launch traced here: 1940 us
  waiting for transfers between devices  1000 us (51%)
  local copies, waits for them, and re-layouts  308 us (16%)
  matrix products  189 us (10%)
  other arithmetic  149 us (8%)
  loops' own time  110 us (6%)
  starting transfers between devices  107 us (5%)
  blocking collectives  60.2 us (3%)
    unnamed x27, waiting for transfers between devices  296 us
    ppermute x14, waiting for transfers between devices, passed_along(): return lax.ppermute(block, axis, route)  274 us
    ppermute x26, waiting for transfers between devices, swapped(): return lax.ppermute(value, axis, pairs)  146 us
    reduce_scatter x1, waiting for transfers between devices, per_device(): lax.psum_scatter(halves[9], 'dp', scatter_dimension=1, tiled=True)  97.3 us
    reduce_scatter x1, waiting for transfers between devices, per_device(): lax.psum_scatter(halves[11], 'dp', scatter_dimension=1, tiled=True)  95.2 us
    another operation x7, loops' own time, backward_step(): lax.switch(which, [attend_grad, feed_grad, spare_grad], inputs, grad, att...  89.1 us
    ppermute x14, starting transfers between devices, passed_along(): return lax.ppermute(block, axis, route)  71.8 us
    reduce_scatter x1, waiting for transfers between devices, per_device(): lax.psum_scatter(halves[2], 'dp', scatter_dimension=1, tiled=True)  61.9 us
  transfers between devices with their start and end apart: 56, of which 33 were waited for; matrix products, arithmetic and copies ran while one was open for 5% of the time, Pallas kernels for 0%

commit v1 on v0

v1 whole, which is shorter than its diff:
```python
import functools
import math

import jax
import jax.numpy as jnp
from jax import lax
from jax.experimental import pallas as pl
from jax.experimental.pallas import tpu as pltpu
from jax.sharding import PartitionSpec as P

HEADS = 12
EPS = 1e-05
HIGHEST = lax.Precision.HIGHEST
MESH = pl.DeviceIdType.MESH
BF = jnp.bfloat16
F32 = jnp.float32
TILES = 12
QKV, PROJ, UP, DOWN = 0, 3, 4, 8
GELU_A = math.sqrt(2.0 / math.pi)
GELU_B = 0.044715


def flipped(value, bit):
    mask = 2**bit
    return value + mask - 2 * mask * lax.rem(lax.div(value, mask), 2)


def mul(a, b):
    return lax.dot_general(a, b, (((1,), (0,)), ((), ())), preferred_element_type=F32)


def mul_nt(a, b):
    return lax.dot_general(a, b, (((1,), (1,)), ((), ())), preferred_element_type=F32)


def mul_tn(a, b):
    return lax.dot_general(a, b, (((0,), (0,)), ((), ())), preferred_element_type=F32)


def normalize(x):
    mean = jnp.mean(x, axis=-1, keepdims=True)
    centered = x - mean
    spread = jnp.mean(centered * centered, axis=-1, keepdims=True)
    rate = lax.rsqrt(spread + EPS)
    return centered * rate, rate


def scaled_back(gh, gain, n, rate):
    gn = gh * gain
    inner = jnp.mean(gn * n, axis=-1, keepdims=True)
    return (gn - jnp.mean(gn, axis=-1, keepdims=True) - n * inner) * rate


def column(values):
    return jnp.sum(values, axis=0, keepdims=True)


def pipeline_kernel(
    seqs,
    length,
    width,
    qkv_in,
    proj_in,
    up_in,
    down_in,
    vec_in,
    ids_in,
    table_in,
    time_in,
    cot_in,
    act_out,
    small_out,
    table_out,
    fixed_out,
    moving_out,
    w,
    vecs,
    par,
    xs,
    n_a,
    n_f,
    r_a,
    r_f,
    qkv,
    probs,
    y1,
    slope,
    gate,
    h_s,
    o_s,
    hf_s,
    gq_s,
    g1,
    go_s,
    acc,
    ybuf,
    ysend,
    gsum,
    tsum,
    own_sem,
    x_send,
    x_recv,
    z_send,
    z_recv,
    c1_send,
    c1_recv,
    c2_send,
    c2_recv,
    y_send,
    y_recv,
    v_sem,
    cot_sem,
    act_sem,
    keep_sem,
    last_sem,
):
    s = lax.axis_index("section")
    d = lax.axis_index("dp")
    stage = lax.div(s, 2)
    part = lax.rem(s, 2)
    other = 1 - part
    x_dev = (flipped(s, 0), d)
    y_dev = (flipped(s, 1), d)
    z_dev = (s, flipped(d, 1))
    c_dev = (s, flipped(d, 0))
    half = width // 2
    quarter = half // 4
    hidden_half = up_in.shape[2] // 2
    mine = lax.rem(d, 4)
    across = flipped(mine, 1)
    scale = 1.0 / math.sqrt(width // HEADS)
    letters_count = table_in.shape[0]

    barrier = pltpu.get_barrier_semaphore()
    for device in (x_dev, y_dev, z_dev, c_dev):
        pl.semaphore_signal(barrier, inc=1, device_id=device, device_id_type=MESH)

    own_rows = pl.ds(pl.multiple_of(part * half, 16), half)

    def own_copies(tile):
        if tile < PROJ:
            pairs = [(qkv_in.at[0, :, pl.ds(tile * width, width)], w.at[tile, own_rows])]
        elif tile < UP:
            pairs = [(proj_in.at[0], w.at[tile, own_rows])]
        elif tile < DOWN:
            pairs = [
                (
                    up_in.at[0, :, pl.ds(side * hidden_half + (tile - UP) * half, half)],
                    w.at[tile, own_rows, pl.ds(side * half, half)],
                )
                for side in range(2)
            ]
        else:
            pairs = [(down_in.at[0, pl.ds((tile - DOWN) * half, half)], w.at[tile, own_rows])]
        return [
            pltpu.make_async_copy(src, dst, own_sem.at[2 * tile + k]) for k, (src, dst) in enumerate(pairs)
        ]

    def x_copy(tile):
        rows = pl.ds(pl.multiple_of(part * half + mine * quarter, 16), quarter)
        return pltpu.make_async_remote_copy(
            src_ref=w.at[tile, rows],
            dst_ref=w.at[tile, rows],
            send_sem=x_send.at[tile],
            recv_sem=x_recv.at[tile],
            device_id=x_dev,
            device_id_type=MESH,
        )

    def relay(tile, which, send, recv, device):
        rows = pl.ds(pl.multiple_of(other * half + which * quarter, 16), quarter)
        return pltpu.make_async_remote_copy(
            src_ref=w.at[tile, rows],
            dst_ref=w.at[tile, rows],
            send_sem=send.at[tile],
            recv_sem=recv.at[tile],
            device_id=device,
            device_id_type=MESH,
        )

    def z_copy(tile):
        return relay(tile, mine, z_send, z_recv, z_dev)

    def c1_copy(tile):
        return relay(tile, mine, c1_send, c1_recv, c_dev)

    def c2_copy(tile):
        return relay(tile, across, c2_send, c2_recv, c_dev)

    def x_arrival(tile):
        return relay(tile, mine, x_send, x_recv, x_dev)

    def z_arrival(tile):
        return relay(tile, across, z_send, z_recv, z_dev)

    def c1_arrival(tile):
        return relay(tile, flipped(mine, 0), c1_send, c1_recv, c_dev)

    def c2_arrival(tile):
        return relay(tile, flipped(across, 0), c2_send, c2_recv, c_dev)

    def vec_copy(which):
        return pltpu.make_async_remote_copy(
            src_ref=vecs.at[which],
            dst_ref=vecs.at[which],
            send_sem=v_sem.at[1],
            recv_sem=v_sem.at[2],
            device_id=x_dev,
            device_id_type=MESH,
        )

    def pass_first(tile):
        x_arrival(tile).wait_recv()
        z_copy(tile).start()
        c1_copy(tile).start()

    def pass_second(tile):
        z_arrival(tile).wait_recv()
        c2_copy(tile).start()

    def ready(tile):
        c1_arrival(tile).wait_recv()
        c2_arrival(tile).wait_recv()

    vec_own = pltpu.make_async_copy(vec_in, vecs.at[part], v_sem.at[0])
    vec_own.start()
    for tile in range(TILES):
        for copy in own_copies(tile):
            copy.start()
    gsum[...] = jnp.zeros_like(gsum)
    tsum[...] = jnp.zeros_like(tsum)
    vec_own.wait()
    pl.semaphore_wait(barrier, 4)
    vec_copy(part).start()
    for tile in range(TILES):
        for copy in own_copies(tile):
            copy.wait()
        x_copy(tile).start()

    pass_first(0)
    pass_first(1)
    pass_second(0)
    pass_first(2)
    pass_second(1)
    pass_first(3)
    pass_second(2)
    pass_first(4)
    pass_second(3)
    pass_first(5)

    @pl.when(stage == 1)
    def _():
        def step(tile, _):
            pass_second(tile - 2)
            pass_first(tile)
            return 0

        lax.fori_loop(6, TILES, step, 0)
        pass_second(TILES - 2)
        pass_second(TILES - 1)

    vec_copy(other).wait_recv()
    par[:, :half] = vecs[0].astype(F32)
    par[:, half:] = vecs[1].astype(F32)
    for tile in range(UP):
        ready(tile)

    def rows_of(i):
        return pl.ds(pl.multiple_of(i * length, 16), length)

    def kept(slot, source, target, place, i):
        return pltpu.make_async_copy(source, target.at[place, rows_of(i)], keep_sem.at[slot])

    def keep_hf(i):
        return [kept(0, hf_s, fixed_out, 0, i)]

    def keep_h(i):
        return [kept(1, h_s, fixed_out, 1, i)]

    def keep_o(i):
        return [kept(2, o_s, fixed_out, 2, i)]

    def keep_g1(i):
        return [kept(3, g1, moving_out, PROJ + 4, i)]

    def keep_gq(i):
        return [kept(4 + j, gq_s.at[j], moving_out, 4 + j, i) for j in range(3)]

    def keep_a(i):
        return [kept(7 + j, gate.at[j], moving_out, 8 + j, i) for j in range(4)]

    def last_gu(i):
        return [
            pltpu.make_async_copy(slope.at[i, j], moving_out.at[j, rows_of(i)], last_sem.at[i, j])
            for j in range(4)
        ]

    def last_gz(i):
        return [pltpu.make_async_copy(ybuf.at[i], fixed_out.at[3, rows_of(i)], last_sem.at[i, 4])]

    def start(copies):
        for copy in copies:
            copy.start()

    def wait(copies):
        for copy in copies:
            copy.wait()

    def act_copy(i):
        return pltpu.make_async_copy(y1.at[i], act_out.at[i], act_sem.at[i])

    def cot_copy(i):
        return pltpu.make_async_copy(cot_in.at[part * seqs + i], ybuf.at[i], cot_sem.at[i])

    def y_copy(i):
        return pltpu.make_async_remote_copy(
            src_ref=ysend.at[i],
            dst_ref=ybuf.at[i],
            send_sem=y_send.at[i],
            recv_sem=y_recv.at[i],
            device_id=y_dev,
            device_id_type=MESH,
        )

    def row(index):
        return par[index : index + 1, :]

    lane = lax.broadcasted_iota(jnp.int32, (length, 128), 1)
    low = lane < 64
    side_ones = [(lane < 64).astype(F32).astype(BF), (lane >= 64).astype(F32).astype(BF)]

    def letters(i):
        ids = ids_in[pl.ds(part * seqs + i, 1), :]
        place = lax.broadcasted_iota(jnp.int32, (letters_count, length), 0)
        return (place == ids).astype(F32).astype(BF)

    def attn_fwd(i):
        @pl.when(stage == 0)
        def _():
            xs[...] = mul_tn(letters(i), table_in[...]) + time_in[pl.ds(part * seqs + i, 1), :]

        @pl.when(stage == 1)
        def _():
            y_copy(i).wait_recv()
            xs[...] = ybuf[i].astype(F32)
            cot_copy(i).start()

        n, rate = normalize(xs[...])
        n_a[i] = n.astype(BF)
        r_a[i] = jnp.broadcast_to(rate, (length, 128))

        @pl.when(i > 0)
        def _():
            wait(keep_h(i))
            wait(keep_o(i))

        h_s[...] = (n * row(0) + row(1)).astype(BF)
        start(keep_h(i))
        for j in range(3):
            joint = mul(h_s[...], w[QKV + j])
            if j == 0:
                joint = joint + row(2)
            if j == 2:
                joint = joint + row(3)
            qkv[i, :, j * width : (j + 1) * width] = joint.astype(BF)

        def pair(hp, _):
            at = pl.multiple_of(hp * 128, 128)
            q2 = qkv[i, :, pl.ds(at, 128)]
            k2 = qkv[i, :, pl.ds(width + at, 128)]
            v2 = qkv[i, :, pl.ds(2 * width + at, 128)]
            outs = []
            for side in range(2):
                scores = mul_nt(q2 * side_ones[side], k2) * scale
                expo = jnp.exp(scores - jnp.max(scores, axis=-1, keepdims=True))
                total = jnp.sum(expo, axis=-1, keepdims=True)
                pb = (expo * (1.0 / total)).astype(BF)
                probs[i, 2 * hp + side] = pb
                outs.append(mul(pb, v2))
            o_s[:, pl.ds(at, 128)] = jnp.where(low, outs[0], outs[1]).astype(BF)
            return 0

        lax.fori_loop(0, HEADS // 2, pair, 0)
        start(keep_o(i))
        y1[i] = (xs[...] + (mul(o_s[...], w[PROJ]) + row(4))).astype(BF)

    def feed_fwd(i):
        @pl.when(i == 0)
        def _():
            def one(tile, _):
                ready(tile)
                return 0

            lax.fori_loop(UP, TILES, one, 0)

        x = y1[i].astype(F32)
        n, rate = normalize(x)
        n_f[i] = n.astype(BF)
        r_f[i] = jnp.broadcast_to(rate, (length, 128))

        @pl.when(i > 0)
        def _():
            wait(keep_hf(i))
            wait(keep_a(i))

        hf_s[...] = (n * row(5) + row(6)).astype(BF)
        start(keep_hf(i))
        acc[...] = x + row(7)

        def one(j, _):
            u = mul(hf_s[...], w[UP + j]) + par[pl.ds(8 + j, 1), :]
            square = u * u
            t = jnp.tanh(u * (GELU_A + GELU_A * GELU_B * square))
            both = 0.5 + 0.5 * t
            a = (u * both).astype(BF)
            gate[j] = a
            bend = (0.5 * GELU_A + 1.5 * GELU_A * GELU_B * square) * u
            slope[i, j] = (both + bend * (1.0 - t * t)).astype(BF)
            acc[...] += mul(a, w[DOWN + j])
            return 0

        lax.fori_loop(0, 4, one, 0)
        start(keep_a(i))

        @pl.when(stage == 0)
        def _():
            ysend[i] = acc[...].astype(BF)
            y_copy(i).start()

        @pl.when(stage == 1)
        def _():
            y1[i] = acc[...].astype(BF)
            act_copy(i).start()

    def feed_bwd(i):
        @pl.when(stage == 0)
        def _():
            y_copy(i).wait_recv()

        @pl.when(stage == 1)
        def _():
            cot_copy(i).wait()

        start(last_gz(i))
        gsum[7:8, :] += column(ybuf[i].astype(F32))
        acc[...] = jnp.zeros_like(acc)

        def one(j, _):
            ga = mul_nt(ybuf[i], w[DOWN + j])
            gu = (ga * slope[i, j].astype(F32)).astype(BF)
            slope[i, j] = gu
            gsum[pl.ds(8 + j, 1), :] += column(gu.astype(F32))
            acc[...] += mul_nt(gu, w[UP + j])
            return 0

        lax.fori_loop(0, 4, one, 0)
        start(last_gu(i))
        gh = acc[...]
        n = n_f[i].astype(F32)
        gsum[5:6, :] += column(gh * n)
        gsum[6:7, :] += column(gh)
        gx = ybuf[i].astype(F32) + scaled_back(gh, row(5), n, r_f[i][:, 0:1])

        @pl.when(i > 0)
        def _():
            wait(keep_g1(i))
            wait(keep_gq(i))

        g1[...] = gx.astype(BF)
        start(keep_g1(i))

    def attn_bwd(i):
        gsum[4:5, :] += column(g1[...].astype(F32))
        go_s[...] = mul_nt(g1[...], w[PROJ]).astype(BF)

        def pair(hp, _):
            at = pl.multiple_of(hp * 128, 128)
            q2 = qkv[i, :, pl.ds(at, 128)]
            k2 = qkv[i, :, pl.ds(width + at, 128)]
            v2 = qkv[i, :, pl.ds(2 * width + at, 128)]
            go2 = go_s[:, pl.ds(at, 128)]
            gq, gk, gv = [], [], []
            for side in range(2):
                pb = probs[i, 2 * hp + side]
                gp = mul_nt(go2 * side_ones[side], v2)
                p = pb.astype(F32)
                pg = p * gp
                gs = (pg - p * jnp.sum(pg, axis=-1, keepdims=True)).astype(BF)
                gv.append(mul_tn(pb, go2))
                gq.append(mul(gs, k2))
                gk.append(mul_tn(gs, q2))
            gq_s[0, :, pl.ds(at, 128)] = (jnp.where(low, gq[0], gq[1]) * scale).astype(BF)
            gq_s[1, :, pl.ds(at, 128)] = (jnp.where(low, gk[0], gk[1]) * scale).astype(BF)
            gq_s[2, :, pl.ds(at, 128)] = jnp.where(low, gv[0], gv[1]).astype(BF)
            return 0

        lax.fori_loop(0, HEADS // 2, pair, 0)
        start(keep_gq(i))
        gsum[2:3, :] += column(gq_s[0].astype(F32))
        gsum[3:4, :] += column(gq_s[2].astype(F32))
        gh = mul_nt(gq_s[0], w[QKV]) + mul_nt(gq_s[1], w[QKV + 1]) + mul_nt(gq_s[2], w[QKV + 2])
        n = n_a[i].astype(F32)
        gsum[0:1, :] += column(gh * n)
        gsum[1:2, :] += column(gh)
        gx = g1[...].astype(F32) + scaled_back(gh, row(0), n, r_a[i][:, 0:1])
        acc[...] = gx

        @pl.when(stage == 1)
        def _():
            ysend[i] = acc[...].astype(BF)
            y_copy(i).start()

        @pl.when(stage == 0)
        def _():
            high = acc[...].astype(BF)
            rest = (acc[...] - high.astype(F32)).astype(BF)
            hot = letters(i)
            tsum[:letters_count, :] += mul(hot, high) + mul(hot, rest)
            tsum[pl.ds(letters_count + part * seqs + i, 1), :] = column(acc[...])

    def unit(u, _):
        early = u < 2 * seqs
        kind0 = jnp.where(early, lax.div(u, seqs), 2 + lax.rem(u, 2))
        index0 = jnp.where(early, lax.rem(u, seqs), lax.div(u, 2) - seqs)
        kind = jnp.where(stage == 0, kind0, lax.rem(u, 4))
        i = jnp.where(stage == 0, index0, lax.div(u, 4))

        @pl.when(jnp.logical_and(stage == 0, jnp.logical_and(u >= 1, u <= 4)))
        def _():
            pass_second(2 + 2 * u)
            pass_second(3 + 2 * u)

        @pl.when(jnp.logical_and(stage == 0, jnp.logical_and(u >= 1, u <= 3)))
        def _():
            pass_first(4 + 2 * u)
            pass_first(5 + 2 * u)

        for index, run in enumerate((attn_fwd, feed_fwd, feed_bwd, attn_bwd)):

            @pl.when(kind == index)
            def _():
                run(i)

        return 0

    lax.fori_loop(0, 4 * seqs, unit, 0)

    small_out[...] = gsum[...]
    table_out[...] = tsum[...]

    vec_copy(part).wait_send()

    def settle(tile, _):
        x_copy(tile).wait_send()
        z_copy(tile).wait_send()
        c1_copy(tile).wait_send()
        c2_copy(tile).wait_send()
        return 0

    lax.fori_loop(0, TILES, settle, 0)
    for done in (keep_h, keep_o, keep_hf, keep_a, keep_gq, keep_g1):
        wait(done(seqs - 1))

    def finish(i, _):
        y_copy(i).wait_send()
        wait(last_gu(i))
        wait(last_gz(i))

        @pl.when(stage == 1)
        def _():
            act_copy(i).wait()

        return 0

    lax.fori_loop(0, seqs, finish, 0)


def run_pipeline(weights, vec, ids, table, times, cot):
    rows, length = ids.shape
    width = cot.shape[2]
    seqs = rows // 2
    tokens = seqs * length
    dma = pltpu.SemaphoreType.DMA
    anywhere = pl.BlockSpec(memory_space=pl.ANY)
    local = pl.BlockSpec(memory_space=pltpu.VMEM)
    vm = pltpu.VMEM
    return pl.pallas_call(
        functools.partial(pipeline_kernel, seqs, length, width),
        out_shape=(
            jax.ShapeDtypeStruct((seqs, length, width), BF),
            jax.ShapeDtypeStruct((16, width), F32),
            jax.ShapeDtypeStruct((table.shape[0] + rows, width), F32),
            jax.ShapeDtypeStruct((4, tokens, width), BF),
            jax.ShapeDtypeStruct((12, tokens, width), BF),
        ),
        in_specs=[anywhere] * 5 + [local] * 3 + [anywhere],
        out_specs=(anywhere, local, local, anywhere, anywhere),
        scratch_shapes=[
            vm((TILES, width, width), BF),
            vm((2, 16, width // 2), BF),
            vm((16, width), F32),
            vm((length, width), F32),
            vm((seqs, length, width), BF),
            vm((seqs, length, width), BF),
            vm((seqs, length, 128), F32),
            vm((seqs, length, 128), F32),
            vm((seqs, length, 3 * width), BF),
            vm((seqs, HEADS, length, length), BF),
            vm((seqs, length, width), BF),
            vm((seqs, 4, length, width), BF),
            vm((4, length, width), BF),
            vm((length, width), BF),
            vm((length, width), BF),
            vm((length, width), BF),
            vm((3, length, width), BF),
            vm((length, width), BF),
            vm((length, width), BF),
            vm((length, width), F32),
            vm((seqs, length, width), BF),
            vm((seqs, length, width), BF),
            vm((16, width), F32),
            vm((table.shape[0] + rows, width), F32),
            dma((2 * TILES,)),
        ]
        + [dma((TILES,))] * 8
        + [
            dma((seqs,)),
            dma((seqs,)),
            dma((3,)),
            dma((seqs,)),
            dma((seqs,)),
            dma((11,)),
            dma((seqs, 5)),
        ],
        compiler_params=pltpu.CompilerParams(
            collective_id=0, has_side_effects=True, vmem_limit_bytes=62 * 2**20
        ),
    )(*weights, vec, ids, table, times, cot)


def reduce_kernel(
    nz,
    half,
    rows,
    fixed_in,
    moving_in,
    qkv_out,
    proj_out,
    up_out,
    down_out,
    fixed,
    moving,
    parts,
    core_buf,
    x_buf,
    right_buf,
    left_buf,
    total,
    fixed_sem,
    moving_sem,
    core_send,
    core_recv,
    x_send,
    x_recv,
    right_send,
    right_recv,
    left_send,
    left_recv,
):
    s = lax.axis_index("section")
    d = lax.axis_index("dp")
    part = lax.rem(s, 2)
    other = 1 - part
    core = lax.rem(d, 2)
    z = lax.div(d, 2)
    x_dev = (flipped(s, 0), d)
    c_dev = (s, flipped(d, 0))
    ends = nz - 1
    slots = moving.shape[0]
    width = 2 * half

    barrier = pltpu.get_barrier_semaphore()
    for device in (x_dev, c_dev):
        pl.semaphore_signal(barrier, inc=1, device_id=device, device_id_type=MESH)

    @pl.when(z > 0)
    def _():
        pl.semaphore_signal(barrier, inc=1, device_id=(s, d - 2), device_id_type=MESH)

    @pl.when(z < ends)
    def _():
        pl.semaphore_signal(barrier, inc=1, device_id=(s, d + 2), device_id_type=MESH)

    def load_fixed(index):
        return pltpu.make_async_copy(fixed_in.at[index], fixed.at[index], fixed_sem.at[index])

    def tile_at(turn):
        pair = turn - 4
        return jnp.where(turn < 4, turn, 4 + lax.div(pair, 2) + 4 * lax.rem(pair, 2))

    def load_moving(turn):
        slot = lax.rem(turn, slots)
        return pltpu.make_async_copy(moving_in.at[tile_at(turn)], moving.at[slot], moving_sem.at[slot])

    for turn in range(slots):
        load_moving(jnp.int32(turn)).start()
        if turn == 0:
            load_fixed(0).start()
    for index in (1, 3, 2):
        load_fixed(index).start()

    neighbours = 2 + (z > 0).astype(jnp.int32) + (z < ends).astype(jnp.int32)
    pl.semaphore_wait(barrier, neighbours)

    def core_copy(k):
        return pltpu.make_async_remote_copy(
            src_ref=parts.at[k, :, :, 1 - core],
            dst_ref=core_buf.at[k],
            send_sem=core_send.at[k],
            recv_sem=core_recv.at[k],
            device_id=c_dev,
            device_id_type=MESH,
        )

    def x_copy(k):
        return pltpu.make_async_remote_copy(
            src_ref=parts.at[k, other, :, core],
            dst_ref=x_buf.at[k],
            send_sem=x_send.at[k],
            recv_sem=x_recv.at[k],
            device_id=x_dev,
            device_id_type=MESH,
        )

    def right_copy(k, j):
        return pltpu.make_async_remote_copy(
            src_ref=parts.at[k, part, j, core],
            dst_ref=right_buf.at[k, j],
            send_sem=right_send.at[k, j],
            recv_sem=right_recv.at[k, j],
            device_id=(s, d + 2),
            device_id_type=MESH,
        )

    def left_copy(k, j):
        return pltpu.make_async_remote_copy(
            src_ref=parts.at[k, part, j, core],
            dst_ref=left_buf.at[k, j],
            send_sem=left_send.at[k, j],
            recv_sem=left_recv.at[k, j],
            device_id=(s, d - 2),
            device_id_type=MESH,
        )

    def right_step(k):
        for j in range(ends, -1, -1):

            @pl.when(jnp.logical_and(z > 0, j >= z))
            def _():
                right_copy(k, j).wait_recv()

            @pl.when(jnp.logical_and(z > 0, j > z))
            def _():
                both = parts[k, part, j, core].astype(F32) + right_buf[k, j].astype(F32)
                parts[k, part, j, core] = both.astype(BF)

            @pl.when(j > z)
            def _():
                right_copy(k, j).start()

    def left_step(k):
        for j in range(nz):

            @pl.when(jnp.logical_and(z < ends, j <= z))
            def _():
                left_copy(k, j).wait_recv()

            @pl.when(jnp.logical_and(z < ends, j < z))
            def _():
                both = parts[k, part, j, core].astype(F32) + left_buf[k, j].astype(F32)
                parts[k, part, j, core] = both.astype(BF)

            @pl.when(j < z)
            def _():
                left_copy(k, j).start()

    def close_step(k):
        @pl.when(z == 0)
        def _():
            total[...] = parts[k, part, z, core].astype(F32) + left_buf[k, z].astype(F32)

        @pl.when(z == ends)
        def _():
            total[...] = parts[k, part, z, core].astype(F32) + right_buf[k, z].astype(F32)

        @pl.when(jnp.logical_and(z > 0, z < ends))
        def _():
            sides = left_buf[k, z].astype(F32) + right_buf[k, z].astype(F32)
            total[...] = parts[k, part, z, core].astype(F32) + sides

        @pl.when(k < 4)
        def _():
            for side in range(2):
                at = pl.multiple_of(side * 4 * half + k * half, 128)
                up_out[0, :, pl.ds(at, half)] = total[:, side * half : (side + 1) * half]

        @pl.when(jnp.logical_and(k >= 4, k < 7))
        def _():
            qkv_out[0, :, pl.ds(pl.multiple_of((k - 4) * width, 128), width)] = total[...]

        @pl.when(k == 7)
        def _():
            proj_out[0] = total[...]

        @pl.when(k >= 8)
        def _():
            down_out[0, pl.ds(pl.multiple_of((k - 8) * rows, 8), rows), :] = total[...]

    def product(turn):
        load_moving(turn).wait()
        m = tile_at(turn)
        slot = lax.rem(turn, slots)

        @pl.when(m == 0)
        def _():
            load_fixed(0).wait()

        @pl.when(m == 4)
        def _():
            load_fixed(1).wait()

        @pl.when(m == 7)
        def _():
            load_fixed(2).wait()

        @pl.when(m == 8)
        def _():
            load_fixed(3).wait()

        @pl.when(m < 8)
        def _():
            upper = (m >= 4).astype(jnp.int32) + (m >= 7).astype(jnp.int32)
            value = mul_tn(fixed[upper], moving[slot]).astype(BF)
            parts[m] = value.reshape(2, nz, 2, rows, width)

        @pl.when(m >= 8)
        def _():
            value = mul_tn(moving[slot], fixed[3]).astype(BF).reshape(2, 2, 4, rows, width)
            for block in range(4):
                parts[8 + block, :, m - 8] = value[:, :, block]

        @pl.when(turn + slots < TILES)
        def _():
            load_moving(turn + slots).start()

    def inside(k):
        return jnp.logical_and(k >= 0, k < TILES)

    def step(t, _):
        @pl.when(t < 4)
        def _():
            product(t)

        @pl.when(jnp.logical_and(t >= 4, t < 8))
        def _():
            product(4 + 2 * (t - 4))
            product(5 + 2 * (t - 4))

        @pl.when(t < TILES)
        def _():
            core_copy(t).start()

        k1 = t - 1

        @pl.when(inside(k1))
        def _():
            core_copy(k1).wait_recv()
            for side in range(2):
                both = parts[k1, side, :, core].astype(F32) + core_buf[k1, side].astype(F32)
                parts[k1, side, :, core] = both.astype(BF)
            x_copy(k1).start()

        k2 = t - 2

        @pl.when(inside(k2))
        def _():
            x_copy(k2).wait_recv()
            both = parts[k2, part, :, core].astype(F32) + x_buf[k2].astype(F32)
            parts[k2, part, :, core] = both.astype(BF)

        k3 = t - 2 - z

        @pl.when(inside(k3))
        def _():
            right_step(k3)

        k4 = t - 2 - (ends - z)

        @pl.when(inside(k4))
        def _():
            left_step(k4)

        k5 = jnp.minimum(k3, k4)

        @pl.when(inside(k5))
        def _():
            close_step(k5)

        return 0

    lax.fori_loop(0, TILES + 2 + ends, step, 0)

    def settle(k, _):
        core_copy(k).wait_send()
        x_copy(k).wait_send()
        for j in range(nz):

            @pl.when(j > z)
            def _():
                right_copy(k, j).wait_send()

            @pl.when(j < z)
            def _():
                left_copy(k, j).wait_send()

        return 0

    lax.fori_loop(0, TILES, settle, 0)


def run_reduce(fixed, moving, replicas):
    tokens, width = fixed.shape[1:]
    nz = replicas // 2
    half = width // 2
    rows = half // replicas
    dma = pltpu.SemaphoreType.DMA
    vm = pltpu.VMEM
    slots = 3
    return pl.pallas_call(
        functools.partial(reduce_kernel, nz, half, rows),
        out_shape=(
            jax.ShapeDtypeStruct((1, rows, 3 * width), F32),
            jax.ShapeDtypeStruct((1, rows, width), F32),
            jax.ShapeDtypeStruct((1, rows, 4 * width), F32),
            jax.ShapeDtypeStruct((1, 4 * rows, width), F32),
        ),
        in_specs=[pl.BlockSpec(memory_space=pl.ANY)] * 2,
        out_specs=(pl.BlockSpec(memory_space=pltpu.VMEM),) * 4,
        scratch_shapes=[
            vm((4, tokens, width), BF),
            vm((slots, tokens, width), BF),
            vm((TILES, 2, nz, 2, rows, width), BF),
            vm((TILES, 2, nz, rows, width), BF),
            vm((TILES, nz, rows, width), BF),
            vm((TILES, nz, rows, width), BF),
            vm((TILES, nz, rows, width), BF),
            vm((rows, width), F32),
            dma((4,)),
            dma((slots,)),
            dma((TILES,)),
            dma((TILES,)),
            dma((TILES,)),
            dma((TILES,)),
            dma((TILES, nz)),
            dma((TILES, nz)),
            dma((TILES, nz)),
            dma((TILES, nz)),
        ],
        compiler_params=pltpu.CompilerParams(
            collective_id=1, has_side_effects=True, vmem_limit_bytes=62 * 2**20
        ),
    )(fixed, moving)


def plain_reduce(fixed, moving, lower):
    def grad(left, right):
        return jnp.einsum("tk,tn->kn", left, right, preferred_element_type=F32)

    width = fixed.shape[2]
    half = width // 2
    hf, h, o, gz = (fixed[index] for index in range(4))
    ups = jnp.stack([grad(hf, moving[j]) for j in range(4)])
    up = ups.reshape(4, width, 2, half).transpose(1, 2, 0, 3).reshape(width, 4 * width)
    joint = jnp.concatenate([grad(h, moving[4 + j]) for j in range(3)], axis=1)
    proj = grad(o, moving[7])
    downs = jnp.stack([grad(moving[8 + j], gz) for j in range(4)])
    down = downs.reshape(4, 2, half, width).transpose(1, 0, 2, 3).reshape(4 * width, width)
    results = []
    for total in (joint, proj, up, down):
        halves = total.reshape((2, total.shape[0] // 2) + total.shape[1:])
        summed = lax.psum_scatter(halves, "dp", scatter_dimension=1, tiled=True)
        ours = jnp.where(lower, summed[0], summed[1])
        theirs = jnp.where(lower, summed[1], summed[0]).astype(BF)
        pairs = [(i, i ^ 1) for i in range(lax.axis_size("section"))]
        results.append((ours + lax.ppermute(theirs, "section", pairs).astype(F32))[None])
    return results


def spread_activations(act, section, width):
    quarter = width // 4
    part = lax.rem(section, 2)

    def piece(index):
        return lax.dynamic_slice_in_dim(act, index * quarter, quarter, axis=2)

    straight = lax.ppermute(piece(part), "section", [(2, 0), (3, 1)])
    crossed = lax.ppermute(piece(1 - part), "section", [(2, 1), (3, 0)])
    beside = lax.ppermute(piece(3 - part), "section", [(2, 3), (3, 2)])
    upper = section >= 2
    same = jnp.where(upper, piece(2 + part), straight)
    far = jnp.where(upper, beside, crossed)
    lower = part == 0
    first = jnp.where(lower, same, far)
    second = jnp.where(lower, far, same)
    return jnp.concatenate([first, second], axis=0).astype(F32)


def per_device(
    token_ids,
    timesteps,
    token_table,
    time_table,
    attn_gain,
    attn_shift,
    qkv_weight,
    query_bias,
    value_bias,
    proj_weight,
    proj_bias,
    mlp_gain,
    mlp_shift,
    up_weight,
    up_bias,
    down_weight,
    down_bias,
    cotangent,
):
    section = lax.axis_index("section")
    replica = lax.axis_index("dp")
    replicas = lax.axis_size("dp")
    rows, length = token_ids.shape
    width = cotangent.shape[2]
    half = width // 2
    layer = section // 2
    part = section % 2
    letters_count = token_table.shape[0]
    times_count = time_table.shape[0]
    padded = -(-letters_count // 16) * 16
    vec = jnp.concatenate(
        [
            attn_gain,
            attn_shift,
            query_bias,
            value_bias,
            proj_bias,
            mlp_gain,
            mlp_shift,
            down_bias,
            up_bias.reshape(4, half),
            jnp.zeros((4, half), BF),
        ],
        axis=0,
    )
    table = jnp.pad(token_table, ((0, padded - letters_count), (0, 0)))
    times = jnp.take(time_table, timesteps, axis=0).astype(F32)
    moments = lax.all_gather(timesteps, "dp", tiled=True)
    weights = (qkv_weight, proj_weight, up_weight, down_weight)
    act, small, tables, fixed, moving = run_pipeline(weights, vec, token_ids, table, times, cotangent)
    activations = spread_activations(act, section, width)
    total_rows = rows * replicas
    mine = jnp.zeros((2, 16, width), F32)
    mine = lax.dynamic_update_slice_in_dim(mine, small[None], layer, 0)
    placed = jnp.zeros((total_rows, width), F32)
    placed = lax.dynamic_update_slice_in_dim(placed, tables[padded:], replica * rows, 0)
    joined = jnp.concatenate([tables[:padded], mine.reshape(32, width), placed], axis=0)
    joined = lax.psum(joined, ("section", "dp"))
    if half % (16 * replicas) == 0:
        qkv_grad, proj_grad, up_grad, down_grad = run_reduce(fixed, moving, replicas)
    else:
        qkv_grad, proj_grad, up_grad, down_grad = plain_reduce(fixed, moving, part == 0)
    quarter = width // 4
    columns = lax.dynamic_slice_in_dim(joined, section * quarter, quarter, axis=1)
    token_grad = columns[:letters_count]
    steps = jnp.arange(times_count, dtype=jnp.int32)
    hot = (steps[:, None] == moments[None, :]).astype(F32)
    time_grad = jnp.einsum("tb,bd->td", hot, columns[padded + 32 :], precision=HIGHEST)
    ours = lax.dynamic_slice(joined, (padded + 16 * layer, part * half), (16, half))
    each = half // replicas
    vectors = lax.dynamic_slice_in_dim(ours[:8], replica * each, each, axis=1)
    ups = lax.dynamic_slice_in_dim(ours[8:12].reshape(1, 4 * half), replica * 4 * each, 4 * each, axis=1)
    return (
        activations,
        token_grad,
        time_grad,
        vectors[0:1],
        vectors[1:2],
        qkv_grad,
        vectors[2:3],
        vectors[3:4],
        proj_grad,
        vectors[4:5],
        vectors[5:6],
        vectors[6:7],
        up_grad,
        ups,
        down_grad,
        vectors[7:8],
    )


def solution(mesh):
    return jax.shard_map(
        per_device,
        mesh=mesh,
        in_specs=(
            P("dp", None),
            P("dp"),
            P(),
            P(),
            P("section", None),
            P("section", None),
            P("section", None, None),
            P("section", None),
            P("section", None),
            P("section", None, None),
            P("section", None),
            P("section", None),
            P("section", None),
            P("section", None, None),
            P("section", None),
            P("section", None, None),
            P("section", None),
            P("dp", None, None),
        ),
        out_specs=(
            P("dp", None, "section"),
            P(None, "section"),
            P(None, "section"),
            P("section", "dp"),
            P("section", "dp"),
            P("section", "dp", None),
            P("section", "dp"),
            P("section", "dp"),
            P("section", "dp", None),
            P("section", "dp"),
            P("section", "dp"),
            P("section", "dp"),
            P("section", "dp", None),
            P("section", "dp"),
            P("section", "dp", None),
            P("section", "dp"),
        ),
        check_vma=False,
    )
```

time: 1950 us -> 369 us (0.19)
  waiting for transfers between devices: 1000 us -> 17 us
  Pallas kernels: 0 us -> 297 us
  local copies, waits for them, and re-layouts: 308 us -> 19.6 us
  matrix products: 189 us -> 2.38 us
  other arithmetic: 149 us -> 7.11 us
  loops' own time: 110 us -> 0 us
  starting transfers between devices: 107 us -> 4.06 us
  blocking collectives: 60.2 us -> 6.47 us
    ppermute x40 -> x3, waiting for transfers between devices: 419 us -> 0.01 us  [the longest x1 0.01 us: spread_activations(): beside = lax.ppermute(piece(3 - part), 'section', [(2, 3), (3, 2)])]
    pallas_call x0 -> x2, Pallas kernels: none -> 297 us  [the longest x1 196 us: run_pipeline(): pl.pallas_call(functools.partial(pipeline_kernel, seqs, length, width), o...]
    unnamed x27 -> x1, waiting for transfers between devices: 296 us -> 0.02 us
    reduce_scatter x5 -> x0, waiting for transfers between devices: 288 us -> none  [the longest x1 97.3 us: per_device(): lax.psum_scatter(halves[9], 'dp', scatter_dimension=1, tiled=True)]
    dot_general x75 -> x1, matrix products: 189 us -> 2.38 us  [per_device(): jnp.einsum('tb,bd->td', hot, columns[padded + 32:], precision=HIGHEST)]
    another operation x23 -> x0, loops' own time: 110 us -> none  [the longest x7 89.1 us: backward_step(): lax.switch(which, [attend_grad, feed_grad, spare_grad], inputs, grad, att...]
    ppermute x40 -> x3, starting transfers between devices: 106 us -> 4.03 us  [the longest x1 1.45 us: spread_activations(): beside = lax.ppermute(piece(3 - part), 'section', [(2, 3), (3, 2)])]
    reshape x37 -> x1, local copies, waits for them, and re-layouts: 63.2 us -> 0.02 us  [per_device(): up_bias.reshape(4, half)]
  transfers between devices with their start and end apart: 56 -> 4, of which waited for: 33 -> 1; matrix products, arithmetic and copies ran while one was open for 5% -> 3% of each run, Pallas kernels for 0% -> 27%
where the time goes in v1:
time: 369 us; the launch traced here: 368 us
  Pallas kernels  297 us (80%)
  local copies, waits for them, and re-layouts  19.6 us (5%)
  waiting for transfers between devices  17 us (5%)
  between operations  14.9 us (4%)
  other arithmetic  7.11 us (2%)
  blocking collectives  6.47 us (2%)
  starting transfers between devices  4.06 us (1%)
    pallas_call x1, Pallas kernels, run_pipeline(): pl.pallas_call(functools.partial(pipeline_kernel, seqs, length, width), o...  196 us
    pallas_call x1, Pallas kernels, run_reduce(): pl.pallas_call(functools.partial(reduce_kernel, nz, half, rows), out_shap...  101 us
    psum x1, waiting for transfers between devices, per_device(): joined = lax.psum(joined, ('section', 'dp'))  16.9 us
    unnamed x26, local copies, waits for them, and re-layouts  7.56 us
  transfers between devices with their start and end apart: 4, of which 1 were waited for; matrix products, arithmetic and copies ran while one was open for 3% of the time, Pallas kernels for 27%

profile of v1, /device:TPU:0, one launch (start us, length us, event | category | flops | bytes accessed | tf_op | source)
XLA Modules:
  0.0 368.2 jit_solution(3530751719671172811)
XLA Ops:
  7.2 0.0 copy-start
  7.2 0.0 all-reduce.4.cloned.1.call-start
  7.2 0.8 compare_select_fusion
  8.0 0.7 compare_and_fusion
  8.7 0.7 reduce
  9.4 1.4 pad.4.table_in
  10.9 0.0 copy-done
  10.9 0.6 gather_fusion
  11.4 0.7 select_convert_fusion.time_in
  12.1 2.0 concatenate.9.vec_in
  14.2 196.2 %shard_map.297 = (bf16[4,256,768]{2,1,0:T(8,128)(2,1)}, f32[16,768]{1,0:T(8,128)}, f32[40,768]{1,0:T(8,128)}, bf16[4,1024,768]{2,1,0:T(8,128)(2,1)}, bf16[12,1024,768]{2,1,0:T(8,128)(2,1)}) custom-call(bf16[1,384,2304]{2,1,0:T(8,128)(2,1)} %qkv_in.1, bf16[1,384,768]{2,1,0:T(8,128)(2,1)} %proj_in.1, bf16[1,384,3072]{2,1,0:T(8,128)(2,1)} %up_in.1, ...), custom_call_target="tpu_custom_call" | custom-call | tf_op jit(solution)/shard_map/pallas_call | solution.py:587
  210.3 0.0 copy-start.1
  210.3 1.0 slice.42
  211.4 0.7 slice_dynamic-update-slice_fusion
  212.1 0.8 bitcast_dynamic-update-slice_fusion
  212.9 0.8 pad_maximum_fusion
  213.7 0.0 all-reduce.4.cloned.1.call-update
  213.7 0.0 copy-done.1
  213.7 1.9 constant_dynamic-slice_fusion.4
  215.7 1.5 collective-permute-start.1
  217.1 1.3 collective-permute-start.2
  218.4 1.3 collective-permute-start
  219.7 0.0 copy-start.7
  219.7 0.0 copy-start.6
  219.8 100.6 %shard_map.298 = (f32[1,48,2304]{2,1,0:T(8,128)}, f32[1,48,768]{2,1,0:T(8,128)}, f32[1,48,3072]{2,1,0:T(8,128)}, f32[1,192,768]{2,1,0:T(8,128)}) custom-call(bf16[4,1024,768]{2,1,0:T(8,128)(2,1)} %get-tuple-element.28.fixed_in, bf16[12,1024,768]{2,1,0:T(8,128)(2,1)} %get-tuple-element.29.moving_in), custom_call_target="tpu_custom_call" | custom-call | tf_op jit(solution)/shard_map/pallas_call | solution.py:939
  320.4 0.6 dynamic-slice
  321.7 0.0 copy-done.6
  321.7 0.2 dynamic-update-slice
  321.9 6.5 %all-reduce.1 = s32[64]{0:T(128)S(1)} all-reduce(s32[64]{0:T(128)S(1)} %dynamic-update-slice), channel_id=1, replica_groups=mesh['section'=4,'dp'=8] {'dp'}, use_global_device_ids=true, to_apply=%add.1 | all-reduce | flops 64 | bytes 512
  328.4 16.9 %all-reduce.4.cloned.1.call-done = f32[128,768]{1,0:T(8,128)} async-done(((f32[128,768]{1,0:T(8,128)}), f32[128,768]{1,0:T(8,128)}) %all-reduce.4.cloned.1.call-update) | async-done | bytes 393232 | tf_op jit(solution)/shard_map/psum | solution.py:1076
  345.3 0.8 dynamic-slice.4
  346.1 0.5 fusion.3
  346.6 0.8 dynamic-slice_bitcast_fusion
  347.4 0.6 constant_dynamic-slice_fusion
  348.1 1.5 constant_dynamic-slice_fusion.1
  349.6 2.4 fusion
  351.9 0.0 collective-permute-done.1
  352.0 0.0 collective-permute-done.2
  352.0 0.0 collective-permute-done
  352.0 1.9 broadcast_select_fusion.2
  353.9 1.6 maximum_convert_fusion
  355.5 2.8 copy.34
  358.3 0.0 copy-done.4
  358.3 0.8 copy.44
  359.1 0.0 copy-done.5
  359.1 0.7 copy.45
  359.8 0.8 copy.46
  360.6 0.8 copy.47
  (14 shorter events, 0.1 us)
Async XLA Ops:
  7.2 3.7 %copy-start = (bf16[1000,768]{1,0:T(8,128)(2,1)S(1)}, bf16[1000,768]{1,0:T(8,128)(2,1)}, u32[]{:S(2)}) copy-start(bf16[1000,768]{1,0:T(8,128)(2,1)} %param.21) | copy-start | bytes 4608004
  7.2 338.1 %all-reduce.4.cloned.1.call-start = ((), (), s32[]{:S(2)}) async-start(), calls=%async_computation | async-start | bytes 786432 | tf_op jit(solution)/shard_map/psum | solution.py:1076
  210.3 3.4 copy-start.1
  215.7 136.3 %collective-permute-start.1 = (bf16[4,256,192]{2,1,0:T(8,128)(2,1)}, bf16[4,256,192]{2,1,0:T(8,128)(2,1)}, u32[]{:S(2)}, u32[]{:S(2)}) collective-permute-start(bf16[4,256,192]{2,1,0:T(8,128)(2,1)} %get-tuple-element.54), channel_id=1, source_target_pairs={{16,24},{24,16},{17,25},{25,17},{18,26},{26,18},{19,27},{27,19},{2... | collective-permute-start | bytes 1179656 | tf_op jit(solution)/shard_map/ppermute | solution.py:1008
  217.1 134.8 %collective-permute-start.2 = (bf16[4,256,192]{2,1,0:T(8,128)(2,1)}, bf16[4,256,192]{2,1,0:T(8,128)(2,1)}, u32[]{:S(2)}, u32[]{:S(2)}) collective-permute-start(bf16[4,256,192]{2,1,0:T(8,128)(2,1)} %get-tuple-element.53), channel_id=1, source_target_pairs={{16,8},{24,0},{17,9},{25,1},{18,10},{26,2},{19,11},{27,3},{20,12},... | collective-permute-start | bytes 1179656 | tf_op jit(solution)/shard_map/ppermute | solution.py:1007
  218.4 133.6 %collective-permute-start = (bf16[4,256,192]{2,1,0:T(8,128)(2,1)}, bf16[4,256,192]{2,1,0:T(8,128)(2,1)}, u32[]{:S(2)}, u32[]{:S(2)}) collective-permute-start(bf16[4,256,192]{2,1,0:T(8,128)(2,1)} %get-tuple-element.52), channel_id=1, source_target_pairs={{16,0},{24,8},{17,1},{25,9},{18,2},{26,10},{19,3},{27,11},{20,4},{... | collective-permute-start | bytes 1179656 | tf_op jit(solution)/shard_map/ppermute | solution.py:1006
  219.7 100.7 %copy-start.7 = (u32[32]{0:T(128)S(1)}, u32[32]{0:T(128)}, u32[]{:S(2)}) copy-start(u32[32]{0:T(128)} %constant.97) | copy-start | bytes 388
  219.7 101.9 %copy-start.6 = (s32[8]{0:T(128)S(1)}, s32[8]{0:T(128)}, u32[]{:S(2)}) copy-start(s32[8]{0:T(128)} %param.19) | copy-start | bytes 100
  355.5 2.9 copy-start.4
  355.5 3.6 copy-start.5
  355.5 4.3 %copy-start.3 = (f32[1,48,3072]{2,1,0:T(8,128)S(1)}, f32[1,48,3072]{2,1,0:T(8,128)}, u32[]{:S(2)}) copy-start(f32[1,48,3072]{2,1,0:T(8,128)} %get-tuple-element.91) | copy-start | bytes 1769476
  358.3 2.3 copy-start.2
Sparse Core Ops, SparseCore 0:
  213.8 131.4 all-reduce.3

commit v2 on v1

--- a/solution.py
+++ b/solution.py
@@ -63,18 +63,26 @@
     proj_in,
     up_in,
     down_in,
-    vec_in,
+    ga_in,
+    sa_in,
+    bq_in,
+    bv_in,
+    bo_in,
+    gm_in,
+    sm_in,
+    bdown_in,
+    bup_in,
     ids_in,
     table_in,
     time_in,
     cot_in,
     act_out,
-    small_out,
-    table_out,
+    sums_out,
     fixed_out,
     moving_out,
     w,
     vecs,
+    table,
     par,
     xs,
     n_a,
@@ -95,8 +103,8 @@
     acc,
     ybuf,
     ysend,
+    act,
     gsum,
-    tsum,
     own_sem,
     x_send,
     x_recv,
@@ -110,7 +118,8 @@
     y_recv,
     v_sem,
     cot_sem,
-    act_sem,
+    act_send,
+    act_recv,
     keep_sem,
     last_sem,
 ):
@@ -123,6 +132,7 @@
     y_dev = (flipped(s, 1), d)
     z_dev = (s, flipped(d, 1))
     c_dev = (s, flipped(d, 0))
+    far_dev = (flipped(flipped(s, 0), 1), d)
     half = width // 2
     quarter = half // 4
     hidden_half = up_in.shape[2] // 2
@@ -130,9 +140,11 @@
     across = flipped(mine, 1)
     scale = 1.0 / math.sqrt(width // HEADS)
     letters_count = table_in.shape[0]
+    padded = table.shape[0]
+    vectors = 16
 
     barrier = pltpu.get_barrier_semaphore()
-    for device in (x_dev, y_dev, z_dev, c_dev):
+    for device in (x_dev, y_dev, z_dev, c_dev, far_dev):
         pl.semaphore_signal(barrier, inc=1, device_id=device, device_id_type=MESH)
 
     own_rows = pl.ds(pl.multiple_of(part * half, 16), half)
@@ -222,15 +234,19 @@
         c1_arrival(tile).wait_recv()
         c2_arrival(tile).wait_recv()
 
-    vec_own = pltpu.make_async_copy(vec_in, vecs.at[part], v_sem.at[0])
-    vec_own.start()
     for tile in range(TILES):
         for copy in own_copies(tile):
             copy.start()
+    singles = (ga_in, sa_in, bq_in, bv_in, bo_in, gm_in, sm_in, bdown_in)
+    for index, single in enumerate(singles):
+        vecs[part, index : index + 1, :] = single[...].astype(F32)
+    for j in range(4):
+        vecs[part, 8 + j : 9 + j, :] = bup_in[:, j * half : (j + 1) * half].astype(F32)
+    vecs[part, 12:16, :] = jnp.zeros((4, half), F32)
+    table[...] = jnp.zeros_like(table)
+    table[:letters_count, :] = table_in[...]
     gsum[...] = jnp.zeros_like(gsum)
-    tsum[...] = jnp.zeros_like(tsum)
-    vec_own.wait()
-    pl.semaphore_wait(barrier, 4)
+    pl.semaphore_wait(barrier, 5)
     vec_copy(part).start()
     for tile in range(TILES):
         for copy in own_copies(tile):
@@ -260,8 +276,8 @@
         pass_second(TILES - 1)
 
     vec_copy(other).wait_recv()
-    par[:, :half] = vecs[0].astype(F32)
-    par[:, half:] = vecs[1].astype(F32)
+    par[:, :half] = vecs[0]
+    par[:, half:] = vecs[1]
     for tile in range(UP):
         ready(tile)
 
@@ -306,8 +322,33 @@
         for copy in copies:
             copy.wait()
 
-    def act_copy(i):
-        return pltpu.make_async_copy(y1.at[i], act_out.at[i], act_sem.at[i])
+    def act_copies(i):
+        copies = []
+        for index, device in enumerate((y_dev, x_dev, far_dev)):
+            copies.append(
+                pltpu.make_async_remote_copy(
+                    src_ref=act.at[i, device[0]],
+                    dst_ref=act_out.at[part, i],
+                    send_sem=act_send.at[i, index],
+                    recv_sem=act_recv.at[part, i],
+                    device_id=device,
+                    device_id_type=MESH,
+                )
+            )
+        return copies
+
+    def act_own(i):
+        return pltpu.make_async_copy(act.at[i, s], act_out.at[part, i], act_send.at[i, 3])
+
+    def act_arrival(side, i):
+        return pltpu.make_async_remote_copy(
+            src_ref=act.at[i, 0],
+            dst_ref=act_out.at[side, i],
+            send_sem=act_send.at[i, 0],
+            recv_sem=act_recv.at[side, i],
+            device_id=y_dev,
+            device_id_type=MESH,
+        )
 
     def cot_copy(i):
         return pltpu.make_async_copy(cot_in.at[part * seqs + i], ybuf.at[i], cot_sem.at[i])
@@ -327,17 +368,18 @@
 
     lane = lax.broadcasted_iota(jnp.int32, (length, 128), 1)
     low = lane < 64
+    side_scaled = [((lane < 64).astype(F32) * scale).astype(BF), ((lane >= 64).astype(F32) * scale).astype(BF)]
     side_ones = [(lane < 64).astype(F32).astype(BF), (lane >= 64).astype(F32).astype(BF)]
 
     def letters(i):
         ids = ids_in[pl.ds(part * seqs + i, 1), :]
-        place = lax.broadcasted_iota(jnp.int32, (letters_count, length), 0)
+        place = lax.broadcasted_iota(jnp.int32, (padded, length), 0)
         return (place == ids).astype(F32).astype(BF)
 
     def attn_fwd(i):
         @pl.when(stage == 0)
         def _():
-            xs[...] = mul_tn(letters(i), table_in[...]) + time_in[pl.ds(part * seqs + i, 1), :]
+            xs[...] = mul_tn(letters(i), table[...]) + time_in[pl.ds(part * seqs + i, 1), :width]
 
         @pl.when(stage == 1)
         def _():
@@ -364,35 +406,40 @@
                 joint = joint + row(3)
             qkv[i, :, j * width : (j + 1) * width] = joint.astype(BF)
 
-        def pair(hp, _):
+        def first(hp, _):
             at = pl.multiple_of(hp * 128, 128)
             q2 = qkv[i, :, pl.ds(at, 128)]
             k2 = qkv[i, :, pl.ds(width + at, 128)]
-            v2 = qkv[i, :, pl.ds(2 * width + at, 128)]
-            outs = []
             for side in range(2):
-                scores = mul_nt(q2 * side_ones[side], k2) * scale
+                scores = mul_nt(q2 * side_scaled[side], k2)
                 expo = jnp.exp(scores - jnp.max(scores, axis=-1, keepdims=True))
                 total = jnp.sum(expo, axis=-1, keepdims=True)
-                pb = (expo * (1.0 / total)).astype(BF)
-                probs[i, 2 * hp + side] = pb
-                outs.append(mul(pb, v2))
+                probs[i, 2 * hp + side] = (expo * (1.0 / total)).astype(BF)
+            return 0
+
+        def second(hp, _):
+            at = pl.multiple_of(hp * 128, 128)
+            v2 = qkv[i, :, pl.ds(2 * width + at, 128)]
+            outs = [mul(probs[i, 2 * hp + side], v2) for side in range(2)]
             o_s[:, pl.ds(at, 128)] = jnp.where(low, outs[0], outs[1]).astype(BF)
             return 0
 
-        lax.fori_loop(0, HEADS // 2, pair, 0)
+        lax.fori_loop(0, HEADS // 2, first, 0, unroll=6)
+        lax.fori_loop(0, HEADS // 2, second, 0, unroll=6)
         start(keep_o(i))
         y1[i] = (xs[...] + (mul(o_s[...], w[PROJ]) + row(4))).astype(BF)
 
     def feed_fwd(i):
-        @pl.when(i == 0)
-        def _():
-            def one(tile, _):
-                ready(tile)
-                return 0
-
-            lax.fori_loop(UP, TILES, one, 0)
-
+        def arrived(first, last):
+            @pl.when(i == 0)
+            def _():
+                def one(tile, _):
+                    ready(tile)
+                    return 0
+
+                lax.fori_loop(first, last, one, 0)
+
+        arrived(UP, DOWN)
         x = y1[i].astype(F32)
         n, rate = normalize(x)
         n_f[i] = n.astype(BF)
@@ -416,11 +463,15 @@
             gate[j] = a
             bend = (0.5 * GELU_A + 1.5 * GELU_A * GELU_B * square) * u
             slope[i, j] = (both + bend * (1.0 - t * t)).astype(BF)
-            acc[...] += mul(a, w[DOWN + j])
             return 0
 
-        lax.fori_loop(0, 4, one, 0)
+        lax.fori_loop(0, 4, one, 0, unroll=4)
         start(keep_a(i))
+        arrived(DOWN, TILES)
+        down = mul(gate[0], w[DOWN])
+        for j in range(1, 4):
+            down = down + mul(gate[j], w[DOWN + j])
+        acc[...] += down
 
         @pl.when(stage == 0)
         def _():
@@ -429,8 +480,10 @@
 
         @pl.when(stage == 1)
         def _():
-            y1[i] = acc[...].astype(BF)
-            act_copy(i).start()
+            for q in range(4):
+                act[i, q] = acc[:, q * (width // 4) : (q + 1) * (width // 4)].astype(BF)
+            start(act_copies(i))
+            act_own(i).start()
 
     def feed_bwd(i):
         @pl.when(stage == 0)
@@ -442,23 +495,24 @@
             cot_copy(i).wait()
 
         start(last_gz(i))
-        gsum[7:8, :] += column(ybuf[i].astype(F32))
+        gsum[7:8, :width] += column(ybuf[i].astype(F32))
         acc[...] = jnp.zeros_like(acc)
 
         def one(j, _):
             ga = mul_nt(ybuf[i], w[DOWN + j])
             gu = (ga * slope[i, j].astype(F32)).astype(BF)
             slope[i, j] = gu
-            gsum[pl.ds(8 + j, 1), :] += column(gu.astype(F32))
-            acc[...] += mul_nt(gu, w[UP + j])
+            gsum[pl.ds(8 + j, 1), :width] += column(gu.astype(F32))
             return 0
 
-        lax.fori_loop(0, 4, one, 0)
+        lax.fori_loop(0, 4, one, 0, unroll=4)
         start(last_gu(i))
-        gh = acc[...]
+        gh = mul_nt(slope[i, 0], w[UP])
+        for j in range(1, 4):
+            gh = gh + mul_nt(slope[i, j], w[UP + j])
         n = n_f[i].astype(F32)
-        gsum[5:6, :] += column(gh * n)
-        gsum[6:7, :] += column(gh)
+        gsum[5:6, :width] += column(gh * n)
+        gsum[6:7, :width] += column(gh)
         gx = ybuf[i].astype(F32) + scaled_back(gh, row(5), n, r_f[i][:, 0:1])
 
         @pl.when(i > 0)
@@ -470,16 +524,14 @@
         start(keep_g1(i))
 
     def attn_bwd(i):
-        gsum[4:5, :] += column(g1[...].astype(F32))
+        gsum[4:5, :width] += column(g1[...].astype(F32))
         go_s[...] = mul_nt(g1[...], w[PROJ]).astype(BF)
 
-        def pair(hp, _):
+        def first(hp, _):
             at = pl.multiple_of(hp * 128, 128)
-            q2 = qkv[i, :, pl.ds(at, 128)]
-            k2 = qkv[i, :, pl.ds(width + at, 128)]
             v2 = qkv[i, :, pl.ds(2 * width + at, 128)]
             go2 = go_s[:, pl.ds(at, 128)]
-            gq, gk, gv = [], [], []
+            gv = []
             for side in range(2):
                 pb = probs[i, 2 * hp + side]
                 gp = mul_nt(go2 * side_ones[side], v2)
@@ -487,21 +539,32 @@
                 pg = p * gp
                 gs = (pg - p * jnp.sum(pg, axis=-1, keepdims=True)).astype(BF)
                 gv.append(mul_tn(pb, go2))
+                probs[i, 2 * hp + side] = gs
+            gq_s[2, :, pl.ds(at, 128)] = jnp.where(low, gv[0], gv[1]).astype(BF)
+            return 0
+
+        def second(hp, _):
+            at = pl.multiple_of(hp * 128, 128)
+            q2 = qkv[i, :, pl.ds(at, 128)]
+            k2 = qkv[i, :, pl.ds(width + at, 128)]
+            gq, gk = [], []
+            for side in range(2):
+                gs = probs[i, 2 * hp + side]
                 gq.append(mul(gs, k2))
                 gk.append(mul_tn(gs, q2))
             gq_s[0, :, pl.ds(at, 128)] = (jnp.where(low, gq[0], gq[1]) * scale).astype(BF)
             gq_s[1, :, pl.ds(at, 128)] = (jnp.where(low, gk[0], gk[1]) * scale).astype(BF)
-            gq_s[2, :, pl.ds(at, 128)] = jnp.where(low, gv[0], gv[1]).astype(BF)
             return 0
 
-        lax.fori_loop(0, HEADS // 2, pair, 0)
+        lax.fori_loop(0, HEADS // 2, first, 0, unroll=6)
+        lax.fori_loop(0, HEADS // 2, second, 0, unroll=6)
         start(keep_gq(i))
-        gsum[2:3, :] += column(gq_s[0].astype(F32))
-        gsum[3:4, :] += column(gq_s[2].astype(F32))
+        gsum[2:3, :width] += column(gq_s[0].astype(F32))
+        gsum[3:4, :width] += column(gq_s[2].astype(F32))
         gh = mul_nt(gq_s[0], w[QKV]) + mul_nt(gq_s[1], w[QKV + 1]) + mul_nt(gq_s[2], w[QKV + 2])
         n = n_a[i].astype(F32)
-        gsum[0:1, :] += column(gh * n)
-        gsum[1:2, :] += column(gh)
+        gsum[0:1, :width] += column(gh * n)
+        gsum[1:2, :width] += column(gh)
         gx = g1[...].astype(F32) + scaled_back(gh, row(0), n, r_a[i][:, 0:1])
         acc[...] = gx
 
@@ -515,8 +578,12 @@
             high = acc[...].astype(BF)
             rest = (acc[...] - high.astype(F32)).astype(BF)
             hot = letters(i)
-            tsum[:letters_count, :] += mul(hot, high) + mul(hot, rest)
-            tsum[pl.ds(letters_count + part * seqs + i, 1), :] = column(acc[...])
+            gsum[vectors : vectors + padded, :width] += mul(hot, high) + mul(hot, rest)
+            mark = part * seqs + i
+            stamp = time_in[pl.ds(mark, 1), :]
+            gsum[pl.ds(vectors + padded + mark, 1), :] = jnp.concatenate(
+                [column(acc[...]), stamp[:, width:]], axis=1
+            )
 
     def unit(u, _):
         early = u < 2 * seqs
@@ -545,8 +612,7 @@
 
     lax.fori_loop(0, 4 * seqs, unit, 0)
 
-    small_out[...] = gsum[...]
-    table_out[...] = tsum[...]
+    sums_out[...] = gsum[...]
 
     vec_copy(part).wait_send()
 
@@ -568,18 +634,27 @@
 
         @pl.when(stage == 1)
         def _():
-            act_copy(i).wait()
+            for copy in act_copies(i):
+                copy.wait_send()
+            act_own(i).wait()
+            act_arrival(other, i).wait_recv()
+
+        @pl.when(stage == 0)
+        def _():
+            act_arrival(0, i).wait_recv()
+            act_arrival(1, i).wait_recv()
 
         return 0
 
     lax.fori_loop(0, seqs, finish, 0)
 
 
-def run_pipeline(weights, vec, ids, table, times, cot):
+def run_pipeline(weights, singles, ids, table, times, cot):
     rows, length = ids.shape
     width = cot.shape[2]
     seqs = rows // 2
     tokens = seqs * length
+    padded = -(-table.shape[0] // 16) * 16
     dma = pltpu.SemaphoreType.DMA
     anywhere = pl.BlockSpec(memory_space=pl.ANY)
     local = pl.BlockSpec(memory_space=pltpu.VMEM)
@@ -587,17 +662,17 @@
     return pl.pallas_call(
         functools.partial(pipeline_kernel, seqs, length, width),
         out_shape=(
-            jax.ShapeDtypeStruct((seqs, length, width), BF),
-            jax.ShapeDtypeStruct((16, width), F32),
-            jax.ShapeDtypeStruct((table.shape[0] + rows, width), F32),
+            jax.ShapeDtypeStruct((2, seqs, length, width // 4), BF),
+            jax.ShapeDtypeStruct((16 + padded + rows, width + 128), F32),
             jax.ShapeDtypeStruct((4, tokens, width), BF),
             jax.ShapeDtypeStruct((12, tokens, width), BF),
         ),
-        in_specs=[anywhere] * 5 + [local] * 3 + [anywhere],
-        out_specs=(anywhere, local, local, anywhere, anywhere),
+        in_specs=[anywhere] * 4 + [local] * 12 + [anywhere],
+        out_specs=(anywhere, local, anywhere, anywhere),
         scratch_shapes=[
             vm((TILES, width, width), BF),
-            vm((2, 16, width // 2), BF),
+            vm((2, 16, width // 2), F32),
+            vm((padded, width), BF),
             vm((16, width), F32),
             vm((length, width), F32),
             vm((seqs, length, width), BF),
@@ -618,8 +693,8 @@
             vm((length, width), F32),
             vm((seqs, length, width), BF),
             vm((seqs, length, width), BF),
-            vm((16, width), F32),
-            vm((table.shape[0] + rows, width), F32),
+            vm((seqs, 4, length, width // 4), BF),
+            vm((16 + padded + rows, width + 128), F32),
             dma((2 * TILES,)),
         ]
         + [dma((TILES,))] * 8
@@ -628,26 +703,29 @@
             dma((seqs,)),
             dma((3,)),
             dma((seqs,)),
-            dma((seqs,)),
+            dma((seqs, 4)),
+            dma((2, seqs)),
             dma((11,)),
             dma((seqs, 5)),
         ],
         compiler_params=pltpu.CompilerParams(
             collective_id=0, has_side_effects=True, vmem_limit_bytes=62 * 2**20
         ),
-    )(*weights, vec, ids, table, times, cot)
+    )(*weights, *singles, ids, table, times, cot)
 
 
 def reduce_kernel(
     nz,
     half,
     rows,
+    bits,
     fixed_in,
     moving_in,
-    qkv_out,
-    proj_out,
-    up_out,
-    down_out,
+    sums_in,
+    grads_out,
+    small_out,
+    token_out,
+    stamp_out,
     fixed,
     moving,
     parts,
@@ -655,7 +733,10 @@
     x_buf,
     right_buf,
     left_buf,
-    total,
+    sums_buf,
+    adds,
+    adds_buf,
+    stamps,
     fixed_sem,
     moving_sem,
     core_send,
@@ -666,6 +747,14 @@
     right_recv,
     left_send,
     left_recv,
+    sums_send,
+    sums_recv,
+    adds_send,
+    adds_recv,
+    stamps_send,
+    stamps_recv,
+    final_send,
+    final_recv,
 ):
     s = lax.axis_index("section")
     d = lax.axis_index("dp")
@@ -673,21 +762,27 @@
     other = 1 - part
     core = lax.rem(d, 2)
     z = lax.div(d, 2)
+    stage = lax.div(s, 2)
     x_dev = (flipped(s, 0), d)
+    y_dev = (flipped(s, 1), d)
     c_dev = (s, flipped(d, 0))
+    bit_devs = [(s, flipped(d, bit)) for bit in range(bits)]
     ends = nz - 1
     slots = moving.shape[0]
     width = 2 * half
 
     barrier = pltpu.get_barrier_semaphore()
-    for device in (x_dev, c_dev):
+    for device in [x_dev, y_dev] + bit_devs:
         pl.semaphore_signal(barrier, inc=1, device_id=device, device_id_type=MESH)
 
-    @pl.when(z > 0)
+    middle_left = jnp.logical_and(z > 0, lax.rem(z, 2) == 0)
+    middle_right = jnp.logical_and(z < ends, lax.rem(z, 2) == 1)
+
+    @pl.when(middle_left)
     def _():
         pl.semaphore_signal(barrier, inc=1, device_id=(s, d - 2), device_id_type=MESH)
 
-    @pl.when(z < ends)
+    @pl.when(middle_right)
     def _():
         pl.semaphore_signal(barrier, inc=1, device_id=(s, d + 2), device_id_type=MESH)
 
@@ -709,7 +804,7 @@
     for index in (1, 3, 2):
         load_fixed(index).start()
 
-    neighbours = 2 + (z > 0).astype(jnp.int32) + (z < ends).astype(jnp.int32)
+    neighbours = 2 + bits + middle_left.astype(jnp.int32) + middle_right.astype(jnp.int32)
     pl.semaphore_wait(barrier, neighbours)
 
     def core_copy(k):
@@ -787,34 +882,112 @@
     def close_step(k):
         @pl.when(z == 0)
         def _():
-            total[...] = parts[k, part, z, core].astype(F32) + left_buf[k, z].astype(F32)
+            grads_out[k] = parts[k, part, z, core].astype(F32) + left_buf[k, z].astype(F32)
 
         @pl.when(z == ends)
         def _():
-            total[...] = parts[k, part, z, core].astype(F32) + right_buf[k, z].astype(F32)
+            grads_out[k] = parts[k, part, z, core].astype(F32) + right_buf[k, z].astype(F32)
 
         @pl.when(jnp.logical_and(z > 0, z < ends))
         def _():
             sides = left_buf[k, z].astype(F32) + right_buf[k, z].astype(F32)
-            total[...] = parts[k, part, z, core].astype(F32) + sides
-
-        @pl.when(k < 4)
-        def _():
-            for side in range(2):
-                at = pl.multiple_of(side * 4 * half + k * half, 128)
-                up_out[0, :, pl.ds(at, half)] = total[:, side * half : (side + 1) * half]
-
-        @pl.when(jnp.logical_and(k >= 4, k < 7))
-        def _():
-            qkv_out[0, :, pl.ds(pl.multiple_of((k - 4) * width, 128), width)] = total[...]
-
-        @pl.when(k == 7)
-        def _():
-            proj_out[0] = total[...]
-
-        @pl.when(k >= 8)
-        def _():
-            down_out[0, pl.ds(pl.multiple_of((k - 8) * rows, 8), rows), :] = total[...]
+            grads_out[k] = parts[k, part, z, core].astype(F32) + sides
+
+    vectors = small_out.shape[0]
+    count = adds.shape[1]
+    own_stamps = sums_in.shape[0] - count
+
+    def sums_copy():
+        return pltpu.make_async_remote_copy(
+            src_ref=sums_in,
+            dst_ref=sums_buf,
+            send_sem=sums_send,
+            recv_sem=sums_recv,
+            device_id=x_dev,
+            device_id_type=MESH,
+        )
+
+    def adds_copy(bit):
+        return pltpu.make_async_remote_copy(
+            src_ref=adds.at[bit],
+            dst_ref=adds_buf.at[bit],
+            send_sem=adds_send.at[bit],
+            recv_sem=adds_recv.at[bit],
+            device_id=bit_devs[bit],
+            device_id_type=MESH,
+        )
+
+    def block(bit, place):
+        size = own_stamps * 2**bit
+        return pl.ds(pl.multiple_of(lax.div(place, 2**bit) * size, 8), size)
+
+    def stamps_copy(bit):
+        return pltpu.make_async_remote_copy(
+            src_ref=stamps.at[block(bit, d)],
+            dst_ref=stamps.at[block(bit, d)],
+            send_sem=stamps_send.at[bit],
+            recv_sem=stamps_recv.at[bit],
+            device_id=bit_devs[bit],
+            device_id_type=MESH,
+        )
+
+    def stamps_arrival(bit):
+        place = block(bit, bit_devs[bit][1])
+        return pltpu.make_async_remote_copy(
+            src_ref=stamps.at[place],
+            dst_ref=stamps.at[place],
+            send_sem=stamps_send.at[bit],
+            recv_sem=stamps_recv.at[bit],
+            device_id=bit_devs[bit],
+            device_id_type=MESH,
+        )
+
+    def final_copies():
+        pairs = ((adds.at[bits, pl.ds(vectors, count - vectors)], token_out), (stamps, stamp_out))
+        return [
+            pltpu.make_async_remote_copy(
+                src_ref=src,
+                dst_ref=dst,
+                send_sem=final_send.at[index],
+                recv_sem=final_recv.at[index],
+                device_id=y_dev,
+                device_id_type=MESH,
+            )
+            for index, (src, dst) in enumerate(pairs)
+        ]
+
+    def small_step(t):
+        @pl.when(t == 2)
+        def _():
+            sums_copy().wait_recv()
+            adds[0] = sums_in[:count, : 2 * half] + sums_buf[:count, : 2 * half]
+            stamps[block(0, d), :] = sums_in[count:, :] + sums_buf[count:, :]
+            adds_copy(0).start()
+            stamps_copy(0).start()
+
+        for bit in range(bits):
+
+            @pl.when(t == 4 + 2 * bit)
+            def _():
+                adds_copy(bit).wait_recv()
+                stamps_arrival(bit).wait_recv()
+                adds[bit + 1] = adds[bit] + adds_buf[bit]
+                if bit + 1 < bits:
+                    adds_copy(bit + 1).start()
+                    stamps_copy(bit + 1).start()
+
+        @pl.when(t == 5 + 2 * bits)
+        def _():
+            small_out[...] = adds[bits, :vectors]
+
+            @pl.when(stage == 0)
+            def _():
+                for copy in final_copies():
+                    copy.start()
+                token_out[...] = adds[bits, vectors:]
+                stamp_out[...] = stamps[...]
+
+    sums_copy().start()
 
     def product(turn):
         load_moving(turn).wait()
@@ -869,6 +1042,8 @@
         @pl.when(t < TILES)
         def _():
             core_copy(t).start()
+
+        small_step(t)
 
         k1 = t - 1
 
@@ -926,9 +1101,23 @@
         return 0
 
     lax.fori_loop(0, TILES, settle, 0)
-
-
-def run_reduce(fixed, moving, replicas):
+    sums_copy().wait_send()
+    for bit in range(bits):
+        adds_copy(bit).wait_send()
+        stamps_copy(bit).wait_send()
+
+    @pl.when(stage == 0)
+    def _():
+        for copy in final_copies():
+            copy.wait_send()
+
+    @pl.when(stage == 1)
+    def _():
+        for copy in final_copies():
+            copy.wait_recv()
+
+
+def run_reduce(fixed, moving, sums, vectors, stamp_rows, replicas):
     tokens, width = fixed.shape[1:]
     nz = replicas // 2
     half = width // 2
@@ -936,16 +1125,19 @@
     dma = pltpu.SemaphoreType.DMA
     vm = pltpu.VMEM
     slots = 3
+    bits = replicas.bit_length() - 1
+    count = sums.shape[0] - stamp_rows
+    local = pl.BlockSpec(memory_space=pltpu.VMEM)
     return pl.pallas_call(
-        functools.partial(reduce_kernel, nz, half, rows),
+        functools.partial(reduce_kernel, nz, half, rows, bits),
         out_shape=(
-            jax.ShapeDtypeStruct((1, rows, 3 * width), F32),
-            jax.ShapeDtypeStruct((1, rows, width), F32),
-            jax.ShapeDtypeStruct((1, rows, 4 * width), F32),
-            jax.ShapeDtypeStruct((1, 4 * rows, width), F32),
+            jax.ShapeDtypeStruct((TILES, rows, width), F32),
+            jax.ShapeDtypeStruct((vectors, width), F32),
+            jax.ShapeDtypeStruct((count - vectors, width), F32),
+            jax.ShapeDtypeStruct((stamp_rows * replicas, sums.shape[1]), F32),
         ),
-        in_specs=[pl.BlockSpec(memory_space=pl.ANY)] * 2,
-        out_specs=(pl.BlockSpec(memory_space=pltpu.VMEM),) * 4,
+        in_specs=[pl.BlockSpec(memory_space=pl.ANY)] * 2 + [local],
+        out_specs=(local,) * 4,
         scratch_shapes=[
             vm((4, tokens, width), BF),
             vm((slots, tokens, width), BF),
@@ -954,7 +1146,10 @@
             vm((TILES, nz, rows, width), BF),
             vm((TILES, nz, rows, width), BF),
             vm((TILES, nz, rows, width), BF),
-            vm((rows, width), F32),
+            vm(sums.shape, F32),
+            vm((bits + 1, count, width), F32),
+            vm((bits, count, width), F32),
+            vm((stamp_rows * replicas, sums.shape[1]), F32),
             dma((4,)),
             dma((slots,)),
             dma((TILES,)),
@@ -965,11 +1160,126 @@
             dma((TILES, nz)),
             dma((TILES, nz)),
             dma((TILES, nz)),
+            dma,
+            dma,
+            dma((bits,)),
+            dma((bits,)),
+            dma((bits,)),
+            dma((bits,)),
+            dma((2,)),
+            dma((2,)),
         ],
         compiler_params=pltpu.CompilerParams(
             collective_id=1, has_side_effects=True, vmem_limit_bytes=62 * 2**20
         ),
-    )(fixed, moving)
+    )(fixed, moving, sums)
+
+
+def three_parts(value):
+    first = value.astype(BF)
+    rest = value - first.astype(F32)
+    second = rest.astype(BF)
+    return first, second, (rest - second.astype(F32)).astype(BF)
+
+
+def finish_kernel(
+    replicas,
+    act,
+    grads,
+    small,
+    token,
+    stamp,
+    act_out,
+    token_out,
+    time_out,
+    ga_out,
+    sa_out,
+    qkv_out,
+    bq_out,
+    bv_out,
+    proj_out,
+    bo_out,
+    gm_out,
+    sm_out,
+    up_out,
+    bup_out,
+    down_out,
+    bdown_out,
+):
+    s = lax.axis_index("section")
+    d = lax.axis_index("dp")
+    part = lax.rem(s, 2)
+    rows, width = grads.shape[1:]
+    half = width // 2
+    quarter = width // 4
+    seqs = act.shape[1]
+    for side in range(2):
+        act_out[side * seqs : (side + 1) * seqs] = act[side].astype(F32)
+    for j in range(4):
+        for side in range(2):
+            first = side * 4 * half + j * half
+            up_out[0, :, first : first + half] = grads[j, :, side * half : (side + 1) * half]
+    for j in range(3):
+        qkv_out[0, :, j * width : (j + 1) * width] = grads[4 + j]
+    proj_out[0] = grads[7]
+    for j in range(4):
+        down_out[0, j * rows : (j + 1) * rows, :] = grads[8 + j]
+    halves = small[:, pl.ds(pl.multiple_of(part * half, 128), half)]
+    turned = pltpu.roll(halves, lax.rem(half - d * rows, half), 1)
+    outs = (ga_out, sa_out, bq_out, bv_out, bo_out, gm_out, sm_out, bdown_out)
+    for index, out in enumerate(outs):
+        out[...] = turned[index : index + 1, :rows]
+    per_row = half // (4 * rows)
+    ups = small[pl.ds(8 + lax.div(d, per_row), 1), pl.ds(pl.multiple_of(part * half, 128), half)]
+    ups = pltpu.roll(jnp.broadcast_to(ups, (8, half)), lax.rem(half - lax.rem(d, per_row) * 4 * rows, half), 1)
+    bup_out[...] = ups[0:1, : 4 * rows]
+    times_count = time_out.shape[0]
+    spread = -(-times_count // 128) * 128
+    place = lax.broadcasted_iota(jnp.int32, (stamp.shape[0], spread), 1).astype(F32)
+    hot = (place == stamp[:, width : width + 1]).astype(F32).astype(BF)
+    for q in range(4):
+
+        @pl.when(s == q)
+        def _():
+            at = slice(q * quarter, (q + 1) * quarter)
+            token_out[...] = token[: token_out.shape[0], at]
+            sums = jnp.zeros((spread, quarter), F32)
+            for piece in three_parts(stamp[:, at]):
+                sums = sums + mul_tn(hot, piece)
+            time_out[...] = sums[:times_count]
+
+
+def run_finish(act, grads, small, token, stamp, letters_count, times_count, replicas):
+    rows, width = grads.shape[1:]
+    length = act.shape[2]
+    quarter = width // 4
+    local = pl.BlockSpec(memory_space=pltpu.VMEM)
+    single = (1, rows)
+    shapes = [
+        (2 * act.shape[1], length, quarter),
+        (letters_count, quarter),
+        (times_count, quarter),
+        single,
+        single,
+        (1, rows, 3 * width),
+        single,
+        single,
+        (1, rows, width),
+        single,
+        single,
+        single,
+        (1, rows, 4 * width),
+        (1, 4 * rows),
+        (1, 4 * rows, width),
+        single,
+    ]
+    return pl.pallas_call(
+        functools.partial(finish_kernel, replicas),
+        out_shape=tuple(jax.ShapeDtypeStruct(shape, F32) for shape in shapes),
+        in_specs=[local] * 5,
+        out_specs=(local,) * len(shapes),
+        compiler_params=pltpu.CompilerParams(vmem_limit_bytes=60 * 2**20),
+    )(act, grads, small, token, stamp)
 
 
 def plain_reduce(fixed, moving, lower):
@@ -994,25 +1304,6 @@
         pairs = [(i, i ^ 1) for i in range(lax.axis_size("section"))]
         results.append((ours + lax.ppermute(theirs, "section", pairs).astype(F32))[None])
     return results
-
-
-def spread_activations(act, section, width):
-    quarter = width // 4
-    part = lax.rem(section, 2)
-
-    def piece(index):
-        return lax.dynamic_slice_in_dim(act, index * quarter, quarter, axis=2)
-
-    straight = lax.ppermute(piece(part), "section", [(2, 0), (3, 1)])
-    crossed = lax.ppermute(piece(1 - part), "section", [(2, 1), (3, 0)])
-    beside = lax.ppermute(piece(3 - part), "section", [(2, 3), (3, 2)])
-    upper = section >= 2
-    same = jnp.where(upper, piece(2 + part), straight)
-    far = jnp.where(upper, beside, crossed)
-    lower = part == 0
-    first = jnp.where(lower, same, far)
-    second = jnp.where(lower, far, same)
-    return jnp.concatenate([first, second], axis=0).astype(F32)
 
 
 def per_device(
@@ -1046,65 +1337,64 @@
     letters_count = token_table.shape[0]
     times_count = time_table.shape[0]
     padded = -(-letters_count // 16) * 16
-    vec = jnp.concatenate(
-        [
-            attn_gain,
-            attn_shift,
-            query_bias,
-            value_bias,
-            proj_bias,
-            mlp_gain,
-            mlp_shift,
-            down_bias,
-            up_bias.reshape(4, half),
-            jnp.zeros((4, half), BF),
-        ],
-        axis=0,
+    singles = (
+        attn_gain,
+        attn_shift,
+        query_bias,
+        value_bias,
+        proj_bias,
+        mlp_gain,
+        mlp_shift,
+        down_bias,
+        up_bias,
     )
-    table = jnp.pad(token_table, ((0, padded - letters_count), (0, 0)))
-    times = jnp.take(time_table, timesteps, axis=0).astype(F32)
-    moments = lax.all_gather(timesteps, "dp", tiled=True)
+    marks = jnp.broadcast_to(timesteps.astype(F32)[:, None], (rows, 128))
+    times = time_table.at[timesteps].get(mode="promise_in_bounds").astype(F32)
+    times = jnp.concatenate([times, marks], axis=1)
     weights = (qkv_weight, proj_weight, up_weight, down_weight)
-    act, small, tables, fixed, moving = run_pipeline(weights, vec, token_ids, table, times, cotangent)
-    activations = spread_activations(act, section, width)
-    total_rows = rows * replicas
-    mine = jnp.zeros((2, 16, width), F32)
-    mine = lax.dynamic_update_slice_in_dim(mine, small[None], layer, 0)
-    placed = jnp.zeros((total_rows, width), F32)
-    placed = lax.dynamic_update_slice_in_dim(placed, tables[padded:], replica * rows, 0)
-    joined = jnp.concatenate([tables[:padded], mine.reshape(32, width), placed], axis=0)
+    act, sums, fixed, moving = run_pipeline(weights, singles, token_ids, token_table, times, cotangent)
+    vectors = 16
+    if half % (16 * replicas) == 0 and replicas & (replicas - 1) == 0:
+        grads, small, token, stamp = run_reduce(fixed, moving, sums, vectors, rows, replicas)
+        return run_finish(act, grads, small, token, stamp, letters_count, times_count, replicas)
+    qkv_grad, proj_grad, up_grad, down_grad = plain_reduce(fixed, moving, part == 0)
+    activations = act.reshape(rows, length, width // 4).astype(F32)
+    mine = jnp.zeros((2, vectors, width + 128), F32)
+    mine = lax.dynamic_update_slice_in_dim(mine, sums[None, :vectors], layer, 0)
+    placed = jnp.zeros((rows * replicas, width + 128), F32)
+    placed = lax.dynamic_update_slice_in_dim(placed, sums[vectors + padded :], replica * rows, 0)
+    joined = jnp.concatenate(
+        [sums[vectors : vectors + padded], mine.reshape(2 * vectors, width + 128), placed], axis=0
+    )
     joined = lax.psum(joined, ("section", "dp"))
-    if half % (16 * replicas) == 0:
-        qkv_grad, proj_grad, up_grad, down_grad = run_reduce(fixed, moving, replicas)
-    else:
-        qkv_grad, proj_grad, up_grad, down_grad = plain_reduce(fixed, moving, part == 0)
     quarter = width // 4
     columns = lax.dynamic_slice_in_dim(joined, section * quarter, quarter, axis=1)
     token_grad = columns[:letters_count]
-    steps = jnp.arange(times_count, dtype=jnp.int32)
-    hot = (steps[:, None] == moments[None, :]).astype(F32)
-    time_grad = jnp.einsum("tb,bd->td", hot, columns[padded + 32 :], precision=HIGHEST)
-    ours = lax.dynamic_slice(joined, (padded + 16 * layer, part * half), (16, half))
+    first = padded + 2 * vectors
+    steps = jnp.arange(times_count, dtype=jnp.int32).astype(F32)
+    hot = (steps[:, None] == joined[first:, width][None, :]).astype(F32)
+    time_grad = jnp.einsum("tb,bd->td", hot, columns[first:], precision=HIGHEST)
+    ours = lax.dynamic_slice(joined, (padded + vectors * layer, part * half), (vectors, half))
     each = half // replicas
-    vectors = lax.dynamic_slice_in_dim(ours[:8], replica * each, each, axis=1)
+    flat = lax.dynamic_slice_in_dim(ours[:8], replica * each, each, axis=1)
     ups = lax.dynamic_slice_in_dim(ours[8:12].reshape(1, 4 * half), replica * 4 * each, 4 * each, axis=1)
     return (
         activations,
         token_grad,
         time_grad,
-        vectors[0:1],
-        vectors[1:2],
+        flat[0:1],
+        flat[1:2],
         qkv_grad,
-        vectors[2:3],
-        vectors[3:4],
+        flat[2:3],
+        flat[3:4],
         proj_grad,
-        vectors[4:5],
-        vectors[5:6],
-        vectors[6:7],
+        flat[4:5],
+        flat[5:6],
+        flat[6:7],
         up_grad,
         ups,
         down_grad,
-        vectors[7:8],
+        flat[7:8],
     )
 
 

time: 369 us -> 265 us (0.72)
  Pallas kernels: 297 us -> 257 us
  waiting for transfers between devices: 17 us -> 0 us
  local copies, waits for them, and re-layouts: 19.6 us -> 5.24 us
  between operations: 14.9 us -> 0.69 us
  blocking collectives: 6.47 us -> 0 us
  other arithmetic: 7.11 us -> 1.42 us
  starting transfers between devices: 4.06 us -> 0 us
    pallas_call x1, Pallas kernels: 196 us -> 148 us  [run_pipeline(): pl.pallas_call(functools.partial(pipeline_kernel, seqs, length, width), o...]
    psum x1 -> x0, waiting for transfers between devices: 16.9 us -> none  [per_device(): joined = lax.psum(joined, ('section', 'dp'))]
    pallas_call x1 -> x2, Pallas kernels: 101 us -> 109 us  [the longest x1 104 us: run_reduce(): pl.pallas_call(functools.partial(reduce_kernel, nz, half, rows, bits), ou...]
    unnamed x26 -> x4, local copies, waits for them, and re-layouts: 7.56 us -> 0.56 us
    unnamed x1 -> x0, blocking collectives: 6.47 us -> none
    pallas_call x0 -> x2, local copies, waits for them, and re-layouts: none -> 4.04 us  [run_finish(): pl.pallas_call(functools.partial(finish_kernel, replicas), out_shape=tupl...]
    ppermute x3 -> x0, starting transfers between devices: 4.03 us -> none  [the longest x1 1.45 us: spread_activations(): beside = lax.ppermute(piece(3 - part), 'section', [(2, 3), (3, 2)])]
  transfers between devices with their start and end apart: 4 -> 0, of which waited for: 1 -> 0; matrix products, arithmetic and copies ran while one was open for 3% -> 0% of each run, Pallas kernels for 27% -> 0%
where the time goes in v2:
time: 265 us; the launch traced here: 264 us
  Pallas kernels  257 us (97%)
  local copies, waits for them, and re-layouts  5.24 us (2%)
    pallas_call x1, Pallas kernels, run_pipeline(): pl.pallas_call(functools.partial(pipeline_kernel, seqs, length, width), o...  148 us
    pallas_call x1, Pallas kernels, run_reduce(): pl.pallas_call(functools.partial(reduce_kernel, nz, half, rows, bits), ou...  104 us

profile of v2, /device:TPU:0, one launch (start us, length us, event | category | flops | bytes accessed | tf_op | source)
XLA Modules:
  0.0 264.3 jit_solution(9517171065208558467)
XLA Ops:
  0.6 0.0 copy-start
  0.7 0.8 compare_select_fusion
  1.5 0.1 broadcast_in_dim.10
  1.5 0.5 copy-done
  2.1 0.6 gather_fusion
  2.7 0.6 pad_maximum_fusion.time_in
  3.3 147.5 %shard_map.297 = (bf16[2,4,256,192]{3,2,1,0:T(8,128)(2,1)}, f32[56,896]{1,0:T(8,128)}, bf16[4,1024,768]{2,1,0:T(8,128)(2,1)}, bf16[12,1024,768]{2,1,0:T(8,128)(2,1)}) custom-call(bf16[1,384,2304]{2,1,0:T(8,128)(2,1)} %qkv_in.1, bf16[1,384,768]{2,1,0:T(8,128)(2,1)} %proj_in.1, bf16[1,384,3072]{2,1,0:T(8,128)(2,1)} %up_in.1, bf16[1,1536,768]{2,1,0:T(8,128)(2,1)} %down_in.1, ...), custom_call_target="tpu_custom_call" | custom-call | tf_op jit(solution)/shard_map/pallas_call | solution.py:662
  150.8 104.4 %shard_map.298 = (f32[12,48,768]{2,1,0:T(8,128)}, f32[16,768]{1,0:T(8,128)}, f32[32,768]{1,0:T(8,128)}, f32[64,896]{1,0:T(8,128)}) custom-call(bf16[4,1024,768]{2,1,0:T(8,128)(2,1)} %get-tuple-element.25.fixed_in, bf16[12,1024,768]{2,1,0:T(8,128)(2,1)} %get-tuple-element.26.moving_in, f32[56,896]{1,0:T(8,128)} %get-tuple-element.27.sums_in), custom_call_target="tpu_custom_call" | custom-call | tf_op jit(solution)/shard_map/pallas_call | solution.py:1131
  255.3 5.0 %shard_map.299 = (f32[8,256,192]{2,1,0:T(8,128)}, f32[27,192]{1,0:T(8,128)}, f32[1000,192]{1,0:T(8,128)}, f32[1,48]{1,0:T(1,128)}, f32[1,48]{1,0:T(1,128)}, /*in...) custom-call(bf16[2,4,256,192]{3,2,1,0:T(8,128)(2,1)} %get-tuple-elem, ...), custom_call_target="tpu_custom_call" | custom-call | tf_op jit(solution)/shard_map/pallas_call | solution.py:1276
  260.3 0.0 copy-start.1
  260.3 2.8 %copy.34 = f32[8,256,192]{1,2,0:T(8,128)} copy(f32[8,256,192]{2,1,0:T(8,128)} %get-tuple-element.32) | data formatting | bytes 3145728 | tf_op jit(solution)/shard_map/pallas_call | solution.py:1276
  263.1 0.0 copy-done.1
  263.1 1.2 copy.35
  (2 shorter events, 0.0 us)
Async XLA Ops:
  0.6 1.4 copy-start
  260.3 2.9 %copy-start.1 = (f32[1000,192]{1,0:T(8,128)S(1)}, f32[1000,192]{1,0:T(8,128)}, u32[]{:S(2)}) copy-start(f32[1000,192]{1,0:T(8,128)} %get-tuple-element.34) | copy-start | bytes 2304004

commit v3 on v1

v3 whole, which is shorter than its diff:
```python
import functools
import math

import jax
import jax.numpy as jnp
from jax import lax
from jax.experimental import pallas as pl
from jax.experimental.pallas import tpu as pltpu
from jax.sharding import PartitionSpec as P

HEADS = 12
EPS = 1e-05
HIGHEST = lax.Precision.HIGHEST
MESH = pl.DeviceIdType.MESH
BF = jnp.bfloat16
F32 = jnp.float32
TILES = 12
QKV, PROJ, UP, DOWN = 0, 3, 4, 8
GELU_A = math.sqrt(2.0 / math.pi)
GELU_B = 0.044715


def flipped(value, bit):
    mask = 2**bit
    return value + mask - 2 * mask * lax.rem(lax.div(value, mask), 2)


def mul(a, b):
    return lax.dot_general(a, b, (((1,), (0,)), ((), ())), preferred_element_type=F32)


def mul_nt(a, b):
    return lax.dot_general(a, b, (((1,), (1,)), ((), ())), preferred_element_type=F32)


def mul_tn(a, b):
    return lax.dot_general(a, b, (((0,), (0,)), ((), ())), preferred_element_type=F32)


def normalize(x):
    mean = jnp.mean(x, axis=-1, keepdims=True)
    centered = x - mean
    spread = jnp.mean(centered * centered, axis=-1, keepdims=True)
    rate = lax.rsqrt(spread + EPS)
    return centered * rate, rate


def scaled_back(gh, gain, n, rate):
    gn = gh * gain
    inner = jnp.mean(gn * n, axis=-1, keepdims=True)
    return (gn - jnp.mean(gn, axis=-1, keepdims=True) - n * inner) * rate


def column(values):
    return jnp.sum(values, axis=0, keepdims=True)


class Refs:
    def __init__(self, names, refs):
        for name, ref in zip(names, refs, strict=True):
            setattr(self, name, ref)


INPUTS = (
    "qkv_in proj_in up_in down_in ga_in sa_in bq_in bv_in bo_in gm_in sm_in bdown_in bup_in "
    "ids_in table_in time_in cot_in"
).split()


def layer_kernel(seqs, length, width, fused, names, *all_refs):
    refs = Refs(names, all_refs)
    w, par, qkv, probs = refs.w, refs.par, refs.qkv, refs.probs
    xs, acc, ybuf, ysend, y1 = refs.xs, refs.acc, refs.ybuf, refs.ysend, refs.y1
    slope, gate, h_s, o_s, hf_s, go_s = refs.slope, refs.gate, refs.h_s, refs.o_s, refs.hf_s, refs.go_s
    act, landed, gsum = refs.act, refs.landed, refs.gsum
    s = lax.axis_index("section")
    d = lax.axis_index("dp")
    stage = lax.div(s, 2)
    part = lax.rem(s, 2)
    other = 1 - part
    core = lax.rem(d, 2)
    z = lax.div(d, 2)
    x_dev = (flipped(s, 0), d)
    y_dev = (flipped(s, 1), d)
    far_dev = (flipped(flipped(s, 0), 1), d)
    z_dev = (s, flipped(d, 1))
    c_dev = (s, flipped(d, 0))
    half = width // 2
    wide = width // 4
    hidden_half = 4 * half
    rows = w.shape[4]
    mine = lax.rem(d, 4)
    across = flipped(mine, 1)
    scale = 1.0 / math.sqrt(width // HEADS)
    letters_count = refs.table_in.shape[0]
    padded = refs.table.shape[0]
    vectors = 16
    count = vectors + padded
    nz = lax.axis_size("dp") // 2
    zbits = nz.bit_length() - 1
    ends = nz - 1

    def send(src, dst, send_sem, recv_sem, device):
        return pltpu.make_async_remote_copy(
            src_ref=src,
            dst_ref=dst,
            send_sem=send_sem,
            recv_sem=recv_sem,
            device_id=device,
            device_id_type=MESH,
        )

    def start(copies):
        for copy in copies:
            copy.start()

    def wait(copies):
        for copy in copies:
            copy.wait()

    def signal(sem, device):
        pl.semaphore_signal(sem, inc=1, device_id=device, device_id_type=MESH)

    barrier = pltpu.get_barrier_semaphore()
    greeted = [x_dev, y_dev, far_dev, c_dev, z_dev]
    if fused:
        greeted += [(s, flipped(d, 1 + bit)) for bit in range(1, zbits)]
    for device in greeted:
        signal(barrier, device)
    expected = len(greeted)
    if fused:
        middle_left = jnp.logical_and(z > 0, lax.rem(z, 2) == 0)
        middle_right = jnp.logical_and(z < ends, lax.rem(z, 2) == 1)

        @pl.when(middle_left)
        def _():
            signal(barrier, (s, d - 2))

        @pl.when(middle_right)
        def _():
            signal(barrier, (s, d + 2))

        expected = expected + middle_left.astype(jnp.int32) + middle_right.astype(jnp.int32)

    def tile(index):
        return w[index].reshape(width, width)

    def own_copies(index):
        if index < PROJ:
            pairs = [(refs.qkv_in.at[:, :, :, pl.ds(index * width, width)], w.at[index, part])]
        elif index < UP:
            pairs = [(refs.proj_in, w.at[index, part])]
        elif index < DOWN:
            pairs = [
                (
                    refs.up_in.at[:, :, :, pl.ds(side * hidden_half + (index - UP) * half, half)],
                    w.at[index, part, :, :, :, pl.ds(side * half, half)],
                )
                for side in range(2)
            ]
        else:
            pairs = [(refs.down_in.at[index - DOWN], w.at[index, part])]
        return [
            pltpu.make_async_copy(src, dst, refs.own_sem.at[2 * index + k])
            for k, (src, dst) in enumerate(pairs)
        ]

    def x_weight(index):
        place = w.at[index, part, mine]
        return send(place, place, refs.wx_send.at[index], refs.wx_recv.at[index], x_dev)

    def relay(index, which, send_sem, recv_sem, device):
        place = w.at[index, other, which]
        return send(place, place, send_sem.at[index], recv_sem.at[index], device)

    def z_weight(index):
        return relay(index, mine, refs.wz_send, refs.wz_recv, z_dev)

    def c1_weight(index):
        return relay(index, mine, refs.c1_send, refs.c1_recv, c_dev)

    def c2_weight(index):
        return relay(index, across, refs.c2_send, refs.c2_recv, c_dev)

    def pass_first(index):
        relay(index, mine, refs.wx_send, refs.wx_recv, x_dev).wait_recv()
        z_weight(index).start()
        c1_weight(index).start()

    def pass_second(index):
        relay(index, across, refs.wz_send, refs.wz_recv, z_dev).wait_recv()
        c2_weight(index).start()

    def ready(index):
        relay(index, flipped(mine, 0), refs.c1_send, refs.c1_recv, c_dev).wait_recv()
        relay(index, flipped(across, 0), refs.c2_send, refs.c2_recv, c_dev).wait_recv()

    def settle_weights():
        def settle(index, _):
            x_weight(index).wait_send()
            z_weight(index).wait_send()
            c1_weight(index).wait_send()
            c2_weight(index).wait_send()
            return 0

        lax.fori_loop(0, TILES, settle, 0)

    def vec_copy(which):
        place = refs.vecs.at[which]
        return send(place, place, refs.vec_sem.at[0], refs.vec_sem.at[1], x_dev)

    for index in range(TILES):
        start(own_copies(index))
    singles = ("ga", "sa", "bq", "bv", "bo", "gm", "sm", "bdown")
    for index, name in enumerate(singles):
        refs.vecs[part, index : index + 1, :] = getattr(refs, name + "_in")[...].astype(F32)
    for j in range(4):
        refs.vecs[part, 8 + j : 9 + j, :] = refs.bup_in[:, j * half : (j + 1) * half].astype(F32)
    refs.vecs[part, 12:16, :] = jnp.zeros((4, half), F32)
    refs.table[...] = jnp.zeros_like(refs.table)
    refs.table[:letters_count, :] = refs.table_in[...]
    gsum[...] = jnp.zeros_like(gsum)
    pl.semaphore_wait(barrier, expected)
    for index in range(TILES):
        wait(own_copies(index))
        x_weight(index).start()
        if index == 3:
            vec_copy(part).start()

    pass_first(0)
    pass_first(1)
    pass_second(0)
    pass_first(2)
    pass_second(1)
    pass_first(3)
    pass_second(2)
    pass_first(4)
    pass_second(3)
    pass_first(5)

    @pl.when(stage == 1)
    def _():
        def step(index, _):
            pass_second(index - 2)
            pass_first(index)
            return 0

        lax.fori_loop(6, TILES, step, 0)
        pass_second(TILES - 2)
        pass_second(TILES - 1)

    vec_copy(other).wait_recv()
    par[:, :half] = refs.vecs[0]
    par[:, half:] = refs.vecs[1]
    for index in range(UP):
        ready(index)

    def act_copies(i):
        slot = lax.rem(i, 2)
        return [
            send(
                act.at[slot, device[0]],
                landed.at[part, i],
                refs.act_send.at[i, index],
                refs.act_recv.at[part, i],
                device,
            )
            for index, device in enumerate((y_dev, x_dev, far_dev))
        ]

    def act_own(i):
        return pltpu.make_async_copy(act.at[lax.rem(i, 2), s], landed.at[part, i], refs.act_send.at[i, 3])

    def act_arrival(side, i):
        return send(act.at[0, 0], landed.at[side, i], refs.act_send.at[i, 0], refs.act_recv.at[side, i], y_dev)

    def act_settle(i):
        for copy in act_copies(i):
            copy.wait_send()

    def cot_copy(i):
        return pltpu.make_async_copy(refs.cot_in.at[part * seqs + i], ybuf.at[i], refs.cot_sem.at[i])

    def y_copy(i):
        return send(ysend.at[i], ybuf.at[i], refs.y_send.at[i], refs.y_recv.at[i], y_dev)

    def row(index):
        return par[index : index + 1, :]

    def add_row(index, values):
        gsum[index : index + 1, :width] += column(values)

    lane = lax.broadcasted_iota(jnp.int32, (length, 128), 1)
    low = lane < 64
    side_ones = [(lane < 64).astype(F32).astype(BF), (lane >= 64).astype(F32).astype(BF)]
    side_scaled = [
        ((lane < 64).astype(F32) * scale).astype(BF),
        ((lane >= 64).astype(F32) * scale).astype(BF),
    ]
    pairs = HEADS // 2

    def letters(i):
        ids = refs.ids_in[pl.ds(part * seqs + i, 1), :]
        place = lax.broadcasted_iota(jnp.int32, (padded, length), 0)
        return (place == ids).astype(F32).astype(BF)

    def attn_fwd(i):
        @pl.when(stage == 0)
        def _():
            xs[...] = mul_tn(letters(i), refs.table[...]) + refs.time_in[pl.ds(part * seqs + i, 1), :width]

        @pl.when(stage == 1)
        def _():
            y_copy(i).wait_recv()
            xs[...] = ybuf[i].astype(F32)
            cot_copy(i).start()

        n, rate = normalize(xs[...])
        refs.n_a[i] = n.astype(BF)
        refs.r_a[i] = jnp.broadcast_to(rate, (length, 128))
        h_s[i] = (n * row(0) + row(1)).astype(BF)
        for j in range(3):
            joint = mul(h_s[i], tile(QKV + j))
            if j == 0:
                joint = joint + row(2)
            if j == 2:
                joint = joint + row(3)
            qkv[i, :, j * width : (j + 1) * width] = joint.astype(BF)

        for hp in range(pairs):
            at = hp * 128
            q2 = qkv[i, :, at : at + 128]
            k2 = qkv[i, :, width + at : width + at + 128]
            for side in range(2):
                scores = mul_nt(q2 * side_scaled[side], k2)
                expo = jnp.exp(scores - jnp.max(scores, axis=-1, keepdims=True))
                total = jnp.sum(expo, axis=-1, keepdims=True)
                probs[i, 2 * hp + side] = (expo * (1.0 / total)).astype(BF)
        for hp in range(pairs):
            at = hp * 128
            v2 = qkv[i, :, 2 * width + at : 2 * width + at + 128]
            outs = [mul(probs[i, 2 * hp + side], v2) for side in range(2)]
            o_s[i, :, at : at + 128] = jnp.where(low, outs[0], outs[1]).astype(BF)
        y1[i] = (xs[...] + (mul(o_s[i], tile(PROJ)) + row(4))).astype(BF)

    def feed_fwd(i):
        def arrived(first, last):
            @pl.when(i == 0)
            def _():
                def one(index, _):
                    ready(index)
                    return 0

                lax.fori_loop(first, last, one, 0)

        arrived(UP, DOWN)
        x = y1[i].astype(F32)
        n, rate = normalize(x)
        refs.n_f[i] = n.astype(BF)
        refs.r_f[i] = jnp.broadcast_to(rate, (length, 128))
        hf_s[i] = (n * row(5) + row(6)).astype(BF)
        acc[...] = x + row(7)
        for j in range(4):
            u = mul(hf_s[i], tile(UP + j)) + row(8 + j)
            square = u * u
            t = jnp.tanh(u * (GELU_A + GELU_A * GELU_B * square))
            both = 0.5 + 0.5 * t
            gate[i, j] = (u * both).astype(BF)
            bend = (0.5 * GELU_A + 1.5 * GELU_A * GELU_B * square) * u
            slope[i, j] = (both + bend * (1.0 - t * t)).astype(BF)
        arrived(DOWN, TILES)
        down = mul(gate[i, 0], tile(DOWN))
        for j in range(1, 4):
            down = down + mul(gate[i, j], tile(DOWN + j))
        acc[...] += down

        @pl.when(stage == 0)
        def _():
            ysend[i] = acc[...].astype(BF)
            y_copy(i).start()

        @pl.when(stage == 1)
        def _():
            @pl.when(i >= 2)
            def _():
                act_settle(i - 2)
                act_own(i - 2).wait()

            for q in range(4):
                act[lax.rem(i, 2), q] = acc[:, q * wide : (q + 1) * wide].astype(BF)
            start(act_copies(i))
            act_own(i).start()

    def feed_bwd(i):
        @pl.when(stage == 0)
        def _():
            y_copy(i).wait_recv()

        @pl.when(stage == 1)
        def _():
            cot_copy(i).wait()

        add_row(7, ybuf[i].astype(F32))
        for j in range(4):
            ga = mul_nt(ybuf[i], tile(DOWN + j))
            gu = (ga * slope[i, j].astype(F32)).astype(BF)
            slope[i, j] = gu
            add_row(8 + j, gu.astype(F32))
        gh = mul_nt(slope[i, 0], tile(UP))
        for j in range(1, 4):
            gh = gh + mul_nt(slope[i, j], tile(UP + j))
        n = refs.n_f[i].astype(F32)
        add_row(5, gh * n)
        add_row(6, gh)
        gx = ybuf[i].astype(F32) + scaled_back(gh, row(5), n, refs.r_f[i][:, 0:1])
        y1[i] = gx.astype(BF)

    def attn_bwd(i):
        add_row(4, y1[i].astype(F32))
        go_s[...] = mul_nt(y1[i], tile(PROJ)).astype(BF)
        for hp in range(pairs):
            at = hp * 128
            v2 = qkv[i, :, 2 * width + at : 2 * width + at + 128]
            go2 = go_s[:, at : at + 128]
            gv = []
            for side in range(2):
                pb = probs[i, 2 * hp + side]
                gp = mul_nt(go2 * side_ones[side], v2)
                p = pb.astype(F32)
                pg = p * gp
                gs = (pg - p * jnp.sum(pg, axis=-1, keepdims=True)).astype(BF)
                gv.append(mul_tn(pb, go2))
                probs[i, 2 * hp + side] = gs
            qkv[i, :, 2 * width + at : 2 * width + at + 128] = jnp.where(low, gv[0], gv[1]).astype(BF)
        for hp in range(pairs):
            at = hp * 128
            q2 = qkv[i, :, at : at + 128]
            k2 = qkv[i, :, width + at : width + at + 128]
            gq, gk = [], []
            for side in range(2):
                gs = probs[i, 2 * hp + side]
                gq.append(mul(gs, k2))
                gk.append(mul_tn(gs, q2))
            qkv[i, :, at : at + 128] = (jnp.where(low, gq[0], gq[1]) * scale).astype(BF)
            qkv[i, :, width + at : width + at + 128] = (jnp.where(low, gk[0], gk[1]) * scale).astype(BF)
        pieces = [qkv[i, :, j * width : (j + 1) * width] for j in range(3)]
        add_row(2, pieces[0].astype(F32))
        add_row(3, pieces[2].astype(F32))
        gh = mul_nt(pieces[0], tile(QKV)) + mul_nt(pieces[1], tile(QKV + 1)) + mul_nt(pieces[2], tile(QKV + 2))
        n = refs.n_a[i].astype(F32)
        add_row(0, gh * n)
        add_row(1, gh)
        acc[...] = y1[i].astype(F32) + scaled_back(gh, row(0), n, refs.r_a[i][:, 0:1])

        @pl.when(stage == 1)
        def _():
            ysend[i] = acc[...].astype(BF)
            y_copy(i).start()

        @pl.when(stage == 0)
        def _():
            high = acc[...].astype(BF)
            rest = (acc[...] - high.astype(F32)).astype(BF)
            hot = letters(i)
            gsum[vectors:count, :width] += mul(hot, high) + mul(hot, rest)
            mark = part * seqs + i
            stamp = refs.time_in[pl.ds(mark, 1), :]
            gsum[pl.ds(count + mark, 1), :] = jnp.concatenate([column(acc[...]), stamp[:, width:]], axis=1)

    units = (attn_fwd, feed_fwd, feed_bwd, attn_bwd)
    steps = 0
    if fused:
        step = reduce_steps(refs, seqs, length, width, send, signal, act_arrival, act_own, settle_weights)
        units = units + (step,)
        steps = TILES + 2 + ends

    def unit(u, _):
        early = u < 2 * seqs
        kind0 = jnp.where(early, lax.div(u, seqs), 2 + lax.rem(u, 2))
        index0 = jnp.where(early, lax.rem(u, seqs), lax.div(u, 2) - seqs)
        kind1 = lax.rem(u, 4)
        index1 = lax.div(u, 4)
        if fused:
            last = 4 * seqs - 1
            ahead = 2
            kind0 = jnp.where(u >= last, 4, kind0)
            index0 = jnp.where(u >= last, jnp.where(u < last + ahead, u - last, u - last - 1), index0)
            kind0 = jnp.where(u == last + ahead, 3, kind0)
            index0 = jnp.where(u == last + ahead, seqs - 1, index0)
            kind1 = jnp.where(u > last, 4, kind1)
            index1 = jnp.where(u > last, u - last - 1, index1)
        kind = jnp.where(stage == 0, kind0, kind1)
        i = jnp.where(stage == 0, index0, index1)

        @pl.when(jnp.logical_and(stage == 0, jnp.logical_and(u >= 1, u <= 4)))
        def _():
            pass_second(2 + 2 * u)
            pass_second(3 + 2 * u)

        @pl.when(jnp.logical_and(stage == 0, jnp.logical_and(u >= 1, u <= 3)))
        def _():
            pass_first(4 + 2 * u)
            pass_first(5 + 2 * u)

        for index, run in enumerate(units):

            @pl.when(kind == index)
            def _():
                run(i)

        return 0

    lax.fori_loop(0, 4 * seqs + steps, unit, 0)

    vec_copy(part).wait_send()
    if not fused:
        settle_weights()

    def finish(i, _):
        y_copy(i).wait_send()

        @pl.when(jnp.logical_and(stage == 1, i >= 2))
        def _():
            act_settle(i)

        return 0

    lax.fori_loop(0, seqs, finish, 0)
    if not fused:

        @pl.when(stage == 1)
        def _():
            for i in range(2, seqs):
                act_own(i).wait()

        for i in range(seqs):
            for side in range(2):

                @pl.when(jnp.logical_or(stage == 0, part != side))
                def _():
                    act_arrival(side, i).wait_recv()

        refs.sums_out[...] = gsum[...]
        copies = []
        for i in range(seqs):
            place = pl.ds(i * length, length)
            for index, ref in enumerate((hf_s, h_s, o_s, ybuf)):
                copies.append((ref.at[i], refs.fixed_out.at[index, place]))
            for j in range(4):
                copies.append((slope.at[i, j], refs.moving_out.at[j, place]))
                copies.append((gate.at[i, j], refs.moving_out.at[8 + j, place]))
            for j in range(3):
                copies.append((qkv.at[i, :, pl.ds(j * width, width)], refs.moving_out.at[4 + j, place]))
            copies.append((y1.at[i], refs.moving_out.at[7, place]))
        copies.append((landed, refs.act_out))
        copies = [
            pltpu.make_async_copy(src, dst, refs.keep_sem.at[index]) for index, (src, dst) in enumerate(copies)
        ]
        start(copies)
        wait(copies)


def reduce_steps(refs, seqs, length, width, send, signal, act_arrival, act_own, settle_weights):
    s = lax.axis_index("section")
    d = lax.axis_index("dp")
    stage = lax.div(s, 2)
    part = lax.rem(s, 2)
    other = 1 - part
    core = lax.rem(d, 2)
    z = lax.div(d, 2)
    x_dev = (flipped(s, 0), d)
    y_dev = (flipped(s, 1), d)
    c_dev = (s, flipped(d, 0))
    right_dev = (s, d + 2)
    left_dev = (s, d - 2)
    w, gsum = refs.w, refs.gsum
    nz = w.shape[2]
    rows = w.shape[4]
    ends = nz - 1
    slots = refs.x_buf.shape[0]
    tokens = seqs * length
    core_buf, x_buf, right_buf, left_buf = refs.core_buf, refs.x_buf, refs.right_buf, refs.left_buf
    vectors = 16
    count = vectors + refs.table.shape[0]
    split = count // 2
    zbits = nz.bit_length() - 1
    own = gsum.shape[0] - count

    def where(k):
        return jnp.where(k < 4, k + 4, jnp.where(k < 8, k - 4, k))

    def slot(k):
        return lax.rem(k, slots)

    def core_copy(k):
        return send(
            w.at[where(k), :, :, 1 - core],
            core_buf.at[slot(k)],
            refs.core_send.at[k],
            refs.core_recv.at[k],
            c_dev,
        )

    def x_copy(k):
        return send(
            w.at[where(k), other, :, core], x_buf.at[slot(k)], refs.x_send.at[k], refs.x_recv.at[k], x_dev
        )

    def right_copy(k, j):
        return send(
            w.at[where(k), part, j, core],
            right_buf.at[slot(k), j],
            refs.right_send.at[k, j],
            refs.right_recv.at[k, j],
            right_dev,
        )

    def left_copy(k, j):
        return send(
            w.at[where(k), part, j, core],
            left_buf.at[slot(k), j],
            refs.left_send.at[k, j],
            refs.left_recv.at[k, j],
            left_dev,
        )

    def add_to(k, j, buffer):
        both = w[where(k), part, j, core].astype(F32) + buffer[slot(k), j].astype(F32)
        w[where(k), part, j, core] = both.astype(BF)

    def spend(k, credit):
        @pl.when(k >= slots)
        def _():
            pl.semaphore_wait(credit, 1)

    def grant(k, credit, device):
        @pl.when(k + slots < TILES)
        def _():
            signal(credit, device)

    def right_step(k):
        @pl.when(z < ends)
        def _():
            spend(k, refs.right_credit)

        for j in range(ends, -1, -1):

            @pl.when(jnp.logical_and(z > 0, j >= z))
            def _():
                right_copy(k, j).wait_recv()

            @pl.when(jnp.logical_and(z > 0, j > z))
            def _():
                add_to(k, j, right_buf)

            @pl.when(j > z)
            def _():
                right_copy(k, j).start()

    def left_step(k):
        @pl.when(z > 0)
        def _():
            spend(k, refs.left_credit)

        for j in range(nz):

            @pl.when(jnp.logical_and(z < ends, j <= z))
            def _():
                left_copy(k, j).wait_recv()

            @pl.when(jnp.logical_and(z < ends, j < z))
            def _():
                add_to(k, j, left_buf)

            @pl.when(j < z)
            def _():
                left_copy(k, j).start()

    def grads_copy(k):
        return pltpu.make_async_copy(refs.grad_stage, refs.grads_out.at[k], refs.out_sem.at[0])

    def act_copy(turn):
        return pltpu.make_async_copy(refs.act_stage, refs.act_out.at[turn], refs.out_sem.at[1])

    def close_step(k):
        base = w[where(k), part, z, core].astype(F32)

        @pl.when(k > 0)
        def _():
            grads_copy(k - 1).wait()

        @pl.when(z == 0)
        def _():
            refs.grad_stage[...] = base + left_buf[slot(k), z].astype(F32)

        @pl.when(z == ends)
        def _():
            refs.grad_stage[...] = base + right_buf[slot(k), z].astype(F32)

        @pl.when(jnp.logical_and(z > 0, z < ends))
        def _():
            sides = left_buf[slot(k), z].astype(F32) + right_buf[slot(k), z].astype(F32)
            refs.grad_stage[...] = base + sides

        grads_copy(k).start()

        @pl.when(z > 0)
        def _():
            grant(k, refs.right_credit, left_dev)

        @pl.when(z < ends)
        def _():
            grant(k, refs.left_credit, right_dev)

    def flat(value):
        return value.reshape(tokens, width)

    def store(k, value):
        w[where(k)] = value.astype(BF).reshape(2, nz, 2, rows, width)

    def products(t):
        @pl.when(t < 4)
        def _():
            store(t, mul_tn(flat(refs.hf_s[...]), flat(refs.slope[:, t])))

        for j in range(3):

            @pl.when(t == 4 + j)
            def _():
                store(t, mul_tn(flat(refs.h_s[...]), flat(refs.qkv[:, :, j * width : (j + 1) * width])))

        @pl.when(t == 7)
        def _():
            store(t, mul_tn(flat(refs.o_s[...]), flat(refs.y1[...])))

        @pl.when(jnp.logical_and(t >= 4, t < 8))
        def _():
            value = mul_tn(flat(refs.gate[:, t - 4]), flat(refs.ybuf[...])).astype(BF)
            value = value.reshape(2, 2, 4, rows, width)
            for block in range(4):
                w[8 + block, :, t - 4] = value[:, :, block]

    def inside(k):
        return jnp.logical_and(k >= 0, k < TILES)

    def core_sums():
        return send(
            gsum.at[pl.ds(0, count)], refs.sums_buf, refs.sums_sem.at[0], refs.sums_sem.at[1], c_dev
        )

    def x_sums():
        return [
            send(refs.adds.at[0], refs.adds_buf.at[0], refs.adds_send.at[0], refs.adds_recv.at[0], x_dev),
            send(
                gsum.at[pl.ds(count, own)],
                refs.stamp_buf,
                refs.stamp_send.at[0],
                refs.stamp_recv.at[0],
                x_dev,
            ),
        ]

    def block(bit, place_core, place_z):
        size = own * 2**bit
        first = place_core * nz * own + lax.div(place_z, 2**bit) * size
        return pl.ds(pl.multiple_of(first, 8), size)

    def z_sums(bit, arriving):
        there = flipped(z, bit)
        place = refs.stamps.at[block(bit, core, there if arriving else z)]
        device = (s, flipped(d, 1 + bit))
        return [
            send(
                refs.adds.at[1 + bit],
                refs.adds_buf.at[1 + bit],
                refs.adds_send.at[1 + bit],
                refs.adds_recv.at[1 + bit],
                device,
            ),
            send(place, place, refs.stamp_send.at[1 + bit], refs.stamp_recv.at[1 + bit], device),
        ]

    def last_sums(arriving):
        side = 1 - core if arriving else core
        place = refs.stamps.at[block(zbits, side, z)]
        half_sums = refs.whole.at[side]
        return [
            send(half_sums, half_sums, refs.sums_sem.at[2], refs.sums_sem.at[3], c_dev),
            send(place, place, refs.stamp_send.at[1 + zbits], refs.stamp_recv.at[1 + zbits], c_dev),
        ]

    def final_copies():
        return [
            send(src, dst, refs.final_send.at[index], refs.final_recv.at[index], y_dev)
            for index, (src, dst) in enumerate(((refs.whole, refs.token_out), (refs.stamps, refs.stamp_out)))
        ]

    def arrive(copies):
        for copy in copies:
            copy.wait_recv()

    def begin(copies):
        for copy in copies:
            copy.start()

    def small_step(t):
        @pl.when(t == 2)
        def _():
            core_sums().start()

        @pl.when(t == 4)
        def _():
            core_sums().wait_recv()
            sums = gsum[:count, :width] + refs.sums_buf[:, :width]

            @pl.when(core == 0)
            def _():
                refs.adds[0] = sums[:split]

            @pl.when(core == 1)
            def _():
                refs.adds[0] = sums[split:]

            begin(x_sums())

        @pl.when(t == 6)
        def _():
            arrive(x_sums())
            refs.adds[1] = refs.adds[0] + refs.adds_buf[0]
            refs.stamps[block(0, core, z), :] = gsum[count:, :] + refs.stamp_buf[...]
            begin(z_sums(0, False))

        for bit in range(zbits):

            @pl.when(t == 8 + 2 * bit)
            def _():
                arrive(z_sums(bit, True))
                total = refs.adds[1 + bit] + refs.adds_buf[1 + bit]
                if bit + 1 < zbits:
                    refs.adds[2 + bit] = total
                    begin(z_sums(bit + 1, False))
                else:
                    refs.whole[core] = total
                    begin(last_sums(False))

        @pl.when(t == 8 + 2 * zbits)
        def _():
            arrive(last_sums(True))
            refs.small_out[...] = refs.whole[...]

            @pl.when(stage == 0)
            def _():
                begin(final_copies())
                refs.token_out[...] = refs.whole[...]
                refs.stamp_out[...] = refs.stamps[...]

    def act_step(t):
        turn = t - 3

        @pl.when(jnp.logical_and(turn >= 0, turn < 2 * seqs))
        def _():
            side = lax.div(turn, seqs)
            i = lax.rem(turn, seqs)
            ours = jnp.logical_and(stage == 1, side == part)

            @pl.when(jnp.logical_not(ours))
            def _():
                act_arrival(side, i).wait_recv()

            @pl.when(jnp.logical_and(ours, i >= 2))
            def _():
                act_own(i).wait()

            @pl.when(turn > 0)
            def _():
                act_copy(turn - 1).wait()

            refs.act_stage[...] = refs.landed[side, i].astype(F32).T
            act_copy(turn).start()

    def step(t):
        @pl.when(t == 0)
        def _():
            settle_weights()

        products(t)

        @pl.when(t < TILES)
        def _():
            spend(t, refs.core_credit)
            core_copy(t).start()

        k1 = t - 1

        @pl.when(inside(k1))
        def _():
            core_copy(k1).wait_recv()
            for side in range(2):
                both = w[where(k1), side, :, core].astype(F32) + core_buf[slot(k1), side].astype(F32)
                w[where(k1), side, :, core] = both.astype(BF)
            grant(k1, refs.core_credit, c_dev)
            spend(k1, refs.x_credit)
            x_copy(k1).start()

        small_step(t)
        act_step(t)
        k2 = t - 2

        @pl.when(inside(k2))
        def _():
            x_copy(k2).wait_recv()
            both = w[where(k2), part, :, core].astype(F32) + x_buf[slot(k2)].astype(F32)
            w[where(k2), part, :, core] = both.astype(BF)
            grant(k2, refs.x_credit, x_dev)

        k3 = t - 2 - z

        @pl.when(inside(k3))
        def _():
            right_step(k3)

        k4 = t - 2 - (ends - z)

        @pl.when(inside(k4))
        def _():
            left_step(k4)

        k5 = jnp.minimum(k3, k4)

        @pl.when(inside(k5))
        def _():
            close_step(k5)

        @pl.when(t == TILES + 1 + ends)
        def _():
            finish()

    def finish():
        def settle(k, _):
            core_copy(k).wait_send()
            x_copy(k).wait_send()
            for j in range(nz):

                @pl.when(j > z)
                def _():
                    right_copy(k, j).wait_send()

                @pl.when(j < z)
                def _():
                    left_copy(k, j).wait_send()

            return 0

        lax.fori_loop(0, TILES, settle, 0)
        grads_copy(TILES - 1).wait()
        act_copy(2 * seqs - 1).wait()
        sends = [core_sums()] + x_sums() + last_sums(False)
        for bit in range(zbits):
            sends += z_sums(bit, False)
        for copy in sends:
            copy.wait_send()

        @pl.when(stage == 0)
        def _():
            for copy in final_copies():
                copy.wait_send()

        @pl.when(stage == 1)
        def _():
            arrive(final_copies())

    return step


def run_layers(weights, singles, ids, table, times, cot, replicas, fused):
    rows, length = ids.shape
    width = cot.shape[2]
    half = width // 2
    seqs = rows // 2
    tokens = seqs * length
    padded = -(-table.shape[0] // 16) * 16
    count = 16 + padded
    nz = replicas // 2
    lane = width + 128
    cut = half // 8
    slots = 3
    dma = pltpu.SemaphoreType.DMA
    credit = pltpu.SemaphoreType.REGULAR
    anywhere = pl.BlockSpec(memory_space=pl.ANY)
    local = pl.BlockSpec(memory_space=pltpu.VMEM)
    vm = pltpu.VMEM
    shape = jax.ShapeDtypeStruct
    if fused:
        outs = {
            "act_out": (shape((2 * seqs, width // 4, length), F32), anywhere),
            "grads_out": (shape((TILES, cut, width), F32), anywhere),
            "small_out": (shape((2, count // 2, width), F32), local),
            "token_out": (shape((2, count // 2, width), F32), local),
            "stamp_out": (shape((rows * replicas, lane), F32), local),
        }
    else:
        outs = {
            "act_out": (shape((2, seqs, length, width // 4), BF), anywhere),
            "sums_out": (shape((count + rows, lane), F32), local),
            "fixed_out": (shape((4, tokens, width), BF), anywhere),
            "moving_out": (shape((12, tokens, width), BF), anywhere),
        }
    scratch = {
        "w": vm((TILES, 2, 4, 2, cut, width), BF),
        "vecs": vm((2, 16, half), F32),
        "table": vm((padded, width), BF),
        "par": vm((16, width), F32),
        "xs": vm((length, width), F32),
        "acc": vm((length, width), F32),
        "n_a": vm((seqs, length, width), BF),
        "n_f": vm((seqs, length, width), BF),
        "r_a": vm((seqs, length, 128), F32),
        "r_f": vm((seqs, length, 128), F32),
        "qkv": vm((seqs, length, 3 * width), BF),
        "probs": vm((seqs, HEADS, length, length), BF),
        "y1": vm((seqs, length, width), BF),
        "slope": vm((seqs, 4, length, width), BF),
        "gate": vm((seqs, 4, length, width), BF),
        "h_s": vm((seqs, length, width), BF),
        "o_s": vm((seqs, length, width), BF),
        "hf_s": vm((seqs, length, width), BF),
        "go_s": vm((length, width), BF),
        "ybuf": vm((seqs, length, width), BF),
        "ysend": vm((seqs, length, width), BF),
        "act": vm((2, 4, length, width // 4), BF),
        "landed": vm((2, seqs, length, width // 4), BF),
        "gsum": vm((count + rows, lane), F32),
        "own_sem": dma((2 * TILES,)),
        "vec_sem": dma((2,)),
        "cot_sem": dma((seqs,)),
        "y_send": dma((seqs,)),
        "y_recv": dma((seqs,)),
        "act_send": dma((seqs, 4)),
        "act_recv": dma((2, seqs)),
    }
    for name in ("wx", "wz", "c1", "c2"):
        scratch[name + "_send"] = dma((TILES,))
        scratch[name + "_recv"] = dma((TILES,))
    if fused:
        zbits = nz.bit_length() - 1
        scratch |= {
            "core_buf": vm((slots, 2, nz, cut, width), BF),
            "x_buf": vm((slots, nz, cut, width), BF),
            "right_buf": vm((slots, nz, cut, width), BF),
            "left_buf": vm((slots, nz, cut, width), BF),
            "sums_buf": vm((count, lane), F32),
            "adds": vm((1 + zbits, count // 2, width), F32),
            "adds_buf": vm((1 + zbits, count // 2, width), F32),
            "whole": vm((2, count // 2, width), F32),
            "stamp_buf": vm((rows, lane), F32),
            "stamps": vm((rows * replicas, lane), F32),
            "grad_stage": vm((cut, width), F32),
            "act_stage": vm((width // 4, length), F32),
            "out_sem": dma((2,)),
            "sums_sem": dma((4,)),
            "adds_send": dma((1 + zbits,)),
            "adds_recv": dma((1 + zbits,)),
            "stamp_send": dma((2 + zbits,)),
            "stamp_recv": dma((2 + zbits,)),
            "final_send": dma((2,)),
            "final_recv": dma((2,)),
            "core_credit": credit,
            "x_credit": credit,
            "right_credit": credit,
            "left_credit": credit,
        }
        for name in ("core", "x"):
            scratch[name + "_send"] = dma((TILES,))
            scratch[name + "_recv"] = dma((TILES,))
        for name in ("right", "left"):
            scratch[name + "_send"] = dma((TILES, nz))
            scratch[name + "_recv"] = dma((TILES, nz))
    else:
        scratch["keep_sem"] = dma((16 * seqs + 1,))
    names = INPUTS + list(outs) + list(scratch)
    return pl.pallas_call(
        functools.partial(layer_kernel, seqs, length, width, fused, names),
        out_shape=tuple(out[0] for out in outs.values()),
        in_specs=[anywhere] * 4 + [local] * 12 + [anywhere],
        out_specs=tuple(out[1] for out in outs.values()),
        scratch_shapes=list(scratch.values()),
        compiler_params=pltpu.CompilerParams(
            collective_id=0, has_side_effects=True, vmem_limit_bytes=64 * 2**20 - 2**17
        ),
    )(*weights, *singles, ids, table, times, cot)


def three_parts(value):
    first = value.astype(BF)
    rest = value - first.astype(F32)
    second = rest.astype(BF)
    return first, second, (rest - second.astype(F32)).astype(BF)


def finish_kernel(
    act,
    grads,
    small,
    token,
    stamp,
    act_out,
    token_out,
    time_out,
    ga_out,
    sa_out,
    qkv_out,
    bq_out,
    bv_out,
    proj_out,
    bo_out,
    gm_out,
    sm_out,
    up_out,
    bup_out,
    down_out,
    bdown_out,
    sem,
):
    s = lax.axis_index("section")
    d = lax.axis_index("dp")
    part = lax.rem(s, 2)
    rows, width = grads.shape[1:]
    half = width // 2
    quarter = width // 4
    pairs = [(act, act_out)]
    for j in range(4):
        for side in range(2):
            first = side * 4 * half + j * half
            pairs.append((grads.at[j, :, pl.ds(side * half, half)], up_out.at[0, :, pl.ds(first, half)]))
    for j in range(3):
        pairs.append((grads.at[4 + j], qkv_out.at[0, :, pl.ds(j * width, width)]))
    pairs.append((grads.at[7], proj_out.at[0]))
    for j in range(4):
        pairs.append((grads.at[8 + j], down_out.at[0, pl.ds(j * rows, rows)]))
    copies = [pltpu.make_async_copy(src, dst, sem.at[index]) for index, (src, dst) in enumerate(pairs)]
    for copy in copies:
        copy.start()
    vectors = small[0, :16, :]
    lower = jnp.where(part == 0, vectors[:, :half], vectors[:, half:])
    turned = pltpu.roll(lower, lax.rem(half - d * rows, half), 1)
    outs = (ga_out, sa_out, bq_out, bv_out, bo_out, gm_out, sm_out, bdown_out)
    for index, out in enumerate(outs):
        out[...] = turned[index : index + 1, :rows]
    per_row = half // (4 * rows)
    shifted = pltpu.roll(lower, lax.rem(half - lax.rem(d, per_row) * 4 * rows, half), 1)
    for j in range(4):

        @pl.when(lax.div(d, per_row) == j)
        def _():
            bup_out[...] = shifted[8 + j : 9 + j, : 4 * rows]

    times_count = time_out.shape[1]
    spread = -(-times_count // 128) * 128
    place = lax.broadcasted_iota(jnp.int32, (stamp.shape[0], spread), 1).astype(F32)
    hot = (place == stamp[:, width : width + 1]).astype(F32).astype(BF)
    letters = token_out.shape[0]
    split = token.shape[1]
    for q in range(4):

        @pl.when(s == q)
        def _():
            at = slice(q * quarter, (q + 1) * quarter)
            token_out[: split - 16, :] = token[0, 16:, at]
            token_out[split - 16 :, :] = token[1, : letters + 16 - split, at]
            sums = jnp.zeros((quarter, spread), F32)
            for piece in three_parts(stamp[:, at]):
                sums = sums + mul_tn(piece, hot)
            time_out[...] = sums[:, :times_count]

    for copy in copies:
        copy.wait()


def run_finish(act, grads, small, token, stamp, letters_count, times_count):
    rows, width = grads.shape[1:]
    quarter = width // 4
    local = pl.BlockSpec(memory_space=pltpu.VMEM)
    anywhere = pl.BlockSpec(memory_space=pl.ANY)
    single = (1, rows)
    shapes = [
        (act.shape, anywhere),
        ((letters_count, quarter), local),
        ((quarter, times_count), local),
        (single, local),
        (single, local),
        ((1, rows, 3 * width), anywhere),
        (single, local),
        (single, local),
        ((1, rows, width), anywhere),
        (single, local),
        (single, local),
        (single, local),
        ((1, rows, 4 * width), anywhere),
        ((1, 4 * rows), local),
        ((1, 4 * rows, width), anywhere),
        (single, local),
    ]
    outs = pl.pallas_call(
        finish_kernel,
        out_shape=tuple(jax.ShapeDtypeStruct(shape, F32) for shape, _ in shapes),
        in_specs=[anywhere] * 2 + [local] * 3,
        out_specs=tuple(spec for _, spec in shapes),
        scratch_shapes=[pltpu.SemaphoreType.DMA((17,))],
        compiler_params=pltpu.CompilerParams(vmem_limit_bytes=32 * 2**20),
    )(act, grads, small, token, stamp)
    return (jnp.swapaxes(outs[0], 1, 2), outs[1], jnp.swapaxes(outs[2], 0, 1)) + tuple(outs[3:])


def plain_reduce(fixed, moving, lower):
    def grad(left, right):
        return jnp.einsum("tk,tn->kn", left, right, preferred_element_type=F32)

    width = fixed.shape[2]
    half = width // 2
    hf, h, o, gz = (fixed[index] for index in range(4))
    ups = jnp.stack([grad(hf, moving[j]) for j in range(4)])
    up = ups.reshape(4, width, 2, half).transpose(1, 2, 0, 3).reshape(width, 4 * width)
    joint = jnp.concatenate([grad(h, moving[4 + j]) for j in range(3)], axis=1)
    proj = grad(o, moving[7])
    downs = jnp.stack([grad(moving[8 + j], gz) for j in range(4)])
    down = downs.reshape(4, 2, half, width).transpose(1, 0, 2, 3).reshape(4 * width, width)
    results = []
    for total in (joint, proj, up, down):
        halves = total.reshape((2, total.shape[0] // 2) + total.shape[1:])
        summed = lax.psum_scatter(halves, "dp", scatter_dimension=1, tiled=True)
        ours = jnp.where(lower, summed[0], summed[1])
        theirs = jnp.where(lower, summed[1], summed[0]).astype(BF)
        pairs = [(i, i ^ 1) for i in range(lax.axis_size("section"))]
        results.append((ours + lax.ppermute(theirs, "section", pairs).astype(F32))[None])
    return results


def per_device(
    token_ids,
    timesteps,
    token_table,
    time_table,
    attn_gain,
    attn_shift,
    qkv_weight,
    query_bias,
    value_bias,
    proj_weight,
    proj_bias,
    mlp_gain,
    mlp_shift,
    up_weight,
    up_bias,
    down_weight,
    down_bias,
    cotangent,
):
    section = lax.axis_index("section")
    replica = lax.axis_index("dp")
    replicas = lax.axis_size("dp")
    rows, length = token_ids.shape
    width = cotangent.shape[2]
    half = width // 2
    layer = section // 2
    part = section % 2
    letters_count = token_table.shape[0]
    times_count = time_table.shape[0]
    padded = -(-letters_count // 16) * 16
    singles = (
        attn_gain,
        attn_shift,
        query_bias,
        value_bias,
        proj_bias,
        mlp_gain,
        mlp_shift,
        down_bias,
        up_bias,
    )
    marks = jnp.broadcast_to(timesteps.astype(F32)[:, None], (rows, 128))
    times = time_table.at[timesteps].get(mode="promise_in_bounds").astype(F32)
    times = jnp.concatenate([times, marks], axis=1)
    cut = half // 8
    weights = (
        qkv_weight.reshape(4, 2, cut, 3 * width),
        proj_weight.reshape(4, 2, cut, width),
        up_weight.reshape(4, 2, cut, 4 * width),
        down_weight.reshape(4, 4, 2, cut, width),
    )
    vectors = 16
    fused = replicas == 8
    layers = run_layers(weights, singles, token_ids, token_table, times, cotangent, replicas, fused)
    if fused:
        return run_finish(*layers, letters_count, times_count)
    act, sums, fixed, moving = layers
    qkv_grad, proj_grad, up_grad, down_grad = plain_reduce(fixed, moving, part == 0)
    activations = act.reshape(rows, length, width // 4).astype(F32)
    mine = jnp.zeros((2, vectors, width + 128), F32)
    mine = lax.dynamic_update_slice_in_dim(mine, sums[None, :vectors], layer, 0)
    placed = jnp.zeros((rows * replicas, width + 128), F32)
    placed = lax.dynamic_update_slice_in_dim(placed, sums[vectors + padded :], replica * rows, 0)
    joined = jnp.concatenate(
        [sums[vectors : vectors + padded], mine.reshape(2 * vectors, width + 128), placed], axis=0
    )
    joined = lax.psum(joined, ("section", "dp"))
    quarter = width // 4
    columns = lax.dynamic_slice_in_dim(joined, section * quarter, quarter, axis=1)
    token_grad = columns[:letters_count]
    first = padded + 2 * vectors
    steps = jnp.arange(times_count, dtype=jnp.int32).astype(F32)
    hot = (steps[:, None] == joined[first:, width][None, :]).astype(F32)
    time_grad = jnp.einsum("tb,bd->td", hot, columns[first:], precision=HIGHEST)
    ours = lax.dynamic_slice(joined, (padded + vectors * layer, part * half), (vectors, half))
    each = half // replicas
    flat = lax.dynamic_slice_in_dim(ours[:8], replica * each, each, axis=1)
    ups = lax.dynamic_slice_in_dim(ours[8:12].reshape(1, 4 * half), replica * 4 * each, 4 * each, axis=1)
    return (
        activations,
        token_grad,
        time_grad,
        flat[0:1],
        flat[1:2],
        qkv_grad,
        flat[2:3],
        flat[3:4],
        proj_grad,
        flat[4:5],
        flat[5:6],
        flat[6:7],
        up_grad,
        ups,
        down_grad,
        flat[7:8],
    )


def solution(mesh):
    return jax.shard_map(
        per_device,
        mesh=mesh,
        in_specs=(
            P("dp", None),
            P("dp"),
            P(),
            P(),
            P("section", None),
            P("section", None),
            P("section", None, None),
            P("section", None),
            P("section", None),
            P("section", None, None),
            P("section", None),
            P("section", None),
            P("section", None),
            P("section", None, None),
            P("section", None),
            P("section", None, None),
            P("section", None),
            P("dp", None, None),
        ),
        out_specs=(
            P("dp", None, "section"),
            P(None, "section"),
            P(None, "section"),
            P("section", "dp"),
            P("section", "dp"),
            P("section", "dp", None),
            P("section", "dp"),
            P("section", "dp"),
            P("section", "dp", None),
            P("section", "dp"),
            P("section", "dp"),
            P("section", "dp"),
            P("section", "dp", None),
            P("section", "dp"),
            P("section", "dp", None),
            P("section", "dp"),
        ),
        check_vma=False,
    )
```

time: 369 us -> 252 us (0.68)
  Pallas kernels: 297 us -> 242 us
  waiting for transfers between devices: 17 us -> 0 us
  between operations: 14.9 us -> 0.68 us
  local copies, waits for them, and re-layouts: 19.6 us -> 7.87 us
  blocking collectives: 6.47 us -> 0 us
  other arithmetic: 7.11 us -> 1.36 us
  starting transfers between devices: 4.06 us -> 0 us
    pallas_call x2, Pallas kernels: 297 us -> 242 us  [the longest x1 239 us: run_layers(): pl.pallas_call(functools.partial(layer_kernel, seqs, length, width, fused...]
    psum x1 -> x0, waiting for transfers between devices: 16.9 us -> none  [per_device(): joined = lax.psum(joined, ('section', 'dp'))]
    unnamed x1 -> x0, blocking collectives: 6.47 us -> none
    ppermute x3 -> x0, starting transfers between devices: 4.03 us -> none  [the longest x1 1.45 us: spread_activations(): beside = lax.ppermute(piece(3 - part), 'section', [(2, 3), (3, 2)])]
    unnamed x26 -> x10, local copies, waits for them, and re-layouts: 7.56 us -> 5.63 us
  transfers between devices with their start and end apart: 4 -> 0, of which waited for: 1 -> 0; matrix products, arithmetic and copies ran while one was open for 3% -> 0% of each run, Pallas kernels for 27% -> 0%
where the time goes in v3:
time: 252 us
  Pallas kernels  242 us (96%)
  local copies, waits for them, and re-layouts  7.87 us (3%)
    pallas_call x1, Pallas kernels, run_layers(): pl.pallas_call(functools.partial(layer_kernel, seqs, length, width, fused...  239 us
    unnamed x10, local copies, waits for them, and re-layouts  5.63 us

profile of v3, /device:TPU:0, one launch (start us, length us, event | category | flops | bytes accessed | tf_op | source)
XLA Modules:
  0.0 252.1 jit_solution(16710941290390470172)
XLA Ops:
  0.6 0.7 compare_select_fusion
  1.4 0.1 broadcast_in_dim.10
  1.5 2.2 gather_fusion
  3.6 0.6 pad_maximum_fusion.all_refs_15_
  4.3 239.5 %shard_map.297 = (f32[8,192,256]{2,1,0:T(8,128)}, f32[12,48,768]{2,1,0:T(8,128)}, f32[2,24,768]{2,1,0:T(8,128)}, f32[2,24,768]{2,1,0:T(8,128)}, f32[64,896]{1,0:T(8,128)}) custom-call(bf16[4,2,48,2304]{3,2,1,0:T(8,128)(2,1)} %bitcast.8, bf16[4,2,48,768]{3,2,1,0:T(8,128)(2,1)} %bitcast.9, bf16[4,2,48,3072]{3,2,1,0:T(8,128)(2,1)} %bitcast.6, ...), custom_call_target="tpu_custom_call" | custom-call | tf_op jit(solution)/shard_map/pallas_call | solution.py:1081
  243.7 0.0 copy-start
  243.7 1.5 copy-done
  245.2 0.0 copy-start.1
  245.2 1.4 copy-done.1
  246.6 0.0 copy-start.2
  246.6 0.9 copy-done.2
  247.6 0.0 copy-start.3
  247.6 0.9 copy-done.3
  248.5 0.0 copy-start.4
  248.5 0.9 copy-done.4
  249.4 2.8 %shard_map.298 = (f32[8,192,256]{2,1,0:T(8,128)}, f32[27,192]{1,0:T(8,128)}, f32[192,1000]{1,0:T(8,128)}, f32[1,48]{1,0:T(1,128)}, f32[1,48]{1,0:T(1,128)}, /*in...) custom-call(f32[8,192,256]{2,1,0:T(8,128)S(1)} %copy-done.1, ...), custom_call_target="tpu_custom_call" | custom-call | tf_op jit(solution)/shard_map/pallas_call | solution.py:1203
  (2 shorter events, 0.0 us)
Async XLA Ops:
  243.7 1.5 copy-start
  245.2 1.4 copy-start.1
  246.6 0.9 copy-start.2
  247.6 0.9 copy-start.3
  248.5 0.9 copy-start.4

commit v4 on v3

--- a/solution.py
+++ b/solution.py
@@ -16,6 +16,9 @@
 F32 = jnp.float32
 TILES = 12
 QKV, PROJ, UP, DOWN = 0, 3, 4, 8
+CHUNKS = 2 * TILES
+LINE_FIRST = (1, 4, 7, 11)
+CORE_LAG, X_LAG, Z_LAG, LINE_START, LINE_LAST = 2, 6, 2, 3, 28
 GELU_A = math.sqrt(2.0 / math.pi)
 GELU_B = 0.044715
 
@@ -472,7 +475,7 @@
     if fused:
         step = reduce_steps(refs, seqs, length, width, send, signal, act_arrival, act_own, settle_weights)
         units = units + (step,)
-        steps = TILES + 2 + ends
+        steps = CHUNKS + X_LAG + Z_LAG * ends
 
     def unit(u, _):
         early = u < 2 * seqs
@@ -482,7 +485,7 @@
         index1 = lax.div(u, 4)
         if fused:
             last = 4 * seqs - 1
-            ahead = 2
+            ahead = 4
             kind0 = jnp.where(u >= last, 4, kind0)
             index0 = jnp.where(u >= last, jnp.where(u < last + ahead, u - last, u - last - 1), index0)
             kind0 = jnp.where(u == last + ahead, 3, kind0)
@@ -578,6 +581,9 @@
     rows = w.shape[4]
     ends = nz - 1
     slots = refs.x_buf.shape[0]
+    core_slots = refs.core_buf.shape[0]
+    directs = CHUNKS - len(LINE_FIRST)
+    half = width // 2
     tokens = seqs * length
     core_buf, x_buf, right_buf, left_buf = refs.core_buf, refs.x_buf, refs.right_buf, refs.left_buf
     vectors = 16
@@ -586,95 +592,165 @@
     zbits = nz.bit_length() - 1
     own = gsum.shape[0] - count
 
-    def where(k):
-        return jnp.where(k < 4, k + 4, jnp.where(k < 8, k - 4, k))
+    def where(tile):
+        return jnp.where(tile < 4, tile + 4, jnp.where(tile < 8, tile - 4, tile))
+
+    def at(k, *index):
+        columns = pl.ds(pl.multiple_of(lax.rem(k, 2) * half, 128), half)
+        return (where(lax.div(k, 2)),) + index + (slice(None), columns)
+
+    everything = slice(None)
+
+    def turned(k):
+        return functools.reduce(jnp.logical_or, [k == chunk for chunk in LINE_FIRST])
+
+    def direct(k):
+        return jnp.logical_and(jnp.logical_and(k >= 0, k < CHUNKS), jnp.logical_not(turned(k)))
+
+    def order(k):
+        return k - sum((k > chunk).astype(jnp.int32) for chunk in LINE_FIRST)
 
     def slot(k):
-        return lax.rem(k, slots)
+        return lax.rem(order(k), slots)
+
+    def core_slot(k):
+        return lax.rem(k, core_slots)
 
     def core_copy(k):
         return send(
-            w.at[where(k), :, :, 1 - core],
-            core_buf.at[slot(k)],
-            refs.core_send.at[k],
-            refs.core_recv.at[k],
+            w.at[at(k, everything, everything, 1 - core)],
+            core_buf.at[core_slot(k)],
+            refs.core_send.at[core_slot(k)],
+            refs.core_recv.at[core_slot(k)],
             c_dev,
         )
 
     def x_copy(k):
         return send(
-            w.at[where(k), other, :, core], x_buf.at[slot(k)], refs.x_send.at[k], refs.x_recv.at[k], x_dev
+            w.at[at(k, other, everything, core)],
+            x_buf.at[slot(k)],
+            refs.x_send.at[slot(k)],
+            refs.x_recv.at[slot(k)],
+            x_dev,
         )
 
-    def right_copy(k, j):
-        return send(
-            w.at[where(k), part, j, core],
-            right_buf.at[slot(k), j],
-            refs.right_send.at[k, j],
-            refs.right_recv.at[k, j],
-            right_dev,
-        )
-
-    def left_copy(k, j):
-        return send(
-            w.at[where(k), part, j, core],
-            left_buf.at[slot(k), j],
-            refs.left_send.at[k, j],
-            refs.left_recv.at[k, j],
-            left_dev,
-        )
-
-    def add_to(k, j, buffer):
-        both = w[where(k), part, j, core].astype(F32) + buffer[slot(k), j].astype(F32)
-        w[where(k), part, j, core] = both.astype(BF)
-
-    def spend(k, credit):
-        @pl.when(k >= slots)
-        def _():
-            pl.semaphore_wait(credit, 1)
-
-    def grant(k, credit, device):
-        @pl.when(k + slots < TILES)
-        def _():
-            signal(credit, device)
-
-    def right_step(k):
-        @pl.when(z < ends)
-        def _():
-            spend(k, refs.right_credit)
-
-        for j in range(ends, -1, -1):
-
-            @pl.when(jnp.logical_and(z > 0, j >= z))
-            def _():
-                right_copy(k, j).wait_recv()
-
-            @pl.when(jnp.logical_and(z > 0, j > z))
-            def _():
-                add_to(k, j, right_buf)
-
-            @pl.when(j > z)
-            def _():
-                right_copy(k, j).start()
-
-    def left_step(k):
-        @pl.when(z > 0)
-        def _():
-            spend(k, refs.left_credit)
-
-        for j in range(nz):
-
-            @pl.when(jnp.logical_and(z < ends, j <= z))
-            def _():
-                left_copy(k, j).wait_recv()
-
-            @pl.when(jnp.logical_and(z < ends, j < z))
-            def _():
-                add_to(k, j, left_buf)
-
-            @pl.when(j < z)
-            def _():
-                left_copy(k, j).start()
+    class Line:
+        def __init__(self, name, slot, side, spend_from, grant_to):
+            self.right_buf = getattr(refs, name + "right_buf")
+            self.left_buf = getattr(refs, name + "left_buf")
+            self.right_sems = getattr(refs, name + "right_send"), getattr(refs, name + "right_recv")
+            self.left_sems = getattr(refs, name + "left_send"), getattr(refs, name + "left_recv")
+            self.right_credit = getattr(refs, name + "right_credit")
+            self.left_credit = getattr(refs, name + "left_credit")
+            self.slots = self.right_buf.shape[0]
+            self.slot = lambda job: lax.rem(slot(job), self.slots)
+            self.side = side
+            self.spend_from = spend_from
+            self.grant_to = grant_to
+
+        def place(self, job, j):
+            k, side = self.side(job)
+            return at(k, side, j, core)
+
+        def right_copy(self, job, j):
+            sends, recvs = self.right_sems
+            slot = self.slot(job)
+            target = self.right_buf.at[slot, j]
+            return send(w.at[self.place(job, j)], target, sends.at[slot, j], recvs.at[slot, j], right_dev)
+
+        def left_copy(self, job, j):
+            sends, recvs = self.left_sems
+            slot = self.slot(job)
+            target = self.left_buf.at[slot, j]
+            return send(w.at[self.place(job, j)], target, sends.at[slot, j], recvs.at[slot, j], left_dev)
+
+        def add(self, job, j, buffer):
+            both = w[self.place(job, j)].astype(F32) + buffer[self.slot(job), j].astype(F32)
+            w[self.place(job, j)] = both.astype(BF)
+
+        def right_step(self, job):
+            @pl.when(jnp.logical_and(z < ends, self.spend_from(job)))
+            def _():
+                pl.semaphore_wait(self.right_credit, 1)
+
+            for j in range(ends, -1, -1):
+
+                @pl.when(jnp.logical_and(z > 0, j >= z))
+                def _():
+                    self.right_copy(job, j).wait_recv()
+                    self.add(job, j, self.right_buf)
+
+                @pl.when(jnp.logical_and(j > z, self.spend_from(job)))
+                def _():
+                    self.right_copy(job, j).wait_send()
+
+                @pl.when(j > z)
+                def _():
+                    self.right_copy(job, j).start()
+
+            @pl.when(jnp.logical_and(z > 0, self.grant_to(job)))
+            def _():
+                signal(self.right_credit, left_dev)
+
+        def left_step(self, job):
+            @pl.when(jnp.logical_and(z > 0, self.spend_from(job)))
+            def _():
+                pl.semaphore_wait(self.left_credit, 1)
+
+            for j in range(nz):
+
+                @pl.when(jnp.logical_and(z < ends, j <= z))
+                def _():
+                    self.left_copy(job, j).wait_recv()
+                    self.add(job, j, self.left_buf)
+
+                @pl.when(jnp.logical_and(j < z, self.spend_from(job)))
+                def _():
+                    self.left_copy(job, j).wait_send()
+
+                @pl.when(j < z)
+                def _():
+                    self.left_copy(job, j).start()
+
+            @pl.when(jnp.logical_and(z < ends, self.grant_to(job)))
+            def _():
+                signal(self.left_credit, right_dev)
+
+        def settle(self, job):
+            for j in range(nz):
+
+                @pl.when(j > z)
+                def _():
+                    self.right_copy(job, j).wait_send()
+
+                @pl.when(j < z)
+                def _():
+                    self.left_copy(job, j).wait_send()
+
+    line_slots = refs.right_buf.shape[0]
+    main = Line(
+        "",
+        order,
+        lambda k: (k, part),
+        lambda k: order(k) >= line_slots,
+        lambda k: order(k) + line_slots < directs,
+    )
+    side_jobs = 2 * len(LINE_FIRST)
+    side_slots = refs.b_right_buf.shape[0]
+
+    def side_place(job):
+        chunk = jnp.int32(LINE_FIRST[-1])
+        for index in range(len(LINE_FIRST) - 1, -1, -1):
+            chunk = jnp.where(job < 2 * (index + 1), LINE_FIRST[index], chunk)
+        return chunk, lax.rem(job, 2)
+
+    beside = Line(
+        "b_",
+        lambda job: job,
+        side_place,
+        lambda job: job >= side_slots,
+        lambda job: job + side_slots < side_jobs,
+    )
 
     def grads_copy(k):
         return pltpu.make_async_copy(refs.grad_stage, refs.grads_out.at[k], refs.out_sem.at[0])
@@ -682,35 +758,28 @@
     def act_copy(turn):
         return pltpu.make_async_copy(refs.act_stage, refs.act_out.at[turn], refs.out_sem.at[1])
 
-    def close_step(k):
-        base = w[where(k), part, z, core].astype(F32)
-
+    def put_grads(k, value):
         @pl.when(k > 0)
         def _():
-            grads_copy(k - 1).wait()
-
-        @pl.when(z == 0)
-        def _():
-            refs.grad_stage[...] = base + left_buf[slot(k), z].astype(F32)
-
-        @pl.when(z == ends)
-        def _():
-            refs.grad_stage[...] = base + right_buf[slot(k), z].astype(F32)
-
-        @pl.when(jnp.logical_and(z > 0, z < ends))
-        def _():
-            sides = left_buf[slot(k), z].astype(F32) + right_buf[slot(k), z].astype(F32)
-            refs.grad_stage[...] = base + sides
-
+            grads_copy(k).wait()
+
+        refs.grad_stage[...] = value
         grads_copy(k).start()
 
-        @pl.when(z > 0)
-        def _():
-            grant(k, refs.right_credit, left_dev)
-
-        @pl.when(z < ends)
-        def _():
-            grant(k, refs.left_credit, right_dev)
+    def last_copy(index):
+        k = jnp.int32(LINE_FIRST[index])
+        return send(
+            w.at[at(k, other, z, core)],
+            refs.last_buf.at[index],
+            refs.last_send.at[index],
+            refs.last_recv.at[index],
+            x_dev,
+        )
+
+    def put_last(index):
+        k = jnp.int32(LINE_FIRST[index])
+        last_copy(index).wait_recv()
+        put_grads(k, w[at(k, part, z, core)].astype(F32) + refs.last_buf[index].astype(F32))
 
     def flat(value):
         return value.reshape(tokens, width)
@@ -718,30 +787,30 @@
     def store(k, value):
         w[where(k)] = value.astype(BF).reshape(2, nz, 2, rows, width)
 
-    def products(t):
-        @pl.when(t < 4)
-        def _():
-            store(t, mul_tn(flat(refs.hf_s[...]), flat(refs.slope[:, t])))
+    def products(tile):
+        @pl.when(tile < 4)
+        def _():
+            store(tile, mul_tn(flat(refs.hf_s[...]), flat(refs.slope[:, tile])))
 
         for j in range(3):
 
-            @pl.when(t == 4 + j)
-            def _():
-                store(t, mul_tn(flat(refs.h_s[...]), flat(refs.qkv[:, :, j * width : (j + 1) * width])))
-
-        @pl.when(t == 7)
-        def _():
-            store(t, mul_tn(flat(refs.o_s[...]), flat(refs.y1[...])))
-
-        @pl.when(jnp.logical_and(t >= 4, t < 8))
-        def _():
-            value = mul_tn(flat(refs.gate[:, t - 4]), flat(refs.ybuf[...])).astype(BF)
+            @pl.when(tile == 4 + j)
+            def _():
+                store(tile, mul_tn(flat(refs.h_s[...]), flat(refs.qkv[:, :, j * width : (j + 1) * width])))
+
+        @pl.when(tile == 7)
+        def _():
+            store(tile, mul_tn(flat(refs.o_s[...]), flat(refs.y1[...])))
+
+        @pl.when(jnp.logical_and(tile >= 4, tile < 8))
+        def _():
+            value = mul_tn(flat(refs.gate[:, tile - 4]), flat(refs.ybuf[...])).astype(BF)
             value = value.reshape(2, 2, 4, rows, width)
             for block in range(4):
-                w[8 + block, :, t - 4] = value[:, :, block]
+                w[8 + block, :, tile - 4] = value[:, :, block]
 
     def inside(k):
-        return jnp.logical_and(k >= 0, k < TILES)
+        return jnp.logical_and(k >= 0, k < CHUNKS)
 
     def core_sums():
         return send(
@@ -804,11 +873,11 @@
             copy.start()
 
     def small_step(t):
-        @pl.when(t == 2)
+        @pl.when(t == 5)
         def _():
             core_sums().start()
 
-        @pl.when(t == 4)
+        @pl.when(t == 8)
         def _():
             core_sums().wait_recv()
             sums = gsum[:count, :width] + refs.sums_buf[:, :width]
@@ -823,7 +892,7 @@
 
             begin(x_sums())
 
-        @pl.when(t == 6)
+        @pl.when(t == 12)
         def _():
             arrive(x_sums())
             refs.adds[1] = refs.adds[0] + refs.adds_buf[0]
@@ -832,7 +901,7 @@
 
         for bit in range(zbits):
 
-            @pl.when(t == 8 + 2 * bit)
+            @pl.when(t == 16 + 4 * bit)
             def _():
                 arrive(z_sums(bit, True))
                 total = refs.adds[1 + bit] + refs.adds_buf[1 + bit]
@@ -843,7 +912,7 @@
                     refs.whole[core] = total
                     begin(last_sums(False))
 
-        @pl.when(t == 8 + 2 * zbits)
+        @pl.when(t == 16 + 4 * zbits)
         def _():
             arrive(last_sums(True))
             refs.small_out[...] = refs.whole[...]
@@ -855,7 +924,7 @@
                 refs.stamp_out[...] = refs.stamps[...]
 
     def act_step(t):
-        turn = t - 3
+        turn = t - 6
 
         @pl.when(jnp.logical_and(turn >= 0, turn < 2 * seqs))
         def _():
@@ -883,76 +952,123 @@
         def _():
             settle_weights()
 
-        products(t)
-
-        @pl.when(t < TILES)
-        def _():
-            spend(t, refs.core_credit)
+        @pl.when(jnp.logical_and(lax.rem(t, 2) == 0, t < 16))
+        def _():
+            products(lax.div(t, 2))
+
+        @pl.when(t < CHUNKS)
+        def _():
+            @pl.when(t >= core_slots)
+            def _():
+                pl.semaphore_wait(refs.core_credit, 1)
+                core_copy(t).wait_send()
+
             core_copy(t).start()
 
-        k1 = t - 1
+        k1 = t - CORE_LAG
 
         @pl.when(inside(k1))
         def _():
             core_copy(k1).wait_recv()
             for side in range(2):
-                both = w[where(k1), side, :, core].astype(F32) + core_buf[slot(k1), side].astype(F32)
-                w[where(k1), side, :, core] = both.astype(BF)
-            grant(k1, refs.core_credit, c_dev)
-            spend(k1, refs.x_credit)
+                place = at(k1, side, everything, core)
+                both = w[place].astype(F32) + core_buf[core_slot(k1), side].astype(F32)
+                w[place] = both.astype(BF)
+
+            @pl.when(k1 + core_slots < CHUNKS)
+            def _():
+                signal(refs.core_credit, c_dev)
+
+        @pl.when(direct(k1))
+        def _():
+            @pl.when(order(k1) >= slots)
+            def _():
+                pl.semaphore_wait(refs.x_credit, 1)
+                x_copy(k1).wait_send()
+
             x_copy(k1).start()
 
         small_step(t)
         act_step(t)
-        k2 = t - 2
-
-        @pl.when(inside(k2))
+        k2 = t - X_LAG
+
+        @pl.when(direct(k2))
         def _():
             x_copy(k2).wait_recv()
-            both = w[where(k2), part, :, core].astype(F32) + x_buf[slot(k2)].astype(F32)
-            w[where(k2), part, :, core] = both.astype(BF)
-            grant(k2, refs.x_credit, x_dev)
-
-        k3 = t - 2 - z
-
-        @pl.when(inside(k3))
-        def _():
-            right_step(k3)
-
-        k4 = t - 2 - (ends - z)
-
-        @pl.when(inside(k4))
-        def _():
-            left_step(k4)
-
+            place = at(k2, part, everything, core)
+            both = w[place].astype(F32) + x_buf[slot(k2)].astype(F32)
+            w[place] = both.astype(BF)
+
+            @pl.when(order(k2) + slots < directs)
+            def _():
+                signal(refs.x_credit, x_dev)
+
+        k3 = t - X_LAG - Z_LAG * z
+        k4 = t - X_LAG - Z_LAG * (ends - z)
         k5 = jnp.minimum(k3, k4)
 
-        @pl.when(inside(k5))
-        def _():
-            close_step(k5)
-
-        @pl.when(t == TILES + 1 + ends)
-        def _():
+        @pl.when(direct(k3))
+        def _():
+            main.right_step(k3)
+
+        @pl.when(direct(k4))
+        def _():
+            main.left_step(k4)
+
+        @pl.when(direct(k5))
+        def _():
+            put_grads(k5, w[main.place(k5, z)].astype(F32))
+
+        def listed(turn):
+            even = lax.rem(turn + 64, 2) == 0
+            return jnp.logical_and(even, jnp.logical_and(turn >= 0, turn < 2 * side_jobs))
+
+        j3 = t - LINE_START - Z_LAG * z
+        j4 = t - LINE_START - Z_LAG * (ends - z)
+
+        @pl.when(listed(j3))
+        def _():
+            beside.right_step(lax.div(j3, 2))
+
+        @pl.when(listed(j4))
+        def _():
+            beside.left_step(lax.div(j4, 2))
+
+        @pl.when(t == LINE_LAST)
+        def _():
+            for index in range(len(LINE_FIRST)):
+                last_copy(index).start()
+
+        @pl.when(t == CHUNKS + X_LAG + Z_LAG * ends - 1)
+        def _():
+            for index in range(len(LINE_FIRST)):
+                put_last(index)
             finish()
 
     def finish():
-        def settle(k, _):
+        def settle_core(k, _):
             core_copy(k).wait_send()
+            return 0
+
+        def settle_x(k, _):
             x_copy(k).wait_send()
-            for j in range(nz):
-
-                @pl.when(j > z)
-                def _():
-                    right_copy(k, j).wait_send()
-
-                @pl.when(j < z)
-                def _():
-                    left_copy(k, j).wait_send()
-
             return 0
 
-        lax.fori_loop(0, TILES, settle, 0)
-        grads_copy(TILES - 1).wait()
+        def settle_main(k, _):
+            main.settle(k)
+            return 0
+
+        def settle_beside(job, _):
+            beside.settle(job)
+            return 0
+
+        lax.fori_loop(CHUNKS - core_slots, CHUNKS, settle_core, 0)
+        lax.fori_loop(CHUNKS - slots, CHUNKS, settle_x, 0)
+        lax.fori_loop(CHUNKS - line_slots, CHUNKS, settle_main, 0)
+        lax.fori_loop(side_jobs - side_slots, side_jobs, settle_beside, 0)
+        for index in range(len(LINE_FIRST)):
+            last_copy(index).wait_send()
+        grads_copy(0).wait()
         act_copy(2 * seqs - 1).wait()
         sends = [core_sums()] + x_sums() + last_sums(False)
         for bit in range(zbits):
@@ -983,7 +1099,6 @@
     nz = replicas // 2
     lane = width + 128
     cut = half // 8
-    slots = 3
     dma = pltpu.SemaphoreType.DMA
     credit = pltpu.SemaphoreType.REGULAR
     anywhere = pl.BlockSpec(memory_space=pl.ANY)
@@ -993,7 +1108,7 @@
     if fused:
         outs = {
             "act_out": (shape((2 * seqs, width // 4, length), F32), anywhere),
-            "grads_out": (shape((TILES, cut, width), F32), anywhere),
+            "grads_out": (shape((CHUNKS, cut, half), F32), anywhere),
             "small_out": (shape((2, count // 2, width), F32), local),
             "token_out": (shape((2, count // 2, width), F32), local),
             "stamp_out": (shape((rows * replicas, lane), F32), local),
@@ -1044,17 +1159,22 @@
     if fused:
         zbits = nz.bit_length() - 1
         scratch |= {
-            "core_buf": vm((slots, 2, nz, cut, width), BF),
-            "x_buf": vm((slots, nz, cut, width), BF),
-            "right_buf": vm((slots, nz, cut, width), BF),
-            "left_buf": vm((slots, nz, cut, width), BF),
+            "core_buf": vm((4, 2, nz, cut, half), BF),
+            "x_buf": vm((X_LAG, nz, cut, half), BF),
+            "right_buf": vm((4, nz, cut, half), BF),
+            "left_buf": vm((4, nz, cut, half), BF),
+            "b_right_buf": vm((2, nz, cut, half), BF),
+            "b_left_buf": vm((2, nz, cut, half), BF),
+            "last_buf": vm((len(LINE_FIRST), cut, half), BF),
+            "last_send": dma((len(LINE_FIRST),)),
+            "last_recv": dma((len(LINE_FIRST),)),
             "sums_buf": vm((count, lane), F32),
             "adds": vm((1 + zbits, count // 2, width), F32),
             "adds_buf": vm((1 + zbits, count // 2, width), F32),
             "whole": vm((2, count // 2, width), F32),
             "stamp_buf": vm((rows, lane), F32),
             "stamps": vm((rows * replicas, lane), F32),
-            "grad_stage": vm((cut, width), F32),
+            "grad_stage": vm((cut, half), F32),
             "act_stage": vm((width // 4, length), F32),
             "out_sem": dma((2,)),
             "sums_sem": dma((4,)),
@@ -1068,13 +1188,17 @@
             "x_credit": credit,
             "right_credit": credit,
             "left_credit": credit,
+            "b_right_credit": credit,
+            "b_left_credit": credit,
         }
         for name in ("core", "x"):
-            scratch[name + "_send"] = dma((TILES,))
-            scratch[name + "_recv"] = dma((TILES,))
-        for name in ("right", "left"):
-            scratch[name + "_send"] = dma((TILES, nz))
-            scratch[name + "_recv"] = dma((TILES, nz))
+            slots = scratch[name + "_buf"].shape[0]
+            scratch[name + "_send"] = dma((slots,))
+            scratch[name + "_recv"] = dma((slots,))
+        for name in ("right", "left", "b_right", "b_left"):
+            slots = scratch[name + "_buf"].shape[0]
+            scratch[name + "_send"] = dma((slots, nz))
+            scratch[name + "_recv"] = dma((slots, nz))
     else:
         scratch["keep_sem"] = dma((16 * seqs + 1,))
     names = INPUTS + list(outs) + list(scratch)
@@ -1119,25 +1243,37 @@
     bup_out,
     down_out,
     bdown_out,
+    act_s,
+    grads_s,
     sem,
 ):
     s = lax.axis_index("section")
     d = lax.axis_index("dp")
     part = lax.rem(s, 2)
-    rows, width = grads.shape[1:]
-    half = width // 2
+    rows, half = grads.shape[1:]
+    width = 2 * half
     quarter = width // 4
-    pairs = [(act, act_out)]
-    for j in range(4):
-        for side in range(2):
-            first = side * 4 * half + j * half
-            pairs.append((grads.at[j, :, pl.ds(side * half, half)], up_out.at[0, :, pl.ds(first, half)]))
-    for j in range(3):
-        pairs.append((grads.at[4 + j], qkv_out.at[0, :, pl.ds(j * width, width)]))
-    pairs.append((grads.at[7], proj_out.at[0]))
-    for j in range(4):
-        pairs.append((grads.at[8 + j], down_out.at[0, pl.ds(j * rows, rows)]))
+    loads = [
+        pltpu.make_async_copy(src, dst, sem.at[25 + index])
+        for index, (src, dst) in enumerate(((act, act_s), (grads, grads_s)))
+    ]
+    for copy in loads:
+        copy.start()
+    pairs = [(act_s, act_out)]
+    for side in range(2):
+        for j in range(4):
+            columns = pl.ds(side * 4 * half + j * half, half)
+            pairs.append((grads_s.at[2 * j + side], up_out.at[0, :, columns]))
+        for j in range(3):
+            columns = pl.ds(j * width + side * half, half)
+            pairs.append((grads_s.at[8 + 2 * j + side], qkv_out.at[0, :, columns]))
+        columns = pl.ds(side * half, half)
+        pairs.append((grads_s.at[14 + side], proj_out.at[0, :, columns]))
+        for j in range(4):
+            pairs.append((grads_s.at[16 + 2 * j + side], down_out.at[0, pl.ds(j * rows, rows), columns]))
     copies = [pltpu.make_async_copy(src, dst, sem.at[index]) for index, (src, dst) in enumerate(pairs)]
+    for copy in loads:
+        copy.wait()
     for copy in copies:
         copy.start()
     vectors = small[0, :16, :]
@@ -1177,7 +1313,8 @@
 
 
 def run_finish(act, grads, small, token, stamp, letters_count, times_count):
-    rows, width = grads.shape[1:]
+    rows, half = grads.shape[1:]
+    width = 2 * half
     quarter = width // 4
     local = pl.BlockSpec(memory_space=pltpu.VMEM)
     anywhere = pl.BlockSpec(memory_space=pl.ANY)
@@ -1205,8 +1342,12 @@
         out_shape=tuple(jax.ShapeDtypeStruct(shape, F32) for shape, _ in shapes),
         in_specs=[anywhere] * 2 + [local] * 3,
         out_specs=tuple(spec for _, spec in shapes),
-        scratch_shapes=[pltpu.SemaphoreType.DMA((17,))],
-        compiler_params=pltpu.CompilerParams(vmem_limit_bytes=32 * 2**20),
+        scratch_shapes=[
+            pltpu.VMEM(act.shape, F32),
+            pltpu.VMEM(grads.shape, F32),
+            pltpu.SemaphoreType.DMA((27,)),
+        ],
+        compiler_params=pltpu.CompilerParams(vmem_limit_bytes=62 * 2**20),
     )(act, grads, small, token, stamp)
     return (jnp.swapaxes(outs[0], 1, 2), outs[1], jnp.swapaxes(outs[2], 0, 1)) + tuple(outs[3:])
 

time: 252 us -> 243 us (0.964)
  local copies, waits for them, and re-layouts: 7.87 us -> 2.24 us
  Pallas kernels: 242 us -> 238 us
    pallas_call x1, Pallas kernels: 239 us -> 233 us  [run_layers(): pl.pallas_call(functools.partial(layer_kernel, seqs, length, width, fused...]
    unnamed x10 -> x0, local copies, waits for them, and re-layouts: 5.63 us -> none
    pallas_call x1, Pallas kernels: 2.76 us -> 5.9 us  [run_finish(): pl.pallas_call(finish_kernel, out_shape=tuple((jax.ShapeDtypeStruct(shape...]
where the time goes in v4:
time: 243 us
  Pallas kernels  238 us (98%)
    pallas_call x1, Pallas kernels, run_layers(): pl.pallas_call(functools.partial(layer_kernel, seqs, length, width, fused...  233 us
    pallas_call x1, Pallas kernels, run_finish(): pl.pallas_call(finish_kernel, out_shape=tuple((jax.ShapeDtypeStruct(shape...  5.9 us

profile of v4, /device:TPU:0, one launch (start us, length us, event | category | flops | bytes accessed | tf_op | source)
XLA Modules:
  0.0 242.7 jit_solution(11375841613999898359)
XLA Ops:
  0.6 0.7 compare_select_fusion
  1.4 0.1 broadcast_in_dim.10
  1.5 2.2 gather_fusion
  3.6 0.6 pad_maximum_fusion.all_refs_15_
  4.3 232.5 %shard_map.297 = (f32[8,192,256]{2,1,0:T(8,128)}, f32[24,48,384]{2,1,0:T(8,128)}, f32[2,24,768]{2,1,0:T(8,128)}, f32[2,24,768]{2,1,0:T(8,128)}, f32[64,896]{1,0:T(8,128)}) custom-call(bf16[4,2,48,2304]{3,2,1,0:T(8,128)(2,1)} %bitcast.8, bf16[4,2,48,768]{3,2,1,0:T(8,128)(2,1)} %bitcast.9, bf16[4,2,48,3072]{3,2,1,0:T(8,128)(2,1)} %bitcast.6, ...), custom_call_target="tpu_custom_call" | custom-call | tf_op jit(solution)/shard_map/pallas_call | solution.py:1205
  236.8 5.9 %shard_map.298 = (f32[8,192,256]{2,1,0:T(8,128)}, f32[27,192]{1,0:T(8,128)}, f32[192,1000]{1,0:T(8,128)}, f32[1,48]{1,0:T(1,128)}, f32[1,48]{1,0:T(1,128)}, /*in...) custom-call(f32[8,192,256]{2,1,0:T(8,128)} %get-tuple-element.37.act, ...), custom_call_target="tpu_custom_call" | custom-call | tf_op jit(solution)/shard_map/pallas_call | solution.py:1340
  (2 shorter events, 0.0 us)

commit v5 on v4

--- a/solution.py
+++ b/solution.py
@@ -19,6 +19,7 @@
 CHUNKS = 2 * TILES
 LINE_FIRST = (1, 4, 7, 11)
 CORE_LAG, X_LAG, Z_LAG, LINE_START, LINE_LAST = 2, 6, 2, 3, 28
+BOTH_BY_X = 1
 GELU_A = math.sqrt(2.0 / math.pi)
 GELU_B = 0.044715
 
@@ -66,14 +67,15 @@
 
 INPUTS = (
     "qkv_in proj_in up_in down_in ga_in sa_in bq_in bv_in bo_in gm_in sm_in bdown_in bup_in "
-    "ids_in table_in time_in cot_in"
+    "ids_in table_in steps_in time_in cot_in"
 ).split()
 
 
 def layer_kernel(seqs, length, width, fused, names, *all_refs):
     refs = Refs(names, all_refs)
     w, par, qkv, probs = refs.w, refs.par, refs.qkv, refs.probs
-    xs, acc, ybuf, ysend, y1 = refs.xs, refs.acc, refs.ybuf, refs.ysend, refs.y1
+    acc, ybuf, ysend, y1 = refs.acc, refs.ybuf, refs.ysend, refs.y1
+    xs = acc
     slope, gate, h_s, o_s, hf_s, go_s = refs.slope, refs.gate, refs.h_s, refs.o_s, refs.hf_s, refs.go_s
     act, landed, gsum = refs.act, refs.landed, refs.gsum
     s = lax.axis_index("section")
@@ -172,6 +174,13 @@
         place = w.at[index, part, mine]
         return send(place, place, refs.wx_send.at[index], refs.wx_recv.at[index], x_dev)
 
+    def x_second(index):
+        place = w.at[index, part, across]
+        return send(place, place, refs.wz_send.at[index], refs.wz_recv.at[index], x_dev)
+
+    def by_z(index):
+        return index < TILES - BOTH_BY_X
+
     def relay(index, which, send_sem, recv_sem, device):
         place = w.at[index, other, which]
         return send(place, place, send_sem.at[index], recv_sem.at[index], device)
@@ -187,7 +196,11 @@
 
     def pass_first(index):
         relay(index, mine, refs.wx_send, refs.wx_recv, x_dev).wait_recv()
-        z_weight(index).start()
+
+        @pl.when(by_z(index))
+        def _():
+            z_weight(index).start()
+
         c1_weight(index).start()
 
     def pass_second(index):
@@ -227,8 +240,19 @@
     for index in range(TILES):
         wait(own_copies(index))
         x_weight(index).start()
+        if not by_z(index):
+            x_second(index).start()
         if index == 3:
             vec_copy(part).start()
+
+    seats, times_count = refs.ids_in.shape[0], refs.time_in.shape[0]
+    line = lax.broadcasted_iota(jnp.int32, (seats, times_count), 0)
+    moment = jnp.zeros((seats, times_count), jnp.int32)
+    for index in range(seats):
+        moment = jnp.where(line == index, refs.steps_in[index], moment)
+    hot = lax.broadcasted_iota(jnp.int32, (seats, times_count), 1) == moment
+    refs.times[:, :width] = mul(hot.astype(F32).astype(BF), refs.time_in[...])
+    refs.times[:, width:] = moment[:, :128].astype(F32)
 
     pass_first(0)
     pass_first(1)
@@ -310,7 +334,7 @@
     def attn_fwd(i):
         @pl.when(stage == 0)
         def _():
-            xs[...] = mul_tn(letters(i), refs.table[...]) + refs.time_in[pl.ds(part * seqs + i, 1), :width]
+            xs[...] = mul_tn(letters(i), refs.table[...]) + refs.times[pl.ds(part * seqs + i, 1), :width]
 
         @pl.when(stage == 1)
         def _():
@@ -320,7 +344,7 @@
 
         n, rate = normalize(xs[...])
         refs.n_a[i] = n.astype(BF)
-        refs.r_a[i] = jnp.broadcast_to(rate, (length, 128))
+        refs.rates[i] = jnp.broadcast_to(rate, (length, 128))
         h_s[i] = (n * row(0) + row(1)).astype(BF)
         for j in range(3):
             joint = mul(h_s[i], tile(QKV + j))
@@ -360,7 +384,7 @@
         x = y1[i].astype(F32)
         n, rate = normalize(x)
         refs.n_f[i] = n.astype(BF)
-        refs.r_f[i] = jnp.broadcast_to(rate, (length, 128))
+        refs.rates[i] = jnp.where(low, refs.rates[i], jnp.broadcast_to(rate, (length, 128)))
         hf_s[i] = (n * row(5) + row(6)).astype(BF)
         acc[...] = x + row(7)
         for j in range(4):
@@ -415,7 +439,7 @@
         n = refs.n_f[i].astype(F32)
         add_row(5, gh * n)
         add_row(6, gh)
-        gx = ybuf[i].astype(F32) + scaled_back(gh, row(5), n, refs.r_f[i][:, 0:1])
+        gx = ybuf[i].astype(F32) + scaled_back(gh, row(5), n, refs.rates[i][:, 64:65])
         y1[i] = gx.astype(BF)
 
     def attn_bwd(i):
@@ -453,7 +477,7 @@
         n = refs.n_a[i].astype(F32)
         add_row(0, gh * n)
         add_row(1, gh)
-        acc[...] = y1[i].astype(F32) + scaled_back(gh, row(0), n, refs.r_a[i][:, 0:1])
+        acc[...] = y1[i].astype(F32) + scaled_back(gh, row(0), n, refs.rates[i][:, 0:1])
 
         @pl.when(stage == 1)
         def _():
@@ -467,7 +491,7 @@
             hot = letters(i)
             gsum[vectors:count, :width] += mul(hot, high) + mul(hot, rest)
             mark = part * seqs + i
-            stamp = refs.time_in[pl.ds(mark, 1), :]
+            stamp = refs.times[pl.ds(mark, 1), :]
             gsum[pl.ds(count + mark, 1), :] = jnp.concatenate([column(acc[...]), stamp[:, width:]], axis=1)
 
     units = (attn_fwd, feed_fwd, feed_bwd, attn_bwd)
@@ -1088,7 +1112,7 @@
     return step
 
 
-def run_layers(weights, singles, ids, table, times, cot, replicas, fused):
+def run_layers(weights, singles, ids, table, steps, times, cot, replicas, fused):
     rows, length = ids.shape
     width = cot.shape[2]
     half = width // 2
@@ -1125,12 +1149,11 @@
         "vecs": vm((2, 16, half), F32),
         "table": vm((padded, width), BF),
         "par": vm((16, width), F32),
-        "xs": vm((length, width), F32),
+        "times": vm((rows, lane), F32),
         "acc": vm((length, width), F32),
         "n_a": vm((seqs, length, width), BF),
         "n_f": vm((seqs, length, width), BF),
-        "r_a": vm((seqs, length, 128), F32),
-        "r_f": vm((seqs, length, 128), F32),
+        "rates": vm((seqs, length, 128), F32),
         "qkv": vm((seqs, length, 3 * width), BF),
         "probs": vm((seqs, HEADS, length, length), BF),
         "y1": vm((seqs, length, width), BF),
@@ -1159,7 +1182,7 @@
     if fused:
         zbits = nz.bit_length() - 1
         scratch |= {
-            "core_buf": vm((4, 2, nz, cut, half), BF),
+            "core_buf": vm((3, 2, nz, cut, half), BF),
             "x_buf": vm((X_LAG, nz, cut, half), BF),
             "right_buf": vm((4, nz, cut, half), BF),
             "left_buf": vm((4, nz, cut, half), BF),
@@ -1205,13 +1228,15 @@
     return pl.pallas_call(
         functools.partial(layer_kernel, seqs, length, width, fused, names),
         out_shape=tuple(out[0] for out in outs.values()),
-        in_specs=[anywhere] * 4 + [local] * 12 + [anywhere],
+        in_specs=[anywhere] * 4
+        + [local] * 11
+        + [pl.BlockSpec(memory_space=pltpu.SMEM), local, anywhere],
         out_specs=tuple(out[1] for out in outs.values()),
         scratch_shapes=list(scratch.values()),
         compiler_params=pltpu.CompilerParams(
             collective_id=0, has_side_effects=True, vmem_limit_bytes=64 * 2**20 - 2**17
         ),
-    )(*weights, *singles, ids, table, times, cot)
+    )(*weights, *singles, ids, table, steps, times, cot)
 
 
 def three_parts(value):
@@ -1418,9 +1443,6 @@
         down_bias,
         up_bias,
     )
-    marks = jnp.broadcast_to(timesteps.astype(F32)[:, None], (rows, 128))
-    times = time_table.at[timesteps].get(mode="promise_in_bounds").astype(F32)
-    times = jnp.concatenate([times, marks], axis=1)
     cut = half // 8
     weights = (
         qkv_weight.reshape(4, 2, cut, 3 * width),
@@ -1430,7 +1452,9 @@
     )
     vectors = 16
     fused = replicas == 8
-    layers = run_layers(weights, singles, token_ids, token_table, times, cotangent, replicas, fused)
+    layers = run_layers(
+        weights, singles, token_ids, token_table, timesteps, time_table, cotangent, replicas, fused
+    )
     if fused:
         return run_finish(*layers, letters_count, times_count)
     act, sums, fixed, moving = layers

time: 243 us -> 241 us (level)
  no operation moved by 1% of the time
where the time goes in v5:
time: 241 us
  Pallas kernels  240 us (100%)
    pallas_call x1, Pallas kernels, run_layers(): pl.pallas_call(functools.partial(layer_kernel, seqs, length, width, fused...  234 us
    pallas_call x1, Pallas kernels, run_finish(): pl.pallas_call(finish_kernel, out_shape=tuple((jax.ShapeDtypeStruct(shape...  5.9 us

profile of v5, /device:TPU:0, one launch (start us, length us, event | category | flops | bytes accessed | tf_op | source)
XLA Modules:
  0.0 241.0 jit_solution(11580401702852517110)
XLA Ops:
  0.7 234.4 %shard_map.297 = (f32[8,192,256]{2,1,0:T(8,128)}, f32[24,48,384]{2,1,0:T(8,128)}, f32[2,24,768]{2,1,0:T(8,128)}, f32[2,24,768]{2,1,0:T(8,128)}, f32[64,896]{1,0:T(8,128)}) custom-call(bf16[4,2,48,2304]{3,2,1,0:T(8,128)(2,1)} %bitcast.8, bf16[4,2,48,768]{3,2,1,0:T(8,128)(2,1)} %bitcast.9, bf16[4,2,48,3072]{3,2,1,0:T(8,128)(2,1)} %bitcast.6, ...), custom_call_target="tpu_custom_call" | custom-call | tf_op jit(solution)/shard_map/pallas_call | solution.py:1228
  235.1 5.9 %shard_map.298 = (f32[8,192,256]{2,1,0:T(8,128)}, f32[27,192]{1,0:T(8,128)}, f32[192,1000]{1,0:T(8,128)}, f32[1,48]{1,0:T(1,128)}, f32[1,48]{1,0:T(1,128)}, /*in...) custom-call(f32[8,192,256]{2,1,0:T(8,128)} %get-tuple-element.37.act, ...), custom_call_target="tpu_custom_call" | custom-call | tf_op jit(solution)/shard_map/pallas_call | solution.py:1365

commit v6 on v5

--- a/solution.py
+++ b/solution.py
@@ -380,7 +380,7 @@
 
                 lax.fori_loop(first, last, one, 0)
 
-        arrived(UP, DOWN)
+        arrived(UP, TILES)
         x = y1[i].astype(F32)
         n, rate = normalize(x)
         refs.n_f[i] = n.astype(BF)
@@ -395,7 +395,6 @@
             gate[i, j] = (u * both).astype(BF)
             bend = (0.5 * GELU_A + 1.5 * GELU_A * GELU_B * square) * u
             slope[i, j] = (both + bend * (1.0 - t * t)).astype(BF)
-        arrived(DOWN, TILES)
         down = mul(gate[i, 0], tile(DOWN))
         for j in range(1, 4):
             down = down + mul(gate[i, j], tile(DOWN + j))
@@ -1278,29 +1277,33 @@
     rows, half = grads.shape[1:]
     width = 2 * half
     quarter = width // 4
+    thirds = [pl.ds(8 * index, 8) for index in range(3)]
     loads = [
         pltpu.make_async_copy(src, dst, sem.at[25 + index])
-        for index, (src, dst) in enumerate(((act, act_s), (grads, grads_s)))
+        for index, (src, dst) in enumerate(
+            [(grads.at[third], grads_s.at[third]) for third in thirds] + [(act, act_s)]
+        )
     ]
     for copy in loads:
         copy.start()
-    pairs = [(act_s, act_out)]
+    pairs = [[], [], [], [(act_s, act_out)]]
     for side in range(2):
         for j in range(4):
             columns = pl.ds(side * 4 * half + j * half, half)
-            pairs.append((grads_s.at[2 * j + side], up_out.at[0, :, columns]))
+            pairs[0].append((grads_s.at[2 * j + side], up_out.at[0, :, columns]))
         for j in range(3):
             columns = pl.ds(j * width + side * half, half)
-            pairs.append((grads_s.at[8 + 2 * j + side], qkv_out.at[0, :, columns]))
+            pairs[1].append((grads_s.at[8 + 2 * j + side], qkv_out.at[0, :, columns]))
         columns = pl.ds(side * half, half)
-        pairs.append((grads_s.at[14 + side], proj_out.at[0, :, columns]))
+        pairs[1].append((grads_s.at[14 + side], proj_out.at[0, :, columns]))
         for j in range(4):
-            pairs.append((grads_s.at[16 + 2 * j + side], down_out.at[0, pl.ds(j * rows, rows), columns]))
-    copies = [pltpu.make_async_copy(src, dst, sem.at[index]) for index, (src, dst) in enumerate(pairs)]
-    for copy in loads:
-        copy.wait()
-    for copy in copies:
-        copy.start()
+            pairs[2].append((grads_s.at[16 + 2 * j + side], down_out.at[0, pl.ds(j * rows, rows), columns]))
+    copies = []
+    for load, group in zip(loads, pairs):
+        load.wait()
+        for src, dst in group:
+            copies.append(pltpu.make_async_copy(src, dst, sem.at[len(copies)]))
+            copies[-1].start()
     vectors = small[0, :16, :]
     lower = jnp.where(part == 0, vectors[:, :half], vectors[:, half:])
     turned = pltpu.roll(lower, lax.rem(half - d * rows, half), 1)
@@ -1370,7 +1373,7 @@
         scratch_shapes=[
             pltpu.VMEM(act.shape, F32),
             pltpu.VMEM(grads.shape, F32),
-            pltpu.SemaphoreType.DMA((27,)),
+            pltpu.SemaphoreType.DMA((29,)),
         ],
         compiler_params=pltpu.CompilerParams(vmem_limit_bytes=62 * 2**20),
     )(act, grads, small, token, stamp)

time: 241 us -> 238 us (0.988)
  Pallas kernels: 240 us -> 237 us
    pallas_call x1, Pallas kernels: 234 us -> 231 us  [run_layers(): pl.pallas_call(functools.partial(layer_kernel, seqs, length, width, fused...]
where the time goes in v6:
time: 238 us; the launch traced here: 237 us
  Pallas kernels  237 us (100%)
    pallas_call x1, Pallas kernels, run_layers(): pl.pallas_call(functools.partial(layer_kernel, seqs, length, width, fused...  231 us
    pallas_call x1, Pallas kernels, run_finish(): pl.pallas_call(finish_kernel, out_shape=tuple((jax.ShapeDtypeStruct(shape...  5.35 us

profile of v6, /device:TPU:0, one launch (start us, length us, event | category | flops | bytes accessed | tf_op | source)
XLA Modules:
  0.0 237.5 jit_solution(10025629016255275174)
XLA Ops:
  0.7 231.5 %shard_map.297 = (f32[8,192,256]{2,1,0:T(8,128)}, f32[24,48,384]{2,1,0:T(8,128)}, f32[2,24,768]{2,1,0:T(8,128)}, f32[2,24,768]{2,1,0:T(8,128)}, f32[64,896]{1,0:T(8,128)}) custom-call(bf16[4,2,48,2304]{3,2,1,0:T(8,128)(2,1)} %bitcast.8, bf16[4,2,48,768]{3,2,1,0:T(8,128)(2,1)} %bitcast.9, bf16[4,2,48,3072]{3,2,1,0:T(8,128)(2,1)} %bitcast.6, ...), custom_call_target="tpu_custom_call" | custom-call | tf_op jit(solution)/shard_map/pallas_call | solution.py:1227
  232.1 5.3 %shard_map.298 = (f32[8,192,256]{2,1,0:T(8,128)}, f32[27,192]{1,0:T(8,128)}, f32[192,1000]{1,0:T(8,128)}, f32[1,48]{1,0:T(1,128)}, f32[1,48]{1,0:T(1,128)}, /*in...) custom-call(f32[8,192,256]{2,1,0:T(8,128)} %get-tuple-element.37.act, ...), custom_call_target="tpu_custom_call" | custom-call | tf_op jit(solution)/shard_map/pallas_call | solution.py:1368
